TPU v7x, 32 devices: a whole 2x2x4 slice. The times are simulated.
32 devices in a mesh: dp: 8 (over y, x, core), fsdp: 4 (over z).
Axes of the slice: x: 2, y: 2, z: 4, core: 2. Of those that a mesh axis runs over, the one named last changes fastest.
Arguments:
- student_tiles: bfloat16 [4096, 16, 256], P(('dp', 'fsdp')), may hold values from -6 to 6
- teacher_tiles: bfloat16 [4096, 16, 512], P(('dp', 'fsdp')), may hold values from -6 to 6
- send_list: int32 [8, 4, 128], P('dp', 'fsdp'), may hold values from -1 to 127, as said below
- clip_weight: float32 [4096], P(('dp', 'fsdp')), may hold values from 0.5 to 64, as said below
- kernel_dilated: bfloat16 [1792, 256], P('fsdp'), may hold values from -0.125 to 0.125
- kernel_mix: bfloat16 [256, 256], P('fsdp'), may hold values from -0.375 to 0.375
- kernel_down: bfloat16 [4096, 512], P('fsdp'), may hold values from -0.09375 to 0.09375
- kernel_proj: bfloat16 [512, 1024], P('fsdp'), may hold values from -0.25 to 0.25
- kernel_teacher: bfloat16 [16, 512, 1024], P(None, 'fsdp'), may hold values from -0.0625 to 0.0625
- alpha_one: float32 [256], replicated, may hold values from 0.5 to 2
- alpha_two: float32 [256], replicated, may hold values from 0.5 to 2
- alpha_three: float32 [256], replicated, may hold values from 0.5 to 2
- alpha_teacher: float32 [512], replicated, may hold values from 0.5 to 2
Outputs:
- student_latent: bfloat16 [4096, 2, 1024], P(('dp', 'fsdp'))
- grad_dilated: float32 [458752], P(('dp', 'fsdp'))
- grad_mix: float32 [65536], P(('dp', 'fsdp'))
- grad_down: float32 [2097152], P(('dp', 'fsdp'))
- grad_proj: float32 [524288], P(('dp', 'fsdp'))
Inputs may be any that keep to these rules, and one draw needn't show every extreme that they name: `send_list`: entries d * 16 .. d * 16 + 15 of a device's list go to dp owner d. Each device's tiles 0 .. L - 1 appear exactly once and no other tile appears, for a count L of 16 to 128 drawn per device; on every device one owner receives 16 tiles, and some device has L = 128. `clip_weight`: positive weights.
All inputs are finite; a program needn't handle non-finite values.
Results may differ from a plain program's by a relative error of at most 0.0067.
Values may be sent and summed in bfloat16 or wider, within the bound.
No kernel may reach another device: no remote copies, remote signals or barrier semaphores. Data moves between devices by JAX's collectives and lax.ppermute only.
A program may use at most 128 MiB of HBM per device.

v0:
```python
import jax
import jax.numpy as jnp
from jax import lax
from jax.sharding import PartitionSpec as P

DL = 1024
KS = 16
STRIDE = 8
DILATED_TAPS = 7
UNIT_DILATION = 3
TILE_FRAMES = 16
OUTF = 2


def snake(values, alpha_vec):
    widened = values.astype(jnp.float32)
    return widened + jnp.square(jnp.sin(alpha_vec * widened)) / alpha_vec


def snake_slope(values, alpha_vec):
    return 1.0 + jnp.sin(2.0 * alpha_vec * values)


def unfold_strided(frames):
    tile_count = frames.shape[0]
    margin = (KS - STRIDE) // 2
    padded_frames = jnp.pad(frames, ((0, 0), (margin, margin), (0, 0)))
    windows = [
        padded_frames[:, STRIDE * offset : STRIDE * offset + KS, :].reshape(tile_count, -1)
        for offset in range(OUTF)
    ]
    return jnp.stack(windows, axis=1)


def fold_strided(columns, channels):
    tile_count = columns.shape[0]
    margin = (KS - STRIDE) // 2
    padded_len = TILE_FRAMES + 2 * margin
    pieces = columns.reshape(tile_count, OUTF, KS, channels)
    folded = jnp.zeros((tile_count, padded_len, channels), jnp.float32)
    for offset in range(OUTF):
        folded = folded + jnp.pad(
            pieces[:, offset],
            ((0, 0), (STRIDE * offset, padded_len - KS - STRIDE * offset), (0, 0)),
        )
    return folded[:, margin : margin + TILE_FRAMES, :]


def unfold_dilated(frames):
    tile_count = frames.shape[0]
    receptive_length = UNIT_DILATION * (DILATED_TAPS - 1) // 2
    padded_frames = jnp.pad(frames, ((0, 0), (receptive_length, receptive_length), (0, 0)))
    tap_offsets = [
        padded_frames[
            :, UNIT_DILATION * tap_position : UNIT_DILATION * tap_position + TILE_FRAMES, :
        ]
        for tap_position in range(DILATED_TAPS)
    ]
    return jnp.stack(tap_offsets, axis=2).reshape(tile_count * TILE_FRAMES, -1)


def teacher_forward(tiles, kernel_teacher, alpha_teacher):
    tile_count = tiles.shape[0]
    activated = snake(tiles, alpha_teacher).astype(jnp.bfloat16)
    spread = lax.all_to_all(activated, "fsdp", split_axis=2, concat_axis=0, tiled=True)
    flat_kernel = kernel_teacher.reshape(-1, DL)
    columns = unfold_strided(spread).reshape(tile_count * lax.axis_size("fsdp") * OUTF, -1)
    return lax.psum_scatter(
        jnp.dot(columns, flat_kernel, preferred_element_type=jnp.float32).reshape(
            tile_count * lax.axis_size("fsdp"), OUTF, DL
        ),
        "fsdp",
        scatter_dimension=0,
        tiled=True,
    ).astype(jnp.bfloat16)


def student_step(tiles, target, weights, kernels, alphas):
    kernel_dilated, kernel_mix, kernel_down, kernel_proj = kernels
    alpha_one, alpha_two, alpha_three = alphas
    tile_count = tiles.shape[0]
    channels = tiles.shape[2]
    act_one = snake(tiles, alpha_one).astype(jnp.bfloat16)
    dilated = unfold_dilated(act_one)
    hidden = jnp.dot(dilated, kernel_dilated, preferred_element_type=jnp.float32)
    act_two = snake(hidden, alpha_two).astype(jnp.bfloat16)
    residual = tiles.reshape(tile_count * TILE_FRAMES, channels).astype(jnp.float32) + jnp.dot(
        act_two, kernel_mix, preferred_element_type=jnp.float32
    )
    act_three = (
        snake(residual, alpha_three).astype(jnp.bfloat16).reshape(tile_count, TILE_FRAMES, channels)
    )
    strided = unfold_strided(act_three).reshape(tile_count * OUTF, -1)
    student = jnp.dot(strided, kernel_down, preferred_element_type=jnp.float32).astype(jnp.bfloat16)
    predicted = jnp.dot(student, kernel_proj, preferred_element_type=jnp.float32)
    row_weight = jnp.repeat(weights, OUTF)[:, None]
    error = (
        row_weight
        * (predicted - target.reshape(tile_count * OUTF, DL).astype(jnp.float32))
        / (tile_count * OUTF)
    ).astype(jnp.bfloat16)
    grad_proj = jnp.dot(student.T, error, preferred_element_type=jnp.float32)
    back_student = jnp.dot(error, kernel_proj.T, preferred_element_type=jnp.float32).astype(
        jnp.bfloat16
    )
    grad_down = jnp.dot(strided.T, back_student, preferred_element_type=jnp.float32)
    back_columns = jnp.dot(back_student, kernel_down.T, preferred_element_type=jnp.float32).reshape(
        tile_count, OUTF, -1
    )
    back_three = fold_strided(back_columns, channels).reshape(tile_count * TILE_FRAMES, channels)
    back_residual = (back_three * snake_slope(residual, alpha_three)).astype(jnp.bfloat16)
    grad_mix = jnp.dot(act_two.T, back_residual, preferred_element_type=jnp.float32)
    back_hidden = (
        jnp.dot(back_residual, kernel_mix.T, preferred_element_type=jnp.float32)
        * snake_slope(hidden, alpha_two)
    ).astype(jnp.bfloat16)
    grad_dilated = jnp.dot(dilated.T, back_hidden, preferred_element_type=jnp.float32)
    latent = predicted.astype(jnp.bfloat16).reshape(tile_count, OUTF, DL)
    return (
        latent,
        (
            grad_dilated.reshape(-1),
            grad_mix.reshape(-1),
            grad_down.reshape(-1),
            grad_proj.reshape(-1),
        ),
    )


def on_device(
    student_tiles,
    teacher_tiles,
    send_list,
    clip_weight,
    kernel_dilated,
    kernel_mix,
    kernel_down,
    kernel_proj,
    kernel_teacher,
    alpha_one,
    alpha_two,
    alpha_three,
    alpha_teacher,
):
    routes = send_list.reshape(-1)
    live_rows = (routes >= 0)[:, None, None]
    picked = jnp.maximum(routes, 0)

    def packed(values):
        return jnp.where(live_rows, jnp.take(values, picked, axis=0), jnp.zeros((), values.dtype))

    student_part, teacher_part = (
        lax.all_to_all(packed(student_tiles), "dp", split_axis=0, concat_axis=0, tiled=True),
        lax.all_to_all(packed(teacher_tiles), "dp", split_axis=0, concat_axis=0, tiled=True),
    )
    target = teacher_forward(teacher_part, kernel_teacher, alpha_teacher)
    kernels = (
        lax.all_gather(kernel_dilated, "fsdp", axis=0, tiled=True),
        lax.all_gather(kernel_mix, "fsdp", axis=0, tiled=True),
        lax.all_gather(kernel_down, "fsdp", axis=0, tiled=True),
        lax.all_gather(kernel_proj, "fsdp", axis=0, tiled=True),
    )
    latent, gradients = student_step(
        student_part, target, clip_weight, kernels, (alpha_one, alpha_two, alpha_three)
    )
    gradients = (
        lax.psum_scatter(gradients[0], ("dp", "fsdp"), scatter_dimension=0, tiled=True),
        lax.psum_scatter(gradients[1], ("dp", "fsdp"), scatter_dimension=0, tiled=True),
        lax.psum_scatter(gradients[2], ("dp", "fsdp"), scatter_dimension=0, tiled=True),
        lax.psum_scatter(gradients[3], ("dp", "fsdp"), scatter_dimension=0, tiled=True),
    )
    return (latent, gradients[0], gradients[1], gradients[2], gradients[3])


def solution(mesh):
    placed = (
        P(("dp", "fsdp"), None, None),
        P(("dp", "fsdp"), None, None),
        P("dp", "fsdp", None),
        P(("dp", "fsdp")),
        P("fsdp", None),
        P("fsdp", None),
        P("fsdp", None),
        P("fsdp", None),
        P(None, "fsdp", None),
        P(),
        P(),
        P(),
        P(),
    )
    return jax.shard_map(
        on_device,
        mesh=mesh,
        in_specs=placed,
        out_specs=(
            P(("dp", "fsdp"), None, None),
            P(("dp", "fsdp")),
            P(("dp", "fsdp")),
            P(("dp", "fsdp")),
            P(("dp", "fsdp")),
        ),
        check_vma=False,
    )
```

profile of v0, /device:TPU:0, one launch (start us, length us, event | category | flops | bytes accessed | tf_op | source)
XLA Modules:
  0.0 625.9 jit_solution(2647648656287500958)
XLA Ops:
  8.8 2.0 gather_fusion.1
  10.8 3.0 select_select_fusion
  13.8 5.3 all-to-all-start.1
  19.9 25.9 %all-to-all-done.1 = bf16[128,16,512]{2,1,0:T(8,128)(2,1)S(1)} async-done(((bf16[128,16,512]{2,1,0:T(8,128)(2,1)}), bf16[128,16,512]{2,1,0:T(8,128)(2,1)S(1)}, u32[]{:S(2)}, u32[]{:S(2)}) %all-to-all-start.1) | async-done | bytes 2097184 | tf_op jit(solution)/shard_map/all_to_all | solution.py:154
  45.7 15.0 %fusion.3 = bf16[128,16,512]{2,1,0:T(8,128)(2,1)} fusion(bf16[128,16,512]{2,1,0:T(8,128)(2,1)S(1)} %all-to-all-done.1, f32[512]{0:T(512)S(1)} %copy-done.13), kind=kLoop, calls=%fused_computation.13 | loop fusion | flops 6291456 | bytes 4196352 | tf_op jit(solution)/shard_map/convert_element_type | solution.py:64
  60.8 4.2 copy.52
  65.0 83.5 %all_to_all.28 = bf16[128,16,512]{0,1,2:T(8,128)(2,1)} all-to-all(bf16[128,16,512]{0,1,2:T(8,128)(2,1)S(1)} %copy.52), channel_id=1, replica_groups=mesh['dp'=8,'fsdp'=4] {'fsdp'}, dimensions={2} | all-to-all | bytes 4194304 | tf_op jit(solution)/shard_map/all_to_all | solution.py:65
  148.5 5.1 copy.53
  153.6 5.3 pad_slice_fusion.7
  158.9 4.1 stack_reshape.15
  163.0 2.3 stack_reshape.14
  165.3 10.0 %fusion.4 = f32[512,2,1024]{2,0,1:T(8,128)} fusion(bf16[2048,1024,1]{1,0,2:T(8,128)(2,1)} %bitcast.109, bf16[512,1,2048]{2,0,1:T(8,128)(2,1)} %stack_reshape.15, bf16[512,1,2048]{2,0,1:T(8,128)(2,1)} %stack_reshape.14), kind=kOutput, calls=%fused_computation.14 | convolution fusion | flops 4297064448 | bytes 12582912 | tf_op jit(solution)/shard_map/dot_general | solution.py:69
  178.7 3.8 all-to-all-start
  183.5 15.5 %all_gather.13 = bf16[256,256]{1,0:T(8,128)(2,1)S(1)} all-gather(bf16[64,256]{1,0:T(8,128)(2,1)S(1)} %copy-done.11), channel_id=1, replica_groups=mesh['dp'=8,'fsdp'=4] {'fsdp'}, dimensions={0}, use_global_device_ids=true | all-gather | bytes 163840 | tf_op jit(solution)/shard_map/all_gather | solution.py:159
  199.0 33.7 %all_gather.12 = bf16[1792,256]{1,0:T(8,128)(2,1)} all-gather(bf16[448,256]{1,0:T(8,128)(2,1)S(1)} %copy-done.10), channel_id=1, replica_groups=mesh['dp'=8,'fsdp'=4] {'fsdp'}, dimensions={0}, use_global_device_ids=true | all-gather | bytes 1146880 | tf_op jit(solution)/shard_map/all_gather | solution.py:158
  232.8 7.3 %add_convert_fusion.2 = bf16[128,16,256]{2,1,0:T(8,128)(2,1)S(1)} fusion(f32[256]{0:T(256)S(1)} %copy-done.12, bf16[128,16,256]{2,1,0:T(8,128)(2,1)S(1)} %all-to-all-done), kind=kLoop, calls=%fused_computation.33 | loop fusion | flops 3145728 | bytes 2098176 | tf_op jit(solution)/shard_map/convert_element_type | solution.py:83
  244.1 7.9 %bitcast_dynamic-update-slice_fusion = bf16[128,16,7,256]{3,1,0,2:T(8,128)(2,1)} fusion(bf16[128,16,7,256]{3,1,0,2:T(8,128)(2,1)} %fusion.15, f32[256]{0:T(256)S(1)} %copy-done.12, bf16[128,16,256]{2,1,0:T(8,128)(2,1)S(1)} %all-to-all-done), kind=kLoop, calls=%fused_computation.53 | loop fusion | flops 3145728 | bytes 2098176
  256.0 14.5 %copy.49 = bf16[128,16,7,256]{3,2,1,0:T(8,128)(2,1)} copy(bf16[128,16,7,256]{3,1,0,2:T(8,128)(2,1)} %fusion.21) | data formatting | bytes 14680064 | tf_op jit(solution)/shard_map/stack | solution.py:59
  270.5 20.2 %copy.59 = bf16[256,8,7,256]{3,1,2,0:T(8,128)(2,1)S(1)} copy(bf16[256,8,7,256]{3,2,1,0:T(8,128)(2,1)} %bitcast.95) | data formatting | bytes 14680064
  290.7 2.1 fusion.26
  293.6 15.2 %add_convert_fusion = (bf16[2048,256]{1,0:T(8,128)(2,1)S(1)}, f32[2048,256]{1,0:T(8,128)}) fusion(f32[256]{0:T(256)S(1)} %copy-done.14, bf16[256,256]{1,0:T(8,128)(2,1)S(1)} %all_gather.13, f32[2048,256]{1,0:T(8,128)S(1)} %fusion.26, f32[256]{0:T(256)S(1)} %copy-done.15, bf16[2048,256]{1,0:T(8,128)(2,1)S(1)} %bitcast.98), kind=kOutput, calls=%fused_computation.31 | convolution fusion | flops 274726912 | bytes 6424576 | tf_op jit(solution)/shard_map/dot_general | solution.py:87
  310.3 4.0 copy.51
  314.3 2.7 reshape.89
  317.1 3.4 convolution_convert_fusion.1
  325.6 2.5 multiply_convert_fusion
  330.4 4.5 convolution_bitcast_fusion
  340.2 7.2 %fusion.9 = bf16[2048,256]{1,0:T(8,128)(2,1)S(1)} fusion(f32[128,16,256]{2,1,0:T(8,128)S(1)} %pad_add_fusion, f32[2048,256]{1,0:T(8,128)S(1)} %copy-done.7, f32[256]{0:T(256)S(1)} %broadcast_multiply_fusion.1), kind=kLoop, calls=%fused_computation.29 | loop fusion | flops 2097152 | bytes 5243904 | tf_op jit(solution)/shard_map/convert_element_type | solution.py:111
  347.4 7.6 %convolution_bitcast_fusion.3 = f32[32,2,8,128]{3,2,1,0:T(8,128)S(1)} fusion(bf16[2048,256]{1,0:T(8,128)(2,1)S(1)} %fusion.9, f32[2048,256]{1,0:T(8,128)S(1)} %copy-done.18, f32[256]{0:T(256)S(1)} %copy-done.15), kind=kOutput, calls=%fused_computation.40 | convolution fusion | flops 271056896 | bytes 3408896 | tf_op jit(solution)/shard_map/dot_general | solution.py:112
  355.0 12.2 %convolution_bitcast_fusion.2 = f32[224,2,8,128]{3,2,1,0:T(8,128)S(1)} fusion(bf16[2048,1792]{1,0:T(8,128)(2,1)} %bitcast.104, bf16[2048,256]{1,0:T(8,128)(2,1)S(1)} %fusion.9, bf16[256,256]{1,0:T(8,128)(2,1)S(1)} %all_gather.13, f32[2048,256]{1,0:T(8,128)} %copy-done.17, f32[256]{0:T(256)S(1)} %broadcast_multiply_fusion), kind=kOutput, calls=%fused_computation.37 | convolution fusion | flops 2149580800 | bytes 12452864 | tf_op jit(solution)/shard_map/dot_general | solution.py:117
  367.2 2.2 copy.61
  370.3 9.0 %copy.63 = f32[512,4,8,128]{3,1,2,0:T(4,128)} copy(f32[512,4,8,128]{3,2,1,0:T(8,128)} %convolution_bitcast_fusion) | data formatting | bytes 16777216
  383.1 230.0 %all-reduce.12.cloned.1.call-done = (f32[458752]{0:T(1024)}, f32[65536]{0:T(1024)}, f32[2097152]{0:T(1024)}, f32[524288]{0:T(1024)}) async-done(((f32[458752]{0:T(1024)}, f32[65536]{0:T(1024)}, f32[2097152]{0:T(1024)}, f32[524288]{0:T(1024)}), (f32[458752]{0:T(1024)}, f32[65536]{0:T(1024)}, f32[2097152]{0:T(1024)}, f32[524288]{0:T(1024)})) %all-reduce.12.cloned.1.call-update) | async-done | bytes 12582928
  (84 shorter events, 40.3 us)
Async XLA Ops:
  7.2 1.6 copy-start
  13.8 32.0 %copy-start.13 = (f32[512]{0:T(512)S(1)}, f32[512]{0:T(512)}, u32[]{:S(2)}) copy-start(f32[512]{0:T(512)} %param.25) | copy-start | bytes 6148
  13.8 31.9 %all-to-all-start.1 = ((bf16[128,16,512]{2,1,0:T(8,128)(2,1)}), bf16[128,16,512]{2,1,0:T(8,128)(2,1)S(1)}, u32[]{:S(2)}, u32[]{:S(2)}) async-start(bf16[128,16,512]{2,1,0:T(8,128)(2,1)} %select_select_fusion), calls=%async_computation.1 | async-start | bytes 4194304 | tf_op jit(solution)/shard_map/all_to_all | solution.py:154
  19.1 298.0 %all-gather.3.cloned.1.call-start = ((), (), s32[]{:S(2)}) async-start(), calls=%async_computation.4 | async-start | bytes 5242880 | tf_op jit(solution)/shard_map/all_gather | solution.py:160
  19.8 300.7 %reduce-scatter.2.cloned.1.call-start = ((), (), s32[]{:S(2)}) async-start(), calls=%async_computation.6 | async-start | bytes 5242880 | tf_op jit(solution)/shard_map/reduce_scatter | solution.py:68
  175.3 1.2 copy-start.8
  177.2 6.1 copy-start.16
  177.2 6.3 %copy-start.11 = (bf16[64,256]{1,0:T(8,128)(2,1)S(1)}, bf16[64,256]{1,0:T(8,128)(2,1)}, u32[]{:S(2)}) copy-start(bf16[64,256]{1,0:T(8,128)(2,1)} %param.18) | copy-start | bytes 98308
  177.2 21.8 %copy-start.14 = (f32[256]{0:T(256)S(1)}, f32[256]{0:T(256)}, u32[]{:S(2)}) copy-start(f32[256]{0:T(256)} %param.24) | copy-start | bytes 3076
  177.2 21.8 %copy-start.15 = (f32[256]{0:T(256)S(1)}, f32[256]{0:T(256)}, u32[]{:S(2)}) copy-start(f32[256]{0:T(256)} %param.23) | copy-start | bytes 3076
  177.2 21.8 %copy-start.10 = (bf16[448,256]{1,0:T(8,128)(2,1)S(1)}, bf16[448,256]{1,0:T(8,128)(2,1)}, u32[]{:S(2)}) copy-start(bf16[448,256]{1,0:T(8,128)(2,1)} %param.17) | copy-start | bytes 688132
  178.7 54.0 %copy-start.12 = (f32[256]{0:T(256)S(1)}, f32[256]{0:T(256)}, u32[]{:S(2)}) copy-start(f32[256]{0:T(256)} %param.22) | copy-start | bytes 3076
  178.7 54.0 %all-to-all-start = ((bf16[128,16,256]{2,1,0:T(8,128)(2,1)}), bf16[128,16,256]{2,1,0:T(8,128)(2,1)S(1)}, u32[]{:S(2)}, u32[]{:S(2)}) async-start(bf16[128,16,256]{2,1,0:T(8,128)(2,1)} %select_select_fusion.1), calls=%async_computation | async-start | bytes 2097152 | tf_op jit(solution)/shard_map/all_to_all | solution.py:153
  182.5 143.1 %all-gather.5.cloned.1.call-start = ((), (), s32[]{:S(2)}) async-start(), calls=%async_computation.5 | async-start | bytes 1310720 | tf_op jit(solution)/shard_map/all_gather | solution.py:161
  183.3 429.8 %all-reduce.12.cloned.1.call-start = ((), (), s32[]{:S(2)}) async-start(), calls=%async_computation.7 | async-start | bytes 25165824
  270.5 20.2 %copy-start.9 = (bf16[1792,256]{1,0:T(8,128)(2,1)S(1)}, bf16[1792,256]{1,0:T(8,128)(2,1)}, u32[]{:S(2)}) copy-start(bf16[1792,256]{1,0:T(8,128)(2,1)} %all_gather.12) | copy-start | bytes 2752516
  290.7 2.9 copy-start.3
  293.6 15.2 %copy-start.17 = (f32[2048,256]{1,0:T(8,128)}, f32[2048,256]{1,0:T(8,128)S(1)}, u32[]{:S(2)}) copy-start(f32[2048,256]{1,0:T(8,128)S(1)} %fusion.26) | copy-start | bytes 6291460
  328.1 1.8 copy-start.4
  330.4 4.6 copy-start.5
  338.6 1.6 copy-start.7
  340.2 7.2 %copy-start.18 = (f32[2048,256]{1,0:T(8,128)S(1)}, f32[2048,256]{1,0:T(8,128)}, u32[]{:S(2)}) copy-start(f32[2048,256]{1,0:T(8,128)} %copy-done.17) | copy-start | bytes 6291460
  370.3 9.0 %copy-start.2 = (f32[64,8,8,128]{3,2,1,0:T(8,128)S(1)}, f32[64,8,8,128]{3,2,1,0:T(8,128)}, u32[]{:S(2)}) copy-start(f32[64,8,8,128]{3,2,1,0:T(8,128)} %convolution_bitcast_fusion.1) | copy-start | bytes 6291460
  381.0 1.0 copy-start.6
  381.1 237.9 %copy-start.1 = (bf16[128,16,512]{2,1,0:T(8,128)(2,1)S(1)}, bf16[128,16,512]{2,1,0:T(8,128)(2,1)}, u32[]{:S(2)}) copy-start(bf16[128,16,512]{2,1,0:T(8,128)(2,1)} %param.14) | copy-start | bytes 6291460
Sparse Core Ops, SparseCore 0:
  21.5 121.2 all-gather.2
  175.5 91.9 reduce-scatter.1
  269.1 28.2 all-gather.4
  381.2 231.8 all-reduce.11
where the time goes:
time: 635 us; the launch traced here: 626 us
  waiting for transfers between devices  257 us (40%)
  blocking collectives  133 us (21%)
  local copies, waits for them, and re-layouts  106 us (17%)
  matrix products  61.1 us (10%)
  other arithmetic  45.3 us (7%)
  between operations  14.5 us (2%)
  starting transfers between devices  9.23 us (1%)
    unnamed x5, waiting for transfers between devices  231 us
    all_to_all x1, blocking collectives, teacher_forward(): lax.all_to_all(activated, 'fsdp', split_axis=2, concat_axis=0, tiled=True)  83.5 us
    unnamed x53, local copies, waits for them, and re-layouts  52.8 us
    all_gather x1, blocking collectives, on_device(): lax.all_gather(kernel_dilated, 'fsdp', axis=0, tiled=True)  33.7 us
    all_to_all x1, waiting for transfers between devices, on_device(): lax.all_to_all(packed(teacher_tiles), 'dp', split_axis=0, concat_axis=0,...  25.9 us
    another operation x2, local copies, waits for them, and re-layouts, unfold_dilated(): return jnp.stack(tap_offsets, axis=2).reshape(tile_count * TILE_FRAMES, -1)  15.6 us
    all_gather x1, blocking collectives, on_device(): lax.all_gather(kernel_mix, 'fsdp', axis=0, tiled=True)  15.5 us
    dot_general x1, matrix products, student_step(): jnp.dot(act_two, kernel_mix, preferred_element_type=jnp.float32)  15.2 us
  transfers between devices with their start and end apart: 6, of which 2 were waited for; matrix products, arithmetic and copies ran while one was open for 23% of the time, Pallas kernels for 0%

commit v1 on v0

v1 whole, which is shorter than its diff:
```python
import jax
import jax.numpy as jnp
from jax import lax
from jax.experimental import pallas as pl
from jax.experimental.pallas import tpu as pltpu
from jax.sharding import PartitionSpec as P

CT = 512
DL = 1024
CS = 256
CSO = 512
KS = 16
STRIDE = 8
DILATED_TAPS = 7
UNIT_DILATION = 3
TILE_FRAMES = 16
TILE_DEV = 128
OUTF = 2
MARGIN = (KS - STRIDE) // 2
ROWS = TILE_DEV * TILE_FRAMES
LATENTS = TILE_DEV * OUTF
N_FSDP = 4
QUARTER = CT // N_FSDP
GROUP = 16
SLABS = 4
F32 = jnp.float32
BF16 = jnp.bfloat16
VMEM_LIMIT = 48 * 1024 * 1024

PACK = {
    "dilated": DILATED_TAPS * CS // N_FSDP // SLABS,
    "mix": CS // N_FSDP // SLABS,
    "down": KS * CS // N_FSDP // SLABS,
    "proj": CSO // N_FSDP // SLABS,
}
PACK_COLS = {"dilated": 1, "mix": 1, "down": 2, "proj": 4}
PACK_ROWS = sum(PACK[name] * PACK_COLS[name] for name in PACK)

INV_PI = 0.3183098861837907
PI_PARTS = (3.125, 0.015625, 9.67502593994140625e-4, 1.509957990978376432e-7)
SIN_TERMS = (0.9999999765137553, -0.16666647593489264, 0.008332899222829617, -0.0001980086530702378, 2.5904300303557895e-06)
COS_TERMS = (0.999999953036273, -0.4999990494860951, 0.0416635772644784, -0.0013853657929132671, 2.3153011971441464e-05)


def _reduced(angle):
    turns = jnp.round(angle * INV_PI)
    for part in PI_PARTS:
        angle = angle - turns * part
    return angle


def _series(square, terms):
    total = square * terms[-1] + terms[-2]
    for term in terms[-3::-1]:
        total = total * square + term
    return total


def _snake(values, alpha, inverse):
    angle = _reduced(alpha * values)
    sine = angle * _series(angle * angle, SIN_TERMS)
    return values + sine * sine * inverse


def _snake_and_slope(values, alpha, inverse):
    angle = _reduced(alpha * values)
    square = angle * angle
    sine = angle * _series(square, SIN_TERMS)
    cosine = _series(square, COS_TERMS)
    return values + sine * sine * inverse, 1.0 + 2.0 * sine * cosine


def _dot(left, right):
    return jnp.dot(left, right, preferred_element_type=F32)


def _dot_nt(left, right):
    return lax.dot_general(left, right, (((1,), (1,)), ((), ())), preferred_element_type=F32)


def _dot_tn(left, right):
    return lax.dot_general(left, right, (((0,), (0,)), ((), ())), preferred_element_type=F32)


def _frame_major(block):
    count = GROUP * TILE_FRAMES
    target = lax.broadcasted_iota(jnp.int32, (count, count), 0)
    source = lax.broadcasted_iota(jnp.int32, (count, count), 1)
    wanted = (target % GROUP) * TILE_FRAMES + target // GROUP
    turn = jnp.where(source == wanted, 1.0, 0.0).astype(BF16)
    return _dot(turn, block)


def _teacher_act_kernel(place, tiles, alpha, *quarters):
    inverse = 1.0 / alpha[...]
    acted = _snake(_frame_major(tiles[...]), alpha[...], inverse).astype(BF16)
    del place
    for index, quarter in enumerate(quarters):
        part = acted[:, index * QUARTER : (index + 1) * QUARTER]
        quarter[...] = part.reshape(TILE_FRAMES, GROUP, QUARTER)


def _teacher_act(place, tiles, alpha):
    steps = TILE_DEV // GROUP
    shape = jax.ShapeDtypeStruct((TILE_FRAMES, TILE_DEV, QUARTER), BF16)
    return pl.pallas_call(
        _teacher_act_kernel,
        grid=(steps,),
        in_specs=[
            pl.BlockSpec(memory_space=pltpu.SMEM),
            pl.BlockSpec((GROUP * TILE_FRAMES, CT), lambda i: (i, 0)),
            pl.BlockSpec((1, CT), lambda i: (0, 0)),
        ],
        out_specs=[pl.BlockSpec((TILE_FRAMES, GROUP, QUARTER), lambda i: (0, i, 0))] * N_FSDP,
        out_shape=[shape] * N_FSDP,
        name="teacher_act",
        compiler_params=pltpu.CompilerParams(vmem_limit_bytes=VMEM_LIMIT),
        cost_estimate=pl.CostEstimate(flops=ROWS * CT * 512, bytes_accessed=4 * ROWS * CT, transcendentals=0),
    )(place, tiles.reshape(ROWS, CT), alpha.reshape(1, CT))


def _teacher_dot_kernel(frames, kernel, out):
    reach = STRIDE + MARGIN
    for offset in range(OUTF):
        first = max(0, STRIDE * offset - MARGIN)
        tap = first - (STRIDE * offset - MARGIN)
        wide = jnp.concatenate([frames[first + step] for step in range(reach)], axis=1)
        part = _dot(wide, kernel[tap * QUARTER : (tap + reach) * QUARTER, :])
        out[offset * TILE_DEV : (offset + 1) * TILE_DEV, :] = part.astype(out.dtype)


def _teacher_dot(frames, kernel, dtype):
    return pl.pallas_call(
        _teacher_dot_kernel,
        out_shape=jax.ShapeDtypeStruct((LATENTS, DL), dtype),
        name="teacher_dot",
        compiler_params=pltpu.CompilerParams(vmem_limit_bytes=VMEM_LIMIT),
        cost_estimate=pl.CostEstimate(
            flops=2 * LATENTS * 12 * QUARTER * DL, bytes_accessed=2 * KS * QUARTER * DL, transcendentals=0
        ),
    )(frames, kernel)


def _forward_kernel(
    place, tiles, own, other, alphas, routes,
    act_one, act_two, act_three, slope_two, slope_three, student, predicted, slots, mix, down, proj,
    dilated, held, sems,
):
    core = place[0]
    copies = []
    for half, (source, side) in enumerate(((own, core), (other, 1 - core))):
        row = 0
        for number, (name, target) in enumerate((("dilated", dilated), ("mix", mix), ("down", down), ("proj", proj))):
            rows, cols = PACK[name], PACK_COLS[name]
            view = target.reshape(N_FSDP, SLABS, rows, 2 * cols * 128)
            for col in range(cols):
                begin = pl.multiple_of(side * (cols * 128) + col * 128, 128)
                for slab in range(SLABS):
                    copies.append((number, pltpu.make_async_copy(
                        source.at[slab, :, pl.ds(row, rows), :],
                        view.at[:, slab, :, pl.ds(begin, 128)],
                        sems.at[number, half, slab * cols + col],
                    )))
                row += rows
    for _, copy in copies:
        copy.start()

    alpha_one, alpha_two, alpha_three = alphas[0:1, :], alphas[1:2, :], alphas[2:3, :]
    inverse_one, inverse_two, inverse_three = 1.0 / alpha_one, 1.0 / alpha_two, 1.0 / alpha_three
    for step in range(TILE_DEV // GROUP):
        turned = _frame_major(tiles[step * GROUP * TILE_FRAMES : (step + 1) * GROUP * TILE_FRAMES, :])
        shape = (TILE_FRAMES, GROUP, CS)
        held[:, step * GROUP : (step + 1) * GROUP, :] = turned.astype(BF16).reshape(shape)
        acted = _snake(turned, alpha_one, inverse_one).astype(BF16)
        act_one[:, step * GROUP : (step + 1) * GROUP, :] = acted.reshape(shape)

    def ready(wanted):
        for number, copy in copies:
            if number == wanted:
                copy.wait()

    ready(0)
    ready(1)
    half_taps = DILATED_TAPS // 2
    spans = []
    for frame in range(TILE_FRAMES):
        valid = [tap for tap in range(DILATED_TAPS) if 0 <= frame + UNIT_DILATION * (tap - half_taps) < TILE_FRAMES]
        span = (valid[0], valid[-1] + 1)
        if spans and spans[-1][2] == span:
            spans[-1][1] = frame + 1
        else:
            spans.append([frame, frame + 1, span])
    for start, stop, (low, high) in spans:
        wide = jnp.concatenate(
            [
                act_one[start + shift : stop + shift].reshape((stop - start) * TILE_DEV, CS)
                for shift in (UNIT_DILATION * (tap - half_taps) for tap in range(low, high))
            ],
            axis=1,
        )
        hidden = _dot(wide, dilated[low * CS : high * CS, :])
        acted, slope = _snake_and_slope(hidden, alpha_two, inverse_two)
        shape = (stop - start, TILE_DEV, CS)
        acted = acted.astype(BF16)
        act_two[start:stop] = acted.reshape(shape)
        slope_two[start:stop] = slope.reshape(shape)
        residual = held[start:stop].reshape((stop - start) * TILE_DEV, CS).astype(F32) + _dot(acted, mix[...])
        acted, slope = _snake_and_slope(residual, alpha_three, inverse_three)
        act_three[start:stop] = acted.astype(BF16).reshape(shape)
        slope_three[start:stop] = slope.reshape(shape)

    ready(2)
    reach = STRIDE + MARGIN
    for offset in range(OUTF):
        first = max(0, STRIDE * offset - MARGIN)
        tap = first - (STRIDE * offset - MARGIN)
        wide = jnp.concatenate([act_three[first + step] for step in range(reach)], axis=1)
        part = _dot(wide, down[tap * CS : (tap + reach) * CS, :])
        student[offset * TILE_DEV : (offset + 1) * TILE_DEV, :] = part.astype(BF16)
    ready(3)
    pick = jnp.where(
        routes[...] == lax.broadcasted_iota(jnp.int32, (TILE_DEV, TILE_DEV), 1), 1.0, 0.0
    ).astype(BF16)
    for offset in range(OUTF):
        rows = slice(offset * TILE_DEV, (offset + 1) * TILE_DEV)
        part = _dot(student[rows, :], proj[...])
        predicted[rows, :] = part
        slots[:, offset * DL : (offset + 1) * DL] = _dot(pick, part.astype(BF16)).astype(BF16)


def _forward(place, tiles, own, other, alphas, routes):
    frames = (TILE_FRAMES, TILE_DEV, CS)
    whole = pl.BlockSpec(memory_space=pltpu.VMEM)
    return pl.pallas_call(
        _forward_kernel,
        in_specs=[
            pl.BlockSpec(memory_space=pltpu.SMEM),
            whole,
            pl.BlockSpec(memory_space=pl.ANY),
            pl.BlockSpec(memory_space=pl.ANY),
            whole,
            whole,
        ],
        out_specs=[whole] * 11,
        out_shape=[
            jax.ShapeDtypeStruct(frames, BF16),
            jax.ShapeDtypeStruct(frames, BF16),
            jax.ShapeDtypeStruct(frames, BF16),
            jax.ShapeDtypeStruct(frames, F32),
            jax.ShapeDtypeStruct(frames, F32),
            jax.ShapeDtypeStruct((LATENTS, CSO), BF16),
            jax.ShapeDtypeStruct((LATENTS, DL), F32),
            jax.ShapeDtypeStruct((TILE_DEV, OUTF * DL), BF16),
            jax.ShapeDtypeStruct((CS, CS), BF16),
            jax.ShapeDtypeStruct((KS * CS, CSO), BF16),
            jax.ShapeDtypeStruct((CSO, DL), BF16),
        ],
        scratch_shapes=[
            pltpu.VMEM((DILATED_TAPS * CS, CS), BF16),
            pltpu.VMEM(frames, BF16),
            pltpu.SemaphoreType.DMA((4, 2, 16)),
        ],
        name="student_forward",
        compiler_params=pltpu.CompilerParams(vmem_limit_bytes=VMEM_LIMIT),
        cost_estimate=pl.CostEstimate(flops=4_000_000_000, bytes_accessed=30_000_000, transcendentals=0),
    )(place, tiles.reshape(ROWS, CS), own, other, alphas, routes)


def _stacked(values, columns):
    return jnp.concatenate(
        [values[:, start : start + columns] for start in range(0, values.shape[1], columns)], axis=0
    )


def _strided_kernel(
    place, target_own, target_one, target_two, target_three, predicted, weights, student, proj, act_three,
    back_student, send_a, send_b, keep_a, keep_b, error, grad_proj, padded,
):
    me = place[1]
    weight = weights[...] * (1.0 / LATENTS)
    for offset in range(OUTF):
        rows = slice(offset * TILE_DEV, (offset + 1) * TILE_DEV)
        target = target_own[rows, :] + target_one[rows, :].astype(F32)
        target += target_two[rows, :].astype(F32)
        target += target_three[rows, :].astype(F32)
        target = target.astype(BF16).astype(F32)
        error[rows, :] = (weight * (predicted[rows, :] - target)).astype(BF16)
    back = _dot_nt(error[...], proj[...]).astype(BF16)
    back_student[...] = back
    grad_proj[...] = _dot_tn(student[...], error[...])

    blank = jnp.zeros((MARGIN, TILE_DEV, CS), BF16)
    padded[0:MARGIN] = blank
    padded[MARGIN : MARGIN + TILE_FRAMES] = act_three[...]
    padded[MARGIN + TILE_FRAMES :] = blank

    for pair in range(KS):
        tap = (me // 2) ^ pair
        wide = jnp.concatenate([padded[tap + STRIDE * offset] for offset in range(OUTF)], axis=0)
        grad = _dot_tn(wide, back)
        outs = (send_a, send_b) if (pair // 2) % 2 else (keep_a, keep_b)
        slot = (pair // 4) * 4 + (pair % 2) * 2
        for half in range(2):
            spot = slot + (half ^ (me % 2))
            part = grad[half * 128 : (half + 1) * 128, :]
            share = grad_proj[pl.ds(pl.multiple_of((tap * 2 + half) * 16, 16), 16), :]
            for index, out in enumerate(outs):
                out[spot, 0:128, :] = part[:, index * 256 : (index + 1) * 256].astype(out.dtype)
                out[spot, 128:160, :] = _stacked(share[:, index * 512 : (index + 1) * 512], 256).astype(out.dtype)


def _strided(place, targets, predicted, weights, student, proj, act_three):
    whole = pl.BlockSpec(memory_space=pltpu.VMEM)
    half = (16, 160, 256)
    return pl.pallas_call(
        _strided_kernel,
        in_specs=[pl.BlockSpec(memory_space=pltpu.SMEM)] + [whole] * 9,
        out_specs=[whole] * 5,
        out_shape=[
            jax.ShapeDtypeStruct((LATENTS, CSO), BF16),
            jax.ShapeDtypeStruct(half, BF16),
            jax.ShapeDtypeStruct(half, BF16),
            jax.ShapeDtypeStruct(half, F32),
            jax.ShapeDtypeStruct(half, F32),
        ],
        scratch_shapes=[
            pltpu.VMEM((LATENTS, DL), BF16),
            pltpu.VMEM((CSO, DL), F32),
            pltpu.VMEM((TILE_FRAMES + 2 * MARGIN, TILE_DEV, CS), BF16),
        ],
        name="strided_backward",
        compiler_params=pltpu.CompilerParams(vmem_limit_bytes=VMEM_LIMIT),
        cost_estimate=pl.CostEstimate(flops=2_000_000_000, bytes_accessed=16_000_000, transcendentals=0),
    )(place, *targets, predicted, weights, student, proj, act_three)


def _residual_kernel(
    place, back_student, down, mix, act_one, act_two, slope_two, slope_three,
    send, keep, back_three, back_residual, back_hidden, grad_dilated, grad_mix,
):
    me = place[1]
    back = back_student[...]
    for tap in range(KS):
        part = _dot_nt(back, down[tap * CS : (tap + 1) * CS, :])
        for offset in range(OUTF):
            frame = STRIDE * offset - MARGIN + tap
            if 0 <= frame < TILE_FRAMES:
                piece = part[offset * TILE_DEV : (offset + 1) * TILE_DEV, :]
                if offset == 0 and frame >= MARGIN:
                    back_three[frame] += piece
                else:
                    back_three[frame] = piece
    for frame in range(0, TILE_FRAMES, 2):
        rows = slice(frame * TILE_DEV, (frame + 2) * TILE_DEV)
        shape = (2 * TILE_DEV, CS)
        share = back_three[frame : frame + 2].reshape(shape) * slope_three[frame : frame + 2].reshape(shape)
        share = share.astype(BF16)
        back_residual[rows, :] = share
        share = _dot_nt(share, mix[...]) * slope_two[frame : frame + 2].reshape(shape)
        back_hidden[rows, :] = share.astype(BF16)
    grad_mix[...] = _dot_tn(act_two[...].reshape(ROWS, CS), back_residual[...])
    half_taps = DILATED_TAPS // 2
    for tap in range(DILATED_TAPS):
        shift = UNIT_DILATION * (tap - half_taps)
        first, last = max(0, -shift), min(TILE_FRAMES, TILE_FRAMES - shift)
        rows = (last - first) * TILE_DEV
        grad_dilated[tap * CS : (tap + 1) * CS, :] = _dot_tn(
            act_one[first + shift : last + shift].reshape(rows, CS), back_hidden[first * TILE_DEV : last * TILE_DEV, :]
        )
    for place_index in range(32):
        chunk = me ^ place_index
        part = jnp.concatenate(
            [
                grad_dilated[pl.ds(pl.multiple_of(chunk * 56, 8), 56), :],
                grad_mix[pl.ds(pl.multiple_of(chunk * 8, 8), 8), :],
            ],
            axis=0,
        )
        out = send if (place_index // 4) % 2 else keep
        out[(place_index // 8) * 4 + place_index % 4] = part.astype(out.dtype)


def _residual(place, back_student, down, mix, act_one, act_two, slope_two, slope_three):
    whole = pl.BlockSpec(memory_space=pltpu.VMEM)
    half = (16, 64, 256)
    return pl.pallas_call(
        _residual_kernel,
        in_specs=[pl.BlockSpec(memory_space=pltpu.SMEM)] + [whole] * 7,
        out_specs=[whole] * 2,
        out_shape=[jax.ShapeDtypeStruct(half, BF16), jax.ShapeDtypeStruct(half, F32)],
        scratch_shapes=[
            pltpu.VMEM((TILE_FRAMES, TILE_DEV, CS), F32),
            pltpu.VMEM((ROWS, CS), BF16),
            pltpu.VMEM((ROWS, CS), BF16),
            pltpu.VMEM((DILATED_TAPS * CS, CS), F32),
            pltpu.VMEM((CS, CS), F32),
        ],
        name="residual_backward",
        compiler_params=pltpu.CompilerParams(vmem_limit_bytes=VMEM_LIMIT),
        cost_estimate=pl.CostEstimate(flops=3_500_000_000, bytes_accessed=16_000_000, transcendentals=0),
    )(place, back_student, down, mix, act_one, act_two, slope_two, slope_three)


def _swap(values, axis, bit):
    return lax.ppermute(values, axis, [(i, i ^ bit) for i in range(lax.axis_size(axis))])


def _share_of(kernel, slab, side):
    rows, cols = kernel.shape[0] // SLABS, kernel.shape[1] // 2
    part = lax.dynamic_slice(kernel, (slab * rows, side * cols), (rows, cols))
    return _stacked(part, 128)


def on_device(
    student_tiles,
    teacher_tiles,
    send_list,
    clip_weight,
    kernel_dilated,
    kernel_mix,
    kernel_down,
    kernel_proj,
    kernel_teacher,
    alpha_one,
    alpha_two,
    alpha_three,
    alpha_teacher,
):
    n_dp = lax.axis_size("dp")
    d, f = lax.axis_index("dp"), lax.axis_index("fsdp")
    core, slab = d % 2, (d // 2) % SLABS
    halving = n_dp == 8
    me = d * N_FSDP + f if halving else jnp.int32(0)
    place = jnp.stack([core, me]).astype(jnp.int32)

    routes = send_list.reshape(-1)
    cap = TILE_DEV // n_dp
    all_weights = lax.all_gather(clip_weight, "dp", axis=0, tiled=False)
    slot_weights = lax.dynamic_slice(all_weights, (0, d * cap), (n_dp, cap)).reshape(-1)
    hits = routes[:, None] == jnp.arange(TILE_DEV, dtype=jnp.int32)[None, :]
    weights = jnp.sum(jnp.where(hits, slot_weights[:, None], 0.0), axis=0)[:, None]

    quarters = jnp.stack(_teacher_act(place, teacher_tiles, alpha_teacher))
    flat_teacher = kernel_teacher.reshape(KS * QUARTER, DL)
    partials = []
    for bit in range(1, N_FSDP):
        sent = _swap(lax.dynamic_index_in_dim(quarters, f ^ bit, 0, keepdims=False), "fsdp", bit)
        partials.append(_swap(_teacher_dot(sent, flat_teacher, BF16), "fsdp", bit))
    own_partial = _teacher_dot(lax.dynamic_index_in_dim(quarters, f, 0, keepdims=False), flat_teacher, F32)

    packed = jnp.concatenate(
        [_share_of(k, slab, core) for k in (kernel_dilated, kernel_mix, kernel_down, kernel_proj)], axis=0
    )
    packed = lax.all_gather(packed, "fsdp", axis=0, tiled=False)
    planes = [[base + 2 * i + c for i in range(SLABS)] for base in range(0, n_dp, 8) for c in range(2)]
    own = lax.all_gather(packed, "dp", axis=0, tiled=False, axis_index_groups=planes)
    other = _swap(own, "dp", 1)

    alphas = jnp.stack([alpha_one, alpha_two, alpha_three])
    (
        act_one, act_two, act_three, slope_two, slope_three, student, predicted, slots, mix, down, proj,
    ) = _forward(place, student_tiles, own, other, alphas, routes[:, None])
    latent = lax.all_to_all(slots, "dp", split_axis=0, concat_axis=0, tiled=True).reshape(TILE_DEV, OUTF, DL)

    back_student, send_a, send_b, keep_a, keep_b = _strided(
        place, (own_partial, *partials), predicted, weights, student, proj, act_three
    )
    send_s, keep_s = _residual(place, back_student, down, mix, act_one, act_two, slope_two, slope_three)

    if halving:
        def halve(keep, received, axis_bit):
            total = keep + received.astype(F32)
            return total[0], total[1].astype(BF16), axis_bit

        def reduce_plane(send, keep, order):
            rows = keep.shape[1]
            keep = keep.reshape(2, 2, N_FSDP, rows, 256)
            received = _swap(send, "dp", 1).reshape(keep.shape)
            if order == "xy":
                keep, received = jnp.swapaxes(keep, 0, 1), jnp.swapaxes(received, 0, 1)
            bits = (2, 4) if order == "xy" else (4, 2)
            for bit in bits:
                keep, out, _ = halve(keep, received, bit)
                received = _swap(out, "dp", bit)
            return keep + received.astype(F32)

        parts = [
            reduce_plane(send_a, keep_a, "xy"),
            reduce_plane(send_b, keep_b, "yx"),
            reduce_plane(send_s, keep_s, "xy"),
        ]
        finals = []
        for part in parts:
            total = part[0]
            for bit in range(1, N_FSDP):
                total = total + _swap(part[bit].astype(BF16), "fsdp", bit).astype(F32)
            finals.append(total)
        part_a, part_b, part_s = finals
        grad_down = jnp.concatenate([part_a[:128], part_b[:128]], axis=1).reshape(-1)
        grad_proj = jnp.concatenate(
            [part_a[128:144], part_a[144:160], part_b[128:144], part_b[144:160]], axis=1
        ).reshape(-1)
        grad_dilated, grad_mix = part_s[:56].reshape(-1), part_s[56:].reshape(-1)
    else:
        def joined(send, keep):
            rows = keep.shape[1]
            both = jnp.stack([keep.reshape(4, 4, rows, 256), send.astype(F32).reshape(4, 4, rows, 256)], axis=1)
            return both.reshape(32, rows, 256)

        part_a, part_b, part_s = joined(send_a, keep_a), joined(send_b, keep_b), joined(send_s, keep_s)

        def scattered(values):
            return lax.psum_scatter(values.reshape(-1), ("dp", "fsdp"), scatter_dimension=0, tiled=True)

        grad_down = scattered(jnp.concatenate([part_a[:, :128], part_b[:, :128]], axis=2))
        grad_proj = scattered(
            jnp.concatenate([part_a[:, 128:144], part_a[:, 144:], part_b[:, 128:144], part_b[:, 144:]], axis=2)
        )
        grad_dilated, grad_mix = scattered(part_s[:, :56]), scattered(part_s[:, 56:])
    return latent, grad_dilated, grad_mix, grad_down, grad_proj


def solution(mesh):
    placed = (
        P(("dp", "fsdp"), None, None),
        P(("dp", "fsdp"), None, None),
        P("dp", "fsdp", None),
        P(("dp", "fsdp")),
        P("fsdp", None),
        P("fsdp", None),
        P("fsdp", None),
        P("fsdp", None),
        P(None, "fsdp", None),
        P(),
        P(),
        P(),
        P(),
    )
    return jax.shard_map(
        on_device,
        mesh=mesh,
        in_specs=placed,
        out_specs=(
            P(("dp", "fsdp"), None, None),
            P(("dp", "fsdp")),
            P(("dp", "fsdp")),
            P(("dp", "fsdp")),
            P(("dp", "fsdp")),
        ),
        check_vma=False,
    )
```

time: 635 us -> 275 us (0.43); the launches traced: 626 us -> 274 us
  waiting for transfers between devices: 257 us -> 135 us
  blocking collectives: 133 us -> 30.4 us
  local copies, waits for them, and re-layouts: 106 us -> 18.6 us
  matrix products: 61.1 us -> 0 us
  other arithmetic: 45.3 us -> 5.46 us
  Pallas kernels: 0 us -> 38.8 us
  starting transfers between devices: 9.23 us -> 31.2 us
    unnamed x5 -> x1, waiting for transfers between devices: 231 us -> 0.02 us
    ppermute x0 -> x25, waiting for transfers between devices: none -> 87.2 us  [_swap(): lax.ppermute(values, axis, [(i, i ^ bit) for i in range(lax.axis_size(axi...]
    all_to_all x1 -> x0, blocking collectives: 83.5 us -> none  [teacher_forward(): lax.all_to_all(activated, 'fsdp', split_axis=2, concat_axis=0, tiled=True)]
    dot_general x11 -> x0, matrix products: 61.1 us -> none  [the longest x1 15.2 us: student_step(): jnp.dot(act_two, kernel_mix, preferred_element_type=jnp.float32)]
    all_gather x2 -> x1, waiting for transfers between devices: 0.04 us -> 43.8 us  [on_device(): lax.all_gather(packed, 'dp', axis=0, tiled=False, axis_index_groups=planes)]
    pallas_call x0 -> x8, Pallas kernels: none -> 38.8 us  [the longest x1 16.1 us: _forward(): pl.pallas_call(_forward_kernel, in_specs=[pl.BlockSpec(memory_space=pltpu...]
    unnamed x53 -> x43, local copies, waits for them, and re-layouts: 52.8 us -> 14.1 us
    convert_element_type x4 -> x0, other arithmetic: 30.8 us -> none  [the longest x1 15 us: teacher_forward(): activated = snake(tiles, alpha_teacher).astype(jnp.bfloat16)]
  transfers between devices with their start and end apart: 6 -> 27, of which waited for: 2 -> 13; matrix products, arithmetic and copies ran while one was open for 23% -> 4% of each run, Pallas kernels for 0% -> 9%
where the time goes in v1:
time: 275 us; the launch traced here: 274 us
  waiting for transfers between devices  135 us (49%)
  Pallas kernels  38.8 us (14%)
  starting transfers between devices  31.2 us (11%)
  blocking collectives  30.4 us (11%)
  local copies, waits for them, and re-layouts  18.6 us (7%)
  between operations  14.6 us (5%)
  other arithmetic  5.46 us (2%)
    ppermute x25, waiting for transfers between devices, _swap(): lax.ppermute(values, axis, [(i, i ^ bit) for i in range(lax.axis_size(axi...  87.2 us
    all_gather x1, waiting for transfers between devices, on_device(): lax.all_gather(packed, 'dp', axis=0, tiled=False, axis_index_groups=planes)  43.8 us
    ppermute x25, starting transfers between devices, _swap(): lax.ppermute(values, axis, [(i, i ^ bit) for i in range(lax.axis_size(axi...  27.6 us
    all_gather x1, blocking collectives, on_device(): packed = lax.all_gather(packed, 'fsdp', axis=0, tiled=False)  21.7 us
    pallas_call x1, Pallas kernels, _forward(): pl.pallas_call(_forward_kernel, in_specs=[pl.BlockSpec(memory_space=pltpu...  16.1 us
    unnamed x43, local copies, waits for them, and re-layouts  14.1 us
    all_gather x1, blocking collectives, on_device(): all_weights = lax.all_gather(clip_weight, 'dp', axis=0, tiled=False)  8.68 us
    pallas_call x1, Pallas kernels, _strided(): pl.pallas_call(_strided_kernel, in_specs=[pl.BlockSpec(memory_space=pltpu...  6.92 us
  transfers between devices with their start and end apart: 27, of which 13 were waited for; matrix products, arithmetic and copies ran while one was open for 4% of the time, Pallas kernels for 9%

profile of v1, /device:TPU:0, one launch (start us, length us, event | category | flops | bytes accessed | tf_op | source)
XLA Modules:
  0.0 274.1 jit_solution(17447247351468707691)
XLA Ops:
  13.4 21.7 %all-gather = bf16[3072,128]{1,0:T(8,128)(2,1)} all-gather(bf16[768,128]{1,0:T(8,128)(2,1)S(1)} %constant_dynamic-update-slice_fusion), channel_id=2, replica_groups=mesh['dp'=8,'fsdp'=4] {'fsdp'}, dimensions={0}, use_global_device_ids=true | all-gather | bytes 983040 | tf_op jit(solution)/shard_map/all_gather | solution.py:454
  35.1 43.8 %all-gather.6.cloned.1.call-done = bf16[16,768,128]{2,1,0:T(8,128)(2,1)} async-done(((bf16[4,768,128]{2,1,0:T(8,128)(2,1)}), bf16[16,768,128]{2,1,0:T(8,128)(2,1)}) %all-gather.6.cloned.1.call-update) | async-done | bytes 3145744 | tf_op jit(solution)/shard_map/all_gather | solution.py:456
  79.0 5.5 %teacher_act.1 = (bf16[16,128,128]{2,1,0:T(8,128)(2,1)S(1)}, bf16[16,128,128]{2,1,0:T(8,128)(2,1)S(1)}, bf16[16,128,128]{2,1,0:T(8,128)(2,1)S(1)}, bf16[16,128,128]{2,1,0:T(8,128)(2,1)S(1)}) custom-call(s32[2]{0:T(128)S(1)} %pad_add_fusion.place, bf16[2048,512]{1,0:T(8,128)(2,1)S(1)} %bitcast.130, f32[1,512]{1,0:T(1,128)S(1)} %bitcast.135), custom_call_target="tpu_custom_call" | custom-call | flops 536870912 | bytes 4194304 | tf_op jit(solution)/shard_map/teacher_act/pallas_call | solution.py:106
  85.8 3.3 %collective-permute-start.5 = (bf16[16,128,128]{2,1,0:T(8,128)(2,1)S(1)}, bf16[16,128,128]{2,1,0:T(8,128)(2,1)S(1)}, u32[]{:S(2)}, u32[]{:S(2)}) collective-permute-start(bf16[16,128,128]{2,1,0:T(8,128)(2,1)S(1)} %get-tuple-element.55), channel_id=1, source_target_pairs={{0,3},{1,2},{2,1},{3,0},{4,7},{5,6},{6,5},{7,4},{8,11},{9,10},{10,... | collective-permute-start | bytes 1572872 | tf_op jit(solution)/shard_map/ppermute | solution.py:405
  90.2 8.7 %all-gather.3 = f32[8,1,128]{2,1,0:T(1,128)S(1)} all-gather(f32[1,1,128]{2,1,0:T(1,128)S(1)} %bitcast.154), channel_id=4, replica_groups=mesh['dp'=8,'fsdp'=4] {'dp'}, dimensions={0}, use_global_device_ids=true | all-gather | bytes 4608 | tf_op jit(solution)/shard_map/all_gather | solution.py:438
  99.1 3.3 %collective-permute-done.5.frames = bf16[16,128,128]{2,1,0:T(8,128)(2,1)S(1)} collective-permute-done((bf16[16,128,128]{2,1,0:T(8,128)(2,1)S(1)}, bf16[16,128,128]{2,1,0:T(8,128)(2,1)S(1)}, u32[]{:S(2)}, u32[]{:S(2)}) %collective-permute-start.5) | collective-permute-done | bytes 524320 | tf_op jit(solution)/shard_map/ppermute | solution.py:405
  102.4 2.2 copy-done
  105.7 3.4 %collective-permute-start.6 = (bf16[256,1024]{1,0:T(8,128)(2,1)S(1)}, bf16[256,1024]{1,0:T(8,128)(2,1)}, u32[]{:S(2)}, u32[]{:S(2)}) collective-permute-start(bf16[256,1024]{1,0:T(8,128)(2,1)S(1)} %teacher_dot.7), channel_id=1, source_target_pairs={{0,3},{1,2},{2,1},{3,0},{4,7},{5,6},{6,5},{7,4},{8,11},{9,10},{10,... | collective-permute-start | bytes 1572872 | tf_op jit(solution)/shard_map/ppermute | solution.py:405
  109.1 37.3 %collective-permute-done.3.frames = bf16[16,128,128]{2,1,0:T(8,128)(2,1)S(1)} collective-permute-done((bf16[16,128,128]{2,1,0:T(8,128)(2,1)}, bf16[16,128,128]{2,1,0:T(8,128)(2,1)S(1)}, u32[]{:S(2)}, u32[]{:S(2)}) %collective-permute-start.3) | collective-permute-done | bytes 524320 | tf_op jit(solution)/shard_map/ppermute | solution.py:405
  148.5 3.0 %collective-permute-start.2 = (bf16[256,1024]{1,0:T(8,128)(2,1)S(1)}, bf16[256,1024]{1,0:T(8,128)(2,1)}, u32[]{:S(2)}, u32[]{:S(2)}) collective-permute-start(bf16[256,1024]{1,0:T(8,128)(2,1)S(1)} %teacher_dot.5), channel_id=1, source_target_pairs={{0,1},{1,0},{2,3},{3,2},{4,5},{5,4},{6,7},{7,6},{8,9},{9,8},{10,11... | collective-permute-start | bytes 1572872 | tf_op jit(solution)/shard_map/ppermute | solution.py:405
  152.8 16.1 %student_forward.1 = (bf16[16,128,256]{2,1,0:T(8,128)(2,1)S(1)}, bf16[16,128,256]{2,1,0:T(8,128)(2,1)S(1)}, bf16[16,128,256]{2,1,0:T(8,128)(2,1)S(1)}, f32[16,12...) custom-call(s32[2]{0:T(128)S(1)} %pad_add_fusion.place, ...), custom_call_target="tpu_custom_call" | custom-call | flops 4000000000 | bytes 30000000 | tf_op jit(solution)/shard_map/student_forward/pallas_call | solution.py:234
  169.8 9.9 %collective-permute-done.4.target_two = bf16[256,1024]{1,0:T(8,128)(2,1)} collective-permute-done((bf16[256,1024]{1,0:T(8,128)(2,1)S(1)}, bf16[256,1024]{1,0:T(8,128)(2,1)}, u32[]{:S(2)}, u32[]{:S(2)}) %collective-permute-start.4) | collective-permute-done | bytes 524320 | tf_op jit(solution)/shard_map/ppermute | solution.py:405
  179.8 1.2 copy-done.5
  181.0 6.9 %strided_backward.1 = (bf16[256,512]{1,0:T(8,128)(2,1)S(1)}, bf16[16,160,256]{2,1,0:T(8,128)(2,1)}, bf16[16,160,256]{2,1,0:T(8,128)(2,1)}, f32[16,160,256]{2,1,0:T(8,128)}, f32[16,160,256]{2,1,0:T(8,128)}) custom-call(s32[2]{0:T(128)S(1)} %pad_add_fusion.place, f32[256,1024]{1,0:T(8,128)S(1)} %teacher_dot.4.target_own, ...), custom_call_target="tpu_custom_call" | custom-call | flops 2000000000 | bytes 16000000 | tf_op jit(solution)/shard_map/strided_backward/pallas_call | solution.py:315
  187.9 6.3 %residual_backward.1 = (bf16[16,64,256]{2,1,0:T(8,128)(2,1)S(1)}, f32[16,64,256]{2,1,0:T(8,128)S(1)}) custom-call(s32[2]{0:T(128)S(1)} %pad_add_fusion.place, bf16[256,512]{1,0:T(8,128)(2,1)S(1)} %get-tuple-element.36.back_student, bf16[4096,512]{1,0:T(8,128)(2,1)} %get-tuple-element.37.down, bf16[256,256]{1,0:T(8,128)(2,1)S(1)} %get-tuple-element.38.mix, ...), custom_call_target="tpu_custom_call" | custom-call | flops 3500000000 | bytes 16000000 | tf_op jit(solution)/shard_map/residual_backward/pallas_call | solution.py:386
  194.3 1.9 collective-permute-done.7
  196.4 1.5 collective-permute-start.8
  197.9 6.9 %collective-permute-done.8 = bf16[2,4,64,256]{3,2,1,0:T(8,128)(2,1)S(1)} collective-permute-done((bf16[2,4,64,256]{3,2,1,0:T(8,128)(2,1)S(1)}, bf16[2,4,64,256]{3,2,1,0:T(8,128)(2,1)S(1)}, u32[]{:S(2)}, u32[]{:S(2)}) %collective-permute-start.8) | collective-permute-done | bytes 262176 | tf_op jit(solution)/shard_map/ppermute | solution.py:405
  205.7 1.5 collective-permute-start.9
  207.2 3.5 %all-to-all-start = ((bf16[8,16,2048]{2,1,0:T(8,128)(2,1)}), bf16[8,16,2048]{2,1,0:T(8,128)(2,1)S(1)}, u32[]{:S(2)}, u32[]{:S(2)}) async-start(bf16[8,16,2048]{2,1,0:T(8,128)(2,1)} %bitcast.9), calls=%async_computation | async-start | bytes 1048576 | tf_op jit(solution)/shard_map/all_to_all | solution.py:463
  212.7 2.4 collective-permute-start.12
  216.2 4.2 %all-to-all-done = bf16[8,16,2048]{2,1,0:T(8,128)(2,1)S(1)} async-done(((bf16[8,16,2048]{2,1,0:T(8,128)(2,1)}), bf16[8,16,2048]{2,1,0:T(8,128)(2,1)S(1)}, u32[]{:S(2)}, u32[]{:S(2)}) %all-to-all-start) | async-done | bytes 524320 | tf_op jit(solution)/shard_map/all_to_all | solution.py:463
  220.4 1.2 reshape.75
  221.6 1.6 convert_add_fusion.1
  224.9 1.7 convert_add_fusion
  228.6 10.4 %collective-permute-done.14 = bf16[2,4,160,256]{3,2,1,0:T(8,128)(2,1)S(1)} collective-permute-done((bf16[2,4,160,256]{3,2,1,0:T(8,128)(2,1)S(1)}, bf16[2,4,160,256]{3,2,1,0:T(8,128)(2,1)S(1)}, u32[]{:S(2)}, u32[]{:S(2)}) %collective-permute-start.14) | collective-permute-done | bytes 655392 | tf_op jit(solution)/shard_map/ppermute | solution.py:405
  239.9 4.3 %collective-permute-done.20 = bf16[2,4,160,256]{3,2,1,0:T(8,128)(2,1)S(1)} collective-permute-done((bf16[2,4,160,256]{3,2,1,0:T(8,128)(2,1)S(1)}, bf16[2,4,160,256]{3,2,1,0:T(8,128)(2,1)S(1)}, u32[]{:S(2)}, u32[]{:S(2)}) %collective-permute-start.20) | collective-permute-done | bytes 655392 | tf_op jit(solution)/shard_map/ppermute | solution.py:405
  245.2 4.2 %collective-permute-done.15 = bf16[4,160,256]{2,1,0:T(8,128)(2,1)S(1)} collective-permute-done((bf16[4,160,256]{2,1,0:T(8,128)(2,1)S(1)}, bf16[4,160,256]{2,1,0:T(8,128)(2,1)S(1)}, u32[]{:S(2)}, u32[]{:S(2)}) %collective-permute-start.15) | collective-permute-done | bytes 327712 | tf_op jit(solution)/shard_map/ppermute | solution.py:405
  249.6 2.4 collective-permute-start.18
  254.2 2.4 collective-permute-start.24
  256.8 7.0 %collective-permute-done.17 = bf16[160,256]{1,0:T(8,128)(2,1)S(1)} collective-permute-done((bf16[160,256]{1,0:T(8,128)(2,1)S(1)}, bf16[160,256]{1,0:T(8,128)(2,1)S(1)}, u32[]{:S(2)}, u32[]{:S(2)}) %collective-permute-start.17) | collective-permute-done | bytes 81952 | tf_op jit(solution)/shard_map/ppermute | solution.py:405
  263.9 1.9 collective-permute-done.23
  (116 shorter events, 28.1 us)
Async XLA Ops:
  7.2 71.9 %copy-start.3 = (f32[512]{0:T(512)S(1)}, f32[512]{0:T(512)}, u32[]{:S(2)}) copy-start(f32[512]{0:T(512)} %param.25) | copy-start | bytes 6148
  7.2 71.9 %copy-start.2 = (bf16[128,16,512]{2,1,0:T(8,128)(2,1)S(1)}, bf16[128,16,512]{2,1,0:T(8,128)(2,1)}, u32[]{:S(2)}) copy-start(bf16[128,16,512]{2,1,0:T(8,128)(2,1)} %param.14) | copy-start | bytes 6291460
  7.2 71.8 %all-gather.6.cloned.1.call-start = ((), (), s32[]{:S(2)}) async-start(), calls=%async_computation.1 | async-start | bytes 3932160 | tf_op jit(solution)/shard_map/all_gather | solution.py:456
  79.0 73.8 %collective-permute-start = (bf16[4,4,768,128]{3,2,1,0:T(8,128)(2,1)}, bf16[4,4,768,128]{3,2,1,0:T(8,128)(2,1)}, u32[]{:S(2)}, u32[]{:S(2)}) collective-permute-start(bf16[4,4,768,128]{3,2,1,0:T(8,128)(2,1)} %bitcast.155), channel_id=1, source_target_pairs={{0,4},{4,0},{8,12},{12,8},{16,20},{20,16},{24,28},{28,24},{1,5},{5... | collective-permute-start | bytes 9437192 | tf_op jit(solution)/shard_map/ppermute | solution.py:405
  84.8 14.2 %copy-start.13 = (s32[1,1,128]{2,1,0:T(1,128)S(1)}, s32[1,1,128]{2,1,0:T(1,128)}, u32[]{:S(2)}) copy-start(s32[1,1,128]{2,1,0:T(1,128)} %param.15) | copy-start | bytes 1540
  85.8 16.7 %collective-permute-start.5 = (bf16[16,128,128]{2,1,0:T(8,128)(2,1)S(1)}, bf16[16,128,128]{2,1,0:T(8,128)(2,1)S(1)}, u32[]{:S(2)}, u32[]{:S(2)}) collective-permute-start(bf16[16,128,128]{2,1,0:T(8,128)(2,1)S(1)} %get-tuple-element.55), channel_id=1, source_target_pairs={{0,3},{1,2},{2,1},{3,0},{4,7},{5,6},{6,5},{7,4},{8,11},{9,10},{10,... | collective-permute-start | bytes 1572872 | tf_op jit(solution)/shard_map/ppermute | solution.py:405
  89.1 57.3 %collective-permute-start.3 = (bf16[16,128,128]{2,1,0:T(8,128)(2,1)}, bf16[16,128,128]{2,1,0:T(8,128)(2,1)S(1)}, u32[]{:S(2)}, u32[]{:S(2)}) collective-permute-start(bf16[16,128,128]{2,1,0:T(8,128)(2,1)} %get-tuple-element.56), channel_id=1, source_target_pairs={{0,2},{1,3},{2,0},{3,1},{4,6},{5,7},{6,4},{7,5},{8,10},{9,11},{10,... | collective-permute-start | bytes 1572872 | tf_op jit(solution)/shard_map/ppermute | solution.py:405
  89.1 58.4 %collective-permute-start.1 = (bf16[16,128,128]{2,1,0:T(8,128)(2,1)S(1)}, bf16[16,128,128]{2,1,0:T(8,128)(2,1)S(1)}, u32[]{:S(2)}, u32[]{:S(2)}) collective-permute-start(bf16[16,128,128]{2,1,0:T(8,128)(2,1)S(1)} %get-tuple-element.57), channel_id=1, source_target_pairs={{0,1},{1,0},{2,3},{3,2},{4,5},{5,4},{6,7},{7,6},{8,9},{9,8},{10,11... | collective-permute-start | bytes 1572872 | tf_op jit(solution)/shard_map/ppermute | solution.py:405
  105.7 64.2 %collective-permute-start.6 = (bf16[256,1024]{1,0:T(8,128)(2,1)S(1)}, bf16[256,1024]{1,0:T(8,128)(2,1)}, u32[]{:S(2)}, u32[]{:S(2)}) collective-permute-start(bf16[256,1024]{1,0:T(8,128)(2,1)S(1)} %teacher_dot.7), channel_id=1, source_target_pairs={{0,3},{1,2},{2,1},{3,0},{4,7},{5,6},{6,5},{7,4},{8,11},{9,10},{10,... | collective-permute-start | bytes 1572872 | tf_op jit(solution)/shard_map/ppermute | solution.py:405
  147.4 32.4 %collective-permute-start.4 = (bf16[256,1024]{1,0:T(8,128)(2,1)S(1)}, bf16[256,1024]{1,0:T(8,128)(2,1)}, u32[]{:S(2)}, u32[]{:S(2)}) collective-permute-start(bf16[256,1024]{1,0:T(8,128)(2,1)S(1)} %teacher_dot.6), channel_id=1, source_target_pairs={{0,2},{1,3},{2,0},{3,1},{4,6},{5,7},{6,4},{7,5},{8,10},{9,11},{10,... | collective-permute-start | bytes 1572872 | tf_op jit(solution)/shard_map/ppermute | solution.py:405
  148.5 31.3 %collective-permute-start.2 = (bf16[256,1024]{1,0:T(8,128)(2,1)S(1)}, bf16[256,1024]{1,0:T(8,128)(2,1)}, u32[]{:S(2)}, u32[]{:S(2)}) collective-permute-start(bf16[256,1024]{1,0:T(8,128)(2,1)S(1)} %teacher_dot.5), channel_id=1, source_target_pairs={{0,1},{1,0},{2,3},{3,2},{4,5},{5,4},{6,7},{7,6},{8,9},{9,8},{10,11... | collective-permute-start | bytes 1572872 | tf_op jit(solution)/shard_map/ppermute | solution.py:405
  181.0 6.9 %copy-start.6 = (f32[16,128,256]{2,1,0:T(8,128)S(1)}, f32[16,128,256]{2,1,0:T(8,128)}, u32[]{:S(2)}) copy-start(f32[16,128,256]{2,1,0:T(8,128)} %get-tuple-element.41.slope_two) | copy-start | bytes 6291460
  194.2 2.0 collective-permute-start.7
  196.4 8.4 %collective-permute-start.8 = (bf16[2,4,64,256]{3,2,1,0:T(8,128)(2,1)S(1)}, bf16[2,4,64,256]{3,2,1,0:T(8,128)(2,1)S(1)}, u32[]{:S(2)}, u32[]{:S(2)}) collective-permute-start(bf16[2,4,64,256]{3,2,1,0:T(8,128)(2,1)S(1)} %fusion.7), channel_id=1, source_target_pairs={{0,8},{4,12},{8,0},{12,4},{16,24},{20,28},{24,16},{28,20},{1,9},{5... | collective-permute-start | bytes 786440 | tf_op jit(solution)/shard_map/ppermute | solution.py:405
  197.9 23.7 %collective-permute-start.13 = (bf16[16,160,256]{2,1,0:T(8,128)(2,1)}, bf16[16,160,256]{2,1,0:T(8,128)(2,1)}, u32[]{:S(2)}, u32[]{:S(2)}) collective-permute-start(bf16[16,160,256]{2,1,0:T(8,128)(2,1)} %get-tuple-element.46), channel_id=1, source_target_pairs={{0,4},{4,0},{8,12},{12,8},{16,20},{20,16},{24,28},{28,24},{1,5},{5... | collective-permute-start | bytes 3932168 | tf_op jit(solution)/shard_map/ppermute | solution.py:405
  205.6 16.0 %copy-start.8 = (f32[16,160,256]{2,1,0:T(8,128)S(1)}, f32[16,160,256]{2,1,0:T(8,128)}, u32[]{:S(2)}) copy-start(f32[16,160,256]{2,1,0:T(8,128)} %get-tuple-element.45) | copy-start | bytes 7864324
  205.7 5.4 %collective-permute-start.9 = (bf16[4,64,256]{2,1,0:T(8,128)(2,1)S(1)}, bf16[4,64,256]{2,1,0:T(8,128)(2,1)S(1)}, u32[]{:S(2)}, u32[]{:S(2)}) collective-permute-start(bf16[4,64,256]{2,1,0:T(8,128)(2,1)S(1)} %fusion.15), channel_id=1, source_target_pairs={{0,16},{4,20},{8,24},{12,28},{16,0},{20,4},{24,8},{28,12},{1,17},{... | collective-permute-start | bytes 393224 | tf_op jit(solution)/shard_map/ppermute | solution.py:405
  207.2 13.2 %all-to-all-start = ((bf16[8,16,2048]{2,1,0:T(8,128)(2,1)}), bf16[8,16,2048]{2,1,0:T(8,128)(2,1)S(1)}, u32[]{:S(2)}, u32[]{:S(2)}) async-start(bf16[8,16,2048]{2,1,0:T(8,128)(2,1)} %bitcast.9), calls=%async_computation | async-start | bytes 1048576 | tf_op jit(solution)/shard_map/all_to_all | solution.py:463
  210.7 13.4 %collective-permute-start.19 = (bf16[16,160,256]{2,1,0:T(8,128)(2,1)}, bf16[16,160,256]{2,1,0:T(8,128)(2,1)}, u32[]{:S(2)}, u32[]{:S(2)}) collective-permute-start(bf16[16,160,256]{2,1,0:T(8,128)(2,1)} %get-tuple-element.48), channel_id=1, source_target_pairs={{0,4},{4,0},{8,12},{12,8},{16,20},{20,16},{24,28},{28,24},{1,5},{5... | collective-permute-start | bytes 3932168 | tf_op jit(solution)/shard_map/ppermute | solution.py:405
  212.7 8.8 %collective-permute-start.10 = (bf16[64,256]{1,0:T(8,128)(2,1)}, bf16[64,256]{1,0:T(8,128)(2,1)S(1)}, u32[]{:S(2)}, u32[]{:S(2)}) collective-permute-start(bf16[64,256]{1,0:T(8,128)(2,1)} %get-tuple-element.69), channel_id=1, source_target_pairs={{0,1},{1,0},{2,3},{3,2},{4,5},{5,4},{6,7},{7,6},{8,9},{9,8},{10,11... | collective-permute-start | bytes 98312 | tf_op jit(solution)/shard_map/ppermute | solution.py:405
  212.7 8.8 %collective-permute-start.12 = (bf16[64,256]{1,0:T(8,128)(2,1)}, bf16[64,256]{1,0:T(8,128)(2,1)S(1)}, u32[]{:S(2)}, u32[]{:S(2)}) collective-permute-start(bf16[64,256]{1,0:T(8,128)(2,1)} %get-tuple-element.70), channel_id=1, source_target_pairs={{0,3},{1,2},{2,1},{3,0},{4,7},{5,6},{6,5},{7,4},{8,11},{9,10},{10,... | collective-permute-start | bytes 98312 | tf_op jit(solution)/shard_map/ppermute | solution.py:405
  215.1 6.4 %collective-permute-start.11 = (bf16[64,256]{1,0:T(8,128)(2,1)S(1)}, bf16[64,256]{1,0:T(8,128)(2,1)S(1)}, u32[]{:S(2)}, u32[]{:S(2)}) collective-permute-start(bf16[64,256]{1,0:T(8,128)(2,1)S(1)} %get-tuple-element.71), channel_id=1, source_target_pairs={{0,2},{1,3},{2,0},{3,1},{4,6},{5,7},{6,4},{7,5},{8,10},{9,11},{10,... | collective-permute-start | bytes 98312 | tf_op jit(solution)/shard_map/ppermute | solution.py:405
  223.5 15.6 %collective-permute-start.14 = (bf16[2,4,160,256]{3,2,1,0:T(8,128)(2,1)S(1)}, bf16[2,4,160,256]{3,2,1,0:T(8,128)(2,1)S(1)}, u32[]{:S(2)}, u32[]{:S(2)}) collective-permute-start(bf16[2,4,160,256]{3,2,1,0:T(8,128)(2,1)S(1)} %fusion.1), channel_id=1, source_target_pairs={{0,8},{4,12},{8,0},{12,4},{16,24},{20,28},{24,16},{28,20},{1,9},{5... | collective-permute-start | bytes 1966088 | tf_op jit(solution)/shard_map/ppermute | solution.py:405
  226.6 17.6 %collective-permute-start.20 = (bf16[2,4,160,256]{3,2,1,0:T(8,128)(2,1)S(1)}, bf16[2,4,160,256]{3,2,1,0:T(8,128)(2,1)S(1)}, u32[]{:S(2)}, u32[]{:S(2)}) collective-permute-start(bf16[2,4,160,256]{3,2,1,0:T(8,128)(2,1)S(1)} %bitcast.143), channel_id=1, source_target_pairs={{0,16},{4,20},{8,24},{12,28},{16,0},{20,4},{24,8},{28,12},{1,17},{... | collective-permute-start | bytes 1966088 | tf_op jit(solution)/shard_map/ppermute | solution.py:405
  239.3 10.1 %collective-permute-start.15 = (bf16[4,160,256]{2,1,0:T(8,128)(2,1)S(1)}, bf16[4,160,256]{2,1,0:T(8,128)(2,1)S(1)}, u32[]{:S(2)}, u32[]{:S(2)}) collective-permute-start(bf16[4,160,256]{2,1,0:T(8,128)(2,1)S(1)} %fusion.5), channel_id=1, source_target_pairs={{0,16},{4,20},{8,24},{12,28},{16,0},{20,4},{24,8},{28,12},{1,17},{... | collective-permute-start | bytes 983048 | tf_op jit(solution)/shard_map/ppermute | solution.py:405
  244.4 8.6 %collective-permute-start.21 = (bf16[4,160,256]{2,1,0:T(8,128)(2,1)S(1)}, bf16[4,160,256]{2,1,0:T(8,128)(2,1)S(1)}, u32[]{:S(2)}, u32[]{:S(2)}) collective-permute-start(bf16[4,160,256]{2,1,0:T(8,128)(2,1)S(1)} %fusion.6), channel_id=1, source_target_pairs={{0,8},{4,12},{8,0},{12,4},{16,24},{20,28},{24,16},{28,20},{1,9},{5... | collective-permute-start | bytes 983048 | tf_op jit(solution)/shard_map/ppermute | solution.py:405
  249.5 7.2 %collective-permute-start.16 = (bf16[160,256]{1,0:T(8,128)(2,1)S(1)}, bf16[160,256]{1,0:T(8,128)(2,1)S(1)}, u32[]{:S(2)}, u32[]{:S(2)}) collective-permute-start(bf16[160,256]{1,0:T(8,128)(2,1)S(1)} %get-tuple-element.59), channel_id=1, source_target_pairs={{0,1},{1,0},{2,3},{3,2},{4,5},{5,4},{6,7},{7,6},{8,9},{9,8},{10,11... | collective-permute-start | bytes 245768 | tf_op jit(solution)/shard_map/ppermute | solution.py:405
  249.6 7.2 %collective-permute-start.18 = (bf16[160,256]{1,0:T(8,128)(2,1)S(1)}, bf16[160,256]{1,0:T(8,128)(2,1)S(1)}, u32[]{:S(2)}, u32[]{:S(2)}) collective-permute-start(bf16[160,256]{1,0:T(8,128)(2,1)S(1)} %get-tuple-element.60), channel_id=1, source_target_pairs={{0,3},{1,2},{2,1},{3,0},{4,7},{5,6},{6,5},{7,4},{8,11},{9,10},{10,... | collective-permute-start | bytes 245768 | tf_op jit(solution)/shard_map/ppermute | solution.py:405
  252.0 11.8 %collective-permute-start.17 = (bf16[160,256]{1,0:T(8,128)(2,1)S(1)}, bf16[160,256]{1,0:T(8,128)(2,1)S(1)}, u32[]{:S(2)}, u32[]{:S(2)}) collective-permute-start(bf16[160,256]{1,0:T(8,128)(2,1)S(1)} %get-tuple-element.61), channel_id=1, source_target_pairs={{0,2},{1,3},{2,0},{3,1},{4,6},{5,7},{6,4},{7,5},{8,10},{9,11},{10,... | collective-permute-start | bytes 245768 | tf_op jit(solution)/shard_map/ppermute | solution.py:405
  253.2 10.7 %collective-permute-start.22 = (bf16[160,256]{1,0:T(8,128)(2,1)S(1)}, bf16[160,256]{1,0:T(8,128)(2,1)S(1)}, u32[]{:S(2)}, u32[]{:S(2)}) collective-permute-start(bf16[160,256]{1,0:T(8,128)(2,1)S(1)} %get-tuple-element.62), channel_id=1, source_target_pairs={{0,1},{1,0},{2,3},{3,2},{4,5},{5,4},{6,7},{7,6},{8,9},{9,8},{10,11... | collective-permute-start | bytes 245768 | tf_op jit(solution)/shard_map/ppermute | solution.py:405
  254.2 9.7 %collective-permute-start.24 = (bf16[160,256]{1,0:T(8,128)(2,1)S(1)}, bf16[160,256]{1,0:T(8,128)(2,1)S(1)}, u32[]{:S(2)}, u32[]{:S(2)}) collective-permute-start(bf16[160,256]{1,0:T(8,128)(2,1)S(1)} %get-tuple-element.63), channel_id=1, source_target_pairs={{0,3},{1,2},{2,1},{3,0},{4,7},{5,6},{6,5},{7,4},{8,11},{9,10},{10,... | collective-permute-start | bytes 245768 | tf_op jit(solution)/shard_map/ppermute | solution.py:405
  256.7 9.1 %collective-permute-start.23 = (bf16[160,256]{1,0:T(8,128)(2,1)S(1)}, bf16[160,256]{1,0:T(8,128)(2,1)S(1)}, u32[]{:S(2)}, u32[]{:S(2)}) collective-permute-start(bf16[160,256]{1,0:T(8,128)(2,1)S(1)} %get-tuple-element.64), channel_id=1, source_target_pairs={{0,2},{1,3},{2,0},{3,1},{4,6},{5,7},{6,4},{7,5},{8,10},{9,11},{10,... | collective-permute-start | bytes 245768 | tf_op jit(solution)/shard_map/ppermute | solution.py:405
  (10 other events, 20.2 us)
Sparse Core Ops, SparseCore 0:
  35.3 43.6 all-gather.5

commit v2 on v1

v2 whole, which is shorter than its diff:
```python
import jax
import jax.numpy as jnp
from jax import lax
from jax.experimental import pallas as pl
from jax.experimental.pallas import tpu as pltpu
from jax.sharding import PartitionSpec as P

CT = 512
DL = 1024
CS = 256
CSO = 512
KS = 16
STRIDE = 8
DILATED_TAPS = 7
UNIT_DILATION = 3
TILE_FRAMES = 16
TILE_DEV = 128
CHUNKS = 32
OUTF = 2
MARGIN = (KS - STRIDE) // 2
SHARE = TILE_DEV // 8
WINDOW_ROWS = 2 * OUTF * TILE_DEV
WEIGHT_ROW = WINDOW_ROWS + OUTF * DL // CS * SHARE
ROWS = TILE_DEV * TILE_FRAMES
LATENTS = TILE_DEV * OUTF
N_FSDP = 4
QUARTER = CT // N_FSDP
GROUP = 16
SLABS = 4
F32 = jnp.float32
BF16 = jnp.bfloat16
VMEM_LIMIT = 48 * 1024 * 1024
COST = pl.CostEstimate(flops=1000, bytes_accessed=1000, transcendentals=0)

PACK = {
    "dilated": DILATED_TAPS * CS // N_FSDP // SLABS,
    "mix": CS // N_FSDP // SLABS,
    "down": KS * CS // N_FSDP // SLABS,
    "proj": CSO // N_FSDP // SLABS,
}
PACK_COLS = {"dilated": 1, "mix": 1, "down": 2, "proj": 4}
PACK_ROWS = sum(PACK[name] * PACK_COLS[name] for name in PACK)

INV_PI = 0.3183098861837907
PI_PARTS = (3.125, 0.015625, 9.67502593994140625e-4, 1.509957990978376432e-7)
SIN_TERMS = (0.9999999765137553, -0.16666647593489264, 0.008332899222829617, -0.0001980086530702378, 2.5904300303557895e-06)
COS_TERMS = (0.999999953036273, -0.4999990494860951, 0.0416635772644784, -0.0013853657929132671, 2.3153011971441464e-05)


def _reduced(angle):
    turns = jnp.round(angle * INV_PI)
    for part in PI_PARTS:
        angle = angle - turns * part
    return angle


def _series(square, terms):
    total = square * terms[-1] + terms[-2]
    for term in terms[-3::-1]:
        total = total * square + term
    return total


def _snake(values, alpha, inverse):
    angle = _reduced(alpha * values)
    sine = angle * _series(angle * angle, SIN_TERMS)
    return values + sine * sine * inverse


def _snake_and_slope(values, alpha, inverse):
    angle = _reduced(alpha * values)
    square = angle * angle
    sine = angle * _series(square, SIN_TERMS)
    cosine = _series(square, COS_TERMS)
    return values + sine * sine * inverse, 1.0 + 2.0 * sine * cosine


def _dot(left, right):
    return jnp.dot(left, right, preferred_element_type=F32)


def _dot_nt(left, right):
    return lax.dot_general(left, right, (((1,), (1,)), ((), ())), preferred_element_type=F32)


def _dot_tn(left, right):
    return lax.dot_general(left, right, (((0,), (0,)), ((), ())), preferred_element_type=F32)


def _turn():
    count = GROUP * TILE_FRAMES
    target = lax.broadcasted_iota(jnp.int32, (count, count), 0)
    source = lax.broadcasted_iota(jnp.int32, (count, count), 1)
    wanted = (target % GROUP) * TILE_FRAMES + target // GROUP
    return jnp.where(source == wanted, 1.0, 0.0).astype(BF16)


def _teacher_act_kernel(place, tiles, alpha, keep, send):
    fsdp = place[2]
    turn = _turn()
    for out, first in ((keep, fsdp), (send, fsdp ^ 1)):
        for index in range(2):
            lanes = pl.ds(pl.multiple_of((first ^ (2 * index)) * QUARTER, QUARTER), QUARTER)
            scale = alpha[:, lanes]
            acted = _snake(_dot(turn, tiles[:, lanes]), scale, 1.0 / scale).astype(BF16)
            out[index] = acted.reshape(TILE_FRAMES, GROUP, QUARTER)


def _teacher_act(place, tiles, alpha):
    steps = TILE_DEV // GROUP
    shape = jax.ShapeDtypeStruct((2, TILE_FRAMES, TILE_DEV, QUARTER), BF16)
    return pl.pallas_call(
        _teacher_act_kernel,
        grid=(steps,),
        in_specs=[
            pl.BlockSpec(memory_space=pltpu.SMEM),
            pl.BlockSpec((GROUP * TILE_FRAMES, CT), lambda i: (i, 0)),
            pl.BlockSpec((1, CT), lambda i: (0, 0)),
        ],
        out_specs=[pl.BlockSpec((2, TILE_FRAMES, GROUP, QUARTER), lambda i: (0, 0, i, 0))] * 2,
        out_shape=[shape] * 2,
        name="teacher_act",
        compiler_params=pltpu.CompilerParams(vmem_limit_bytes=VMEM_LIMIT),
        cost_estimate=COST,
    )(place, tiles.reshape(ROWS, CT), alpha.reshape(1, CT))


def _pack_kernel(place, dilated, mix, down, proj, teacher, packed, columns, sems):
    core, slab = place[0], place[3]
    copies = []
    row = 0
    for name, source in (("dilated", dilated), ("mix", mix), ("down", down), ("proj", proj)):
        rows = PACK[name]
        for block in range(PACK_COLS[name]):
            begin = pl.multiple_of((core * PACK_COLS[name] + block) * 128, 128)
            copies.append(pltpu.make_async_copy(
                source.at[pl.ds(pl.multiple_of(slab * rows, 16), rows), pl.ds(begin, 128)],
                packed.at[pl.ds(row, rows), :],
                sems.at[len(copies)],
            ))
            row += rows
    begin = pl.multiple_of((core * SLABS + slab) * 128, 128)
    copies.append(pltpu.make_async_copy(teacher.at[:, pl.ds(begin, 128)], columns, sems.at[len(copies)]))
    for copy in copies:
        copy.start()
    for copy in copies:
        copy.wait()


def _pack(place, *kernels):
    anywhere = pl.BlockSpec(memory_space=pl.ANY)
    return pl.pallas_call(
        _pack_kernel,
        in_specs=[pl.BlockSpec(memory_space=pltpu.SMEM)] + [anywhere] * 5,
        out_specs=[pl.BlockSpec(memory_space=pltpu.VMEM)] * 2,
        out_shape=[
            jax.ShapeDtypeStruct((PACK_ROWS, 128), BF16),
            jax.ShapeDtypeStruct((KS * QUARTER, 128), BF16),
        ],
        scratch_shapes=[pltpu.SemaphoreType.DMA((9,))],
        name="pack_kernels",
        cost_estimate=COST,
    )(place, *kernels)


def _early(parts, slab):
    return parts[slab // 2].at[slab % 2]


def _late(parts, slab):
    return parts[2 + slab % 2].at[slab // 2]


def _windows(mine, theirs, quarter, offset):
    first = max(0, STRIDE * offset - MARGIN)
    wide = [
        jnp.concatenate([tiles[quarter, first + step] for step in range(STRIDE + MARGIN)], axis=1)
        for tiles in (mine, theirs)
    ]
    return jnp.concatenate(wide, axis=0), first - (STRIDE * offset - MARGIN)


def _teacher_near_kernel(mine, theirs, kernel, out):
    for offset in range(OUTF):
        wide, tap = _windows(mine, theirs, 0, offset)
        part = _dot(wide, kernel[tap * QUARTER : (tap + STRIDE + MARGIN) * QUARTER, :])
        for device in range(2):
            start = device * LATENTS + offset * TILE_DEV
            out[start : start + TILE_DEV, :] = part[device * TILE_DEV : (device + 1) * TILE_DEV, :]


def _teacher_near(mine, theirs, kernel):
    return pl.pallas_call(
        _teacher_near_kernel,
        out_shape=jax.ShapeDtypeStruct((2 * LATENTS, DL), F32),
        name="teacher_near",
        compiler_params=pltpu.CompilerParams(vmem_limit_bytes=VMEM_LIMIT),
        cost_estimate=COST,
    )(mine, theirs, kernel)


def _teacher_far_kernel(place, near, mine, theirs, *refs):
    own, other, (keep, send) = refs[:4], refs[4:8], refs[8:]
    core, plane = place[0], place[3]
    taps = KS // 2 * QUARTER
    skipped = MARGIN * QUARTER
    for offset in range(OUTF):
        wide, tap = _windows(mine, theirs, 1, offset)
        for side, source in enumerate((own, other)):
            for pair in range(0, SLABS, 2):
                columns = []
                for slab in (pair, pair + 1):
                    early, late = _early(source, slab)[...], _late(source, slab)[...]
                    if tap:
                        columns.append(jnp.concatenate([early[skipped:], late], axis=0))
                    else:
                        columns.append(jnp.concatenate([early, late[: taps - skipped]], axis=0))
                part = _dot(wide, jnp.concatenate(columns, axis=1))
                for index, slab in enumerate((pair, pair + 1)):
                    block = (core ^ side) * SLABS + (plane ^ slab)
                    lanes = pl.ds(pl.multiple_of(block * 128, 128), 128)
                    for device, out in enumerate((keep, send)):
                        piece = part[device * TILE_DEV : (device + 1) * TILE_DEV, index * 128 : (index + 1) * 128]
                        start = device * LATENTS + offset * TILE_DEV
                        piece += near[start : start + TILE_DEV, lanes]
                        out[offset * TILE_DEV : (offset + 1) * TILE_DEV, lanes] = piece.astype(out.dtype)


def _teacher_far(place, near, mine, theirs, own, other):
    whole = pl.BlockSpec(memory_space=pltpu.VMEM)
    return pl.pallas_call(
        _teacher_far_kernel,
        in_specs=[pl.BlockSpec(memory_space=pltpu.SMEM)] + [whole] * 11,
        out_specs=[whole] * 2,
        out_shape=[jax.ShapeDtypeStruct((LATENTS, DL), F32), jax.ShapeDtypeStruct((LATENTS, DL), BF16)],
        name="teacher_far",
        compiler_params=pltpu.CompilerParams(vmem_limit_bytes=VMEM_LIMIT),
        cost_estimate=COST,
    )(place, near, mine, theirs, *own, *other)


def _lanes(blocks, rows):
    return jnp.concatenate([blocks[index, rows, :] for index in range(blocks.shape[0])], axis=1)


def _forward_kernel(
    place, tiles, own_a, own_b, own_c, own_d, other_a, other_b, other_c, other_d,
    near_dilated, near_mix, near_down, near_proj, alphas, routes, weights,
    act_one, act_two, act_three, slope_two, slope_three, student, predicted, mix, down, proj, parcel,
    dilated, held,
):
    own, other = (own_a, own_b, own_c, own_d), (other_a, other_b, other_c, other_d)
    core, fsdp, plane = place[0], place[2], place[3]

    def rows_of(quarter, slab, share):
        return pl.ds(pl.multiple_of(quarter * (SLABS * share) + slab * share, 16), share)

    kinds = ((near_dilated, dilated), (near_mix, mix), (near_down, down), (near_proj, proj))
    for name, (source, target) in zip(PACK, kinds):
        rows = pl.ds(pl.multiple_of(fsdp * (SLABS * PACK[name]), 16), SLABS * PACK[name])
        for block in range(target.shape[0]):
            target[block, rows, :] = source[:, block * 128 : (block + 1) * 128]
    for flip, pieces in enumerate((own, other)):
        side = core ^ flip
        for slab in range(SLABS):
            for bit in range(1, N_FSDP):
                early, late = _early(pieces, slab).at[bit - 1], _late(pieces, slab).at[bit - 1]
                quarter, chip = fsdp ^ bit, plane ^ slab
                dilated[side, rows_of(quarter, chip, PACK["dilated"]), :] = early[0:112, :]
                mix[side, rows_of(quarter, chip, PACK["mix"]), :] = early[112:128, :]
                rows = rows_of(quarter, chip, PACK["down"])
                down[side * 2, rows, :] = early[128:384, :]
                down[side * 2 + 1, rows, :] = late[0:256, :]
                rows = rows_of(quarter, chip, PACK["proj"])
                for block in range(4):
                    proj[side * 4 + block, rows, :] = late[256 + block * 32 : 288 + block * 32, :]

    alpha_one, alpha_two, alpha_three = alphas[0:1, :], alphas[1:2, :], alphas[2:3, :]
    inverse_one, inverse_two, inverse_three = 1.0 / alpha_one, 1.0 / alpha_two, 1.0 / alpha_three
    turn = _turn()
    for step in range(TILE_DEV // GROUP):
        turned = _dot(turn, tiles[step * GROUP * TILE_FRAMES : (step + 1) * GROUP * TILE_FRAMES, :])
        shape = (TILE_FRAMES, GROUP, CS)
        held[:, step * GROUP : (step + 1) * GROUP, :] = turned.astype(BF16).reshape(shape)
        acted = _snake(turned, alpha_one, inverse_one).astype(BF16)
        act_one[:, step * GROUP : (step + 1) * GROUP, :] = acted.reshape(shape)

    half_taps = DILATED_TAPS // 2
    spans = []
    for frame in range(TILE_FRAMES):
        valid = [tap for tap in range(DILATED_TAPS) if 0 <= frame + UNIT_DILATION * (tap - half_taps) < TILE_FRAMES]
        span = (valid[0], valid[-1] + 1)
        if spans and spans[-1][2] == span:
            spans[-1][1] = frame + 1
        else:
            spans.append([frame, frame + 1, span])
    for start, stop, (low, high) in spans:
        wide = jnp.concatenate(
            [
                act_one[start + shift : stop + shift].reshape((stop - start) * TILE_DEV, CS)
                for shift in (UNIT_DILATION * (tap - half_taps) for tap in range(low, high))
            ],
            axis=1,
        )
        hidden = _dot(wide, _lanes(dilated, slice(low * CS, high * CS)))
        acted, slope = _snake_and_slope(hidden, alpha_two, inverse_two)
        shape = (stop - start, TILE_DEV, CS)
        acted = acted.astype(BF16)
        act_two[start:stop] = acted.reshape(shape)
        slope_two[start:stop] = slope.reshape(shape)
        residual = held[start:stop].reshape((stop - start) * TILE_DEV, CS).astype(F32) + _dot(acted, _lanes(mix, slice(None)))
        acted, slope = _snake_and_slope(residual, alpha_three, inverse_three)
        act_three[start:stop] = acted.astype(BF16).reshape(shape)
        slope_three[start:stop] = slope.reshape(shape)

    reach = STRIDE + MARGIN
    for offset in range(OUTF):
        first = max(0, STRIDE * offset - MARGIN)
        tap = first - (STRIDE * offset - MARGIN)
        wide = jnp.concatenate([act_three[first + step] for step in range(reach)], axis=1)
        part = _dot(wide, _lanes(down, slice(tap * CS, (tap + reach) * CS)))
        student[offset * TILE_DEV : (offset + 1) * TILE_DEV, :] = part.astype(BF16)
    pick = jnp.where(
        routes[...] == lax.broadcasted_iota(jnp.int32, (TILE_DEV, TILE_DEV), 1), 1.0, 0.0
    ).astype(BF16)
    for offset in range(OUTF):
        rows = slice(offset * TILE_DEV, (offset + 1) * TILE_DEV)
        part = _dot(student[rows, :], _lanes(proj, slice(None)))
        predicted[rows, :] = part
        picked = _dot(pick, part.astype(BF16)).astype(BF16)
        for block in range(DL // CS):
            row = WINDOW_ROWS + (offset * (DL // CS) + block) * SHARE
            for owner in range(8):
                parcel[owner, row : row + SHARE, :] = picked[
                    owner * SHARE : (owner + 1) * SHARE, block * CS : (block + 1) * CS
                ]
    first = weights[...].astype(BF16).astype(F32)
    second = (weights[...] - first).astype(BF16).astype(F32)
    third = weights[...] - first - second
    lane = lax.broadcasted_iota(jnp.int32, (TILE_DEV, CS), 1)
    split = jnp.where(lane == 0, first, jnp.where(lane == 1, second, jnp.where(lane == 2, third, 0.0))).astype(BF16)
    for owner in range(8):
        parcel[owner, WEIGHT_ROW:, :] = split[owner * SHARE : (owner + 1) * SHARE, :]
    for tap in range(KS):
        for offset in range(OUTF):
            frame = STRIDE * offset - MARGIN + tap
            row = (tap % 2 * OUTF + offset) * TILE_DEV
            if 0 <= frame < TILE_FRAMES:
                parcel[tap // 2, row : row + TILE_DEV, :] = act_three[frame]
            else:
                parcel[tap // 2, row : row + TILE_DEV, :] = jnp.zeros((TILE_DEV, CS), BF16)


def _forward(place, tiles, own, other, kernels, alphas, routes, weights):
    frames = (TILE_FRAMES, TILE_DEV, CS)
    whole = pl.BlockSpec(memory_space=pltpu.VMEM)
    return pl.pallas_call(
        _forward_kernel,
        in_specs=[
            pl.BlockSpec(memory_space=pltpu.SMEM),
            whole,
        ]
        + [whole] * 15,
        out_specs=[whole] * 11,
        out_shape=[
            jax.ShapeDtypeStruct(frames, BF16),
            jax.ShapeDtypeStruct(frames, BF16),
            jax.ShapeDtypeStruct(frames, BF16),
            jax.ShapeDtypeStruct(frames, F32),
            jax.ShapeDtypeStruct(frames, F32),
            jax.ShapeDtypeStruct((LATENTS, CSO), BF16),
            jax.ShapeDtypeStruct((LATENTS, DL), F32),
            jax.ShapeDtypeStruct((CS // 128, CS, 128), BF16),
            jax.ShapeDtypeStruct((CSO // 128, KS * CS, 128), BF16),
            jax.ShapeDtypeStruct((DL // 128, CSO, 128), BF16),
            jax.ShapeDtypeStruct((8, WEIGHT_ROW + SHARE, CS), BF16),
        ],
        scratch_shapes=[
            pltpu.VMEM((CS // 128, DILATED_TAPS * CS, 128), BF16),
            pltpu.VMEM(frames, BF16),
        ],
        name="student_forward",
        compiler_params=pltpu.CompilerParams(vmem_limit_bytes=VMEM_LIMIT),
        cost_estimate=COST,
    )(place, tiles.reshape(ROWS, CS), *own, *other, *kernels, alphas, routes, weights)


def _stacked(values, columns):
    return jnp.concatenate(
        [values[:, start : start + columns] for start in range(0, values.shape[1], columns)], axis=0
    )


def _error_kernel(target_own, target_other, predicted, weights, proj, back_student, error):
    weight = weights[...] * (1.0 / LATENTS)
    for offset in range(OUTF):
        rows = slice(offset * TILE_DEV, (offset + 1) * TILE_DEV)
        target = target_own[rows, :] + target_other[rows, :].astype(F32)
        target = target.astype(BF16).astype(F32)
        error[rows, :] = (weight * (predicted[rows, :] - target)).astype(BF16)
    back = _dot_nt(error[...], _lanes(proj, slice(None))).astype(BF16)
    back_student[...] = back.reshape(OUTF, TILE_DEV, CSO)


def _error(targets, predicted, weights, proj):
    whole = pl.BlockSpec(memory_space=pltpu.VMEM)
    return pl.pallas_call(
        _error_kernel,
        in_specs=[whole] * 5,
        out_specs=[whole] * 2,
        out_shape=[
            jax.ShapeDtypeStruct((OUTF, TILE_DEV, CSO), BF16),
            jax.ShapeDtypeStruct((LATENTS, DL), BF16),
        ],
        name="error_backward",
        compiler_params=pltpu.CompilerParams(vmem_limit_bytes=VMEM_LIMIT),
        cost_estimate=COST,
    )(*targets, predicted, weights, proj)


def _down_kernel(place, parcels, rest_keep, rest_received, *refs):
    own, other, (keep, *sends), grads = refs[:4], refs[4:8], refs[8:12], refs[12]
    fsdp, chip = place[2], place[4]
    back = []
    for source in (own, other):
        for slab in range(SLABS):
            back += [_early(source, slab)[...], _late(source, slab)[...]]
    back = jnp.concatenate(back, axis=0)
    for tap in range(2):
        rows = []
        for side in range(2):
            for slab in range(SLABS):
                rows.append(parcels[chip ^ (2 * slab + side), tap * LATENTS : (tap + 1) * LATENTS, :])
        grads[tap * CS : (tap + 1) * CS, :] = _dot_tn(jnp.concatenate(rows, axis=0), back)
    for spot, out in enumerate((keep, *sends)):
        part = grads[pl.ds(pl.multiple_of((spot ^ fsdp) * 128, 128), 128), :]
        out[0:256, :] = _stacked(part, 256).astype(out.dtype)
        out[256:384, :] = (rest_keep[spot] + rest_received[spot].astype(F32)).astype(out.dtype)


def _down(place, parcels, rest, own, other):
    whole = pl.BlockSpec(memory_space=pltpu.VMEM)
    return pl.pallas_call(
        _down_kernel,
        in_specs=[pl.BlockSpec(memory_space=pltpu.SMEM)] + [whole] * 11,
        out_specs=[whole] * 4,
        out_shape=[jax.ShapeDtypeStruct((384, 256), F32)] + [jax.ShapeDtypeStruct((384, 256), BF16)] * 3,
        scratch_shapes=[pltpu.VMEM((CSO, CSO), F32)],
        name="down_gradient",
        compiler_params=pltpu.CompilerParams(vmem_limit_bytes=VMEM_LIMIT),
        cost_estimate=COST,
    )(place, parcels, *rest, *own, *other)


def _residual_kernel(
    place, back_student, error, student, down, mix, act_one, act_two, slope_two, slope_three,
    send, keep, back_three, back_residual, back_hidden, grad_dilated, grad_mix, grad_proj,
):
    me = place[1]
    back = back_student[...].reshape(LATENTS, CSO)
    for tap in range(KS):
        part = _dot_nt(back, _lanes(down, slice(tap * CS, (tap + 1) * CS)))
        for offset in range(OUTF):
            frame = STRIDE * offset - MARGIN + tap
            if 0 <= frame < TILE_FRAMES:
                piece = part[offset * TILE_DEV : (offset + 1) * TILE_DEV, :]
                if offset == 0 and frame >= MARGIN:
                    back_three[frame] += piece
                else:
                    back_three[frame] = piece
    for frame in range(0, TILE_FRAMES, 2):
        rows = slice(frame * TILE_DEV, (frame + 2) * TILE_DEV)
        shape = (2 * TILE_DEV, CS)
        share = back_three[frame : frame + 2].reshape(shape) * slope_three[frame : frame + 2].reshape(shape)
        share = share.astype(BF16)
        back_residual[rows, :] = share
        share = _dot_nt(share, _lanes(mix, slice(None))) * slope_two[frame : frame + 2].reshape(shape)
        back_hidden[rows, :] = share.astype(BF16)
    grad_mix[...] = _dot_tn(act_two[...].reshape(ROWS, CS), back_residual[...])
    half_taps = DILATED_TAPS // 2
    for tap in range(DILATED_TAPS):
        shift = UNIT_DILATION * (tap - half_taps)
        first, last = max(0, -shift), min(TILE_FRAMES, TILE_FRAMES - shift)
        rows = (last - first) * TILE_DEV
        grad_dilated[tap * CS : (tap + 1) * CS, :] = _dot_tn(
            act_one[first + shift : last + shift].reshape(rows, CS), back_hidden[first * TILE_DEV : last * TILE_DEV, :]
        )
    grad_proj[...] = _dot_tn(student[...], error[...])
    for place_index in range(CHUNKS):
        chunk = me ^ place_index
        part = jnp.concatenate(
            [
                _stacked(grad_proj[pl.ds(pl.multiple_of(chunk * 16, 16), 16), :], 256),
                grad_dilated[pl.ds(pl.multiple_of(chunk * 56, 8), 56), :],
                grad_mix[pl.ds(pl.multiple_of(chunk * 8, 8), 8), :],
            ],
            axis=0,
        )
        out = send if (place_index // 4) % 2 else keep
        out[(place_index // 8) * 4 + place_index % 4] = part.astype(out.dtype)


def _residual(place, back_student, error, student, down, mix, act_one, act_two, slope_two, slope_three):
    whole = pl.BlockSpec(memory_space=pltpu.VMEM)
    half = (CHUNKS // 2, 128, 256)
    return pl.pallas_call(
        _residual_kernel,
        in_specs=[pl.BlockSpec(memory_space=pltpu.SMEM)] + [whole] * 9,
        out_specs=[whole] * 2,
        out_shape=[jax.ShapeDtypeStruct(half, BF16), jax.ShapeDtypeStruct(half, F32)],
        scratch_shapes=[
            pltpu.VMEM((TILE_FRAMES, TILE_DEV, CS), F32),
            pltpu.VMEM((ROWS, CS), BF16),
            pltpu.VMEM((ROWS, CS), BF16),
            pltpu.VMEM((DILATED_TAPS * CS, CS), F32),
            pltpu.VMEM((CS, CS), F32),
            pltpu.VMEM((CSO, DL), F32),
        ],
        name="residual_backward",
        compiler_params=pltpu.CompilerParams(vmem_limit_bytes=VMEM_LIMIT),
        cost_estimate=COST,
    )(place, back_student, error, student, down, mix, act_one, act_two, slope_two, slope_three)


def _swap(values, axis, bit):
    return lax.ppermute(values, axis, [(i, i ^ bit) for i in range(lax.axis_size(axis))])


def on_device(
    student_tiles,
    teacher_tiles,
    send_list,
    clip_weight,
    kernel_dilated,
    kernel_mix,
    kernel_down,
    kernel_proj,
    kernel_teacher,
    alpha_one,
    alpha_two,
    alpha_three,
    alpha_teacher,
):
    n_dp = lax.axis_size("dp")
    d, f = lax.axis_index("dp"), lax.axis_index("fsdp")
    core, slab = d % 2, (d // 2) % SLABS
    halving = n_dp == 8
    me = d * N_FSDP + f if halving else jnp.int32(0)
    place = jnp.stack([core, me, f, slab, d % 8]).astype(jnp.int32)

    def plane_spread(early, late):
        return jnp.stack([early, _swap(early, "dp", 2)]), jnp.stack([late, _swap(late, "dp", 4)])

    def plane_gather(early, late):
        own = (early, _swap(early, "dp", 4), late, _swap(late, "dp", 2))
        return own, tuple(_swap(part, "dp", 1) for part in own)

    kernels = (kernel_dilated, kernel_mix, kernel_down, kernel_proj)
    flat_teacher = kernel_teacher.reshape(KS * QUARTER, DL)
    packed, columns = _pack(place, *kernels, flat_teacher)
    fetched = [_swap(packed, "fsdp", bit) for bit in range(1, N_FSDP)]
    columns = _swap(columns, "fsdp", 2)

    mine, sent = _teacher_act(place, teacher_tiles, alpha_teacher)
    fetched, sent = lax.optimization_barrier((fetched, sent))
    theirs = _swap(sent, "fsdp", 1)

    half = PACK_ROWS // 2
    spread = plane_spread(
        jnp.stack([part[:half] for part in fetched]), jnp.stack([part[half:] for part in fetched])
    )
    own, other = plane_gather(*spread)
    spread = plane_spread(columns[: KS * QUARTER // 2], columns[KS * QUARTER // 2 :])
    near = _teacher_near(mine, theirs, flat_teacher)
    teacher_own, teacher_other = plane_gather(*spread)
    own, other, _, near = lax.optimization_barrier((own, other, spread, near))

    alphas = jnp.stack([alpha_one, alpha_two, alpha_three])
    routes = send_list.reshape(-1)
    (
        act_one, act_two, act_three, slope_two, slope_three, student, predicted, mix, down, proj, parcel,
    ) = _forward(place, student_tiles, own, other, kernels, alphas, routes[:, None], clip_weight[:, None])
    near, predicted = lax.optimization_barrier((near, predicted))
    target, partial = _teacher_far(place, near, mine, theirs, teacher_own, teacher_other)
    targets = (target, _swap(partial, "fsdp", 1))

    latent_rows = parcel[:, WINDOW_ROWS:WEIGHT_ROW].reshape(8, OUTF * DL // CS, SHARE, CS)
    if halving:
        parcel, _ = lax.optimization_barrier((parcel, teacher_own))
        parcels = lax.all_to_all(parcel, "dp", split_axis=0, concat_axis=0, tiled=True)
        latent = parcels[:, WINDOW_ROWS:WEIGHT_ROW].reshape(8, OUTF * DL // CS, SHARE, CS).transpose(0, 2, 1, 3)
        slot_weights = jnp.sum(parcels[:, WEIGHT_ROW:, :3].astype(F32), axis=2).reshape(-1)
    else:
        latent = latent_rows.transpose(0, 2, 1, 3).reshape(TILE_DEV, OUTF * DL)
        latent = lax.all_to_all(latent, "dp", split_axis=0, concat_axis=0, tiled=True)
        slot_weights = lax.all_to_all(
            clip_weight.reshape(n_dp, TILE_DEV // n_dp), "dp", split_axis=0, concat_axis=0, tiled=True
        ).reshape(-1)
    latent = latent.reshape(TILE_DEV, OUTF, DL)
    hits = routes[:, None] == jnp.arange(TILE_DEV, dtype=jnp.int32)[None, :]
    weights = jnp.sum(jnp.where(hits, slot_weights[:, None], 0.0), axis=0)[:, None]

    back_student, error = _error(targets, predicted, weights, proj)
    send, keep = _residual(place, back_student, error, student, down, mix, act_one, act_two, slope_two, slope_three)

    if halving:
        keep = keep.reshape(2, 2, N_FSDP, 128, 256)
        received = _swap(send, "dp", 1).reshape(keep.shape)
        for bit in (4, 2):
            keep, out = keep[0] + received[0].astype(F32), (keep[1] + received[1].astype(F32)).astype(BF16)
            received = _swap(out, "dp", bit)
        part, *sends = _down(
            place, parcels, (keep, received), *plane_gather(*plane_spread(back_student[0], back_student[1]))
        )
        for bit, out in zip(range(1, N_FSDP), sends):
            part = part + _swap(out, "fsdp", bit).astype(F32)
        grad_down = jnp.concatenate([part[:128], part[128:256]], axis=1).reshape(-1)
        grad_proj = jnp.concatenate([part[256 + 16 * i : 272 + 16 * i] for i in range(4)], axis=1).reshape(-1)
        grad_dilated, grad_mix = part[320:376].reshape(-1), part[376:].reshape(-1)
    else:
        def joined(send, keep):
            rows = keep.shape[1]
            both = jnp.stack([keep.reshape(4, 4, rows, 256), send.astype(F32).reshape(4, 4, rows, 256)], axis=1)
            return both.reshape(CHUNKS, rows, 256)

        def scattered(values):
            return lax.psum_scatter(values.reshape(-1), ("dp", "fsdp"), scatter_dimension=0, tiled=True)

        part = joined(send, keep)
        windows = parcel[:, :WINDOW_ROWS].reshape(KS, OUTF, TILE_DEV, CS)
        grad_down = scattered(jnp.einsum("kotc,otd->kcd", windows, back_student, preferred_element_type=F32))
        grad_proj = scattered(jnp.concatenate([part[:, 16 * i : 16 * (i + 1)] for i in range(4)], axis=2))
        grad_dilated, grad_mix = scattered(part[:, 64:120]), scattered(part[:, 120:])
    return latent, grad_dilated, grad_mix, grad_down, grad_proj


def solution(mesh):
    placed = (
        P(("dp", "fsdp"), None, None),
        P(("dp", "fsdp"), None, None),
        P("dp", "fsdp", None),
        P(("dp", "fsdp")),
        P("fsdp", None),
        P("fsdp", None),
        P("fsdp", None),
        P("fsdp", None),
        P(None, "fsdp", None),
        P(),
        P(),
        P(),
        P(),
    )
    return jax.shard_map(
        on_device,
        mesh=mesh,
        in_specs=placed,
        out_specs=(
            P(("dp", "fsdp"), None, None),
            P(("dp", "fsdp")),
            P(("dp", "fsdp")),
            P(("dp", "fsdp")),
            P(("dp", "fsdp")),
        ),
        check_vma=False,
    )
```

time: 275 us -> 203 us (0.74)
  waiting for transfers between devices: 135 us -> 99.4 us
  blocking collectives: 30.4 us -> 0 us
  between operations: 14.6 us -> 1.15 us
  Pallas kernels: 38.8 us -> 48.8 us
  local copies, waits for them, and re-layouts: 18.6 us -> 13.3 us
  starting transfers between devices: 31.2 us -> 34.8 us
    all_gather x1 -> x0, waiting for transfers between devices: 43.8 us -> none  [on_device(): lax.all_gather(packed, 'dp', axis=0, tiled=False, axis_index_groups=planes)]
    all_gather x2 -> x0, blocking collectives: 30.4 us -> none  [the longest x1 21.7 us: on_device(): packed = lax.all_gather(packed, 'fsdp', axis=0, tiled=False)]
    all_to_all x1, waiting for transfers between devices: 4.16 us -> 21.5 us  [on_device(): lax.all_to_all(parcel, 'dp', split_axis=0, concat_axis=0, tiled=True)]
    ppermute x25 -> x36, waiting for transfers between devices: 87.2 us -> 77.9 us  [_swap(): lax.ppermute(values, axis, [(i, i ^ bit) for i in range(lax.axis_size(axi...]
    pallas_call x5, Pallas kernels: 11 us -> 17.5 us  [the longest x1 5.69 us: _teacher_far(): pl.pallas_call(_teacher_far_kernel, in_specs=[pl.BlockSpec(memory_space=p...]
    unnamed x43 -> x60, local copies, waits for them, and re-layouts: 14.1 us -> 9.74 us
    add x9 -> x1, other arithmetic: 3.81 us -> 0.08 us  [on_device(): part = part + _swap(out, 'fsdp', bit).astype(F32)]
    ppermute x25 -> x36, starting transfers between devices: 27.6 us -> 30.3 us  [_swap(): lax.ppermute(values, axis, [(i, i ^ bit) for i in range(lax.axis_size(axi...]
  transfers between devices with their start and end apart: 27 -> 37, of which waited for: 13 -> 20; matrix products, arithmetic and copies ran while one was open for 4% -> 4% of each run, Pallas kernels for 9% -> 16%
where the time goes in v2:
time: 203 us; the launch traced here: 202 us
  waiting for transfers between devices  99.4 us (49%)
  Pallas kernels  48.8 us (24%)
  starting transfers between devices  34.8 us (17%)
  local copies, waits for them, and re-layouts  13.3 us (7%)
  other arithmetic  4.91 us (2%)
    ppermute x36, waiting for transfers between devices, _swap(): lax.ppermute(values, axis, [(i, i ^ bit) for i in range(lax.axis_size(axi...  77.9 us
    ppermute x36, starting transfers between devices, _swap(): lax.ppermute(values, axis, [(i, i ^ bit) for i in range(lax.axis_size(axi...  30.3 us
    all_to_all x1, waiting for transfers between devices, on_device(): lax.all_to_all(parcel, 'dp', split_axis=0, concat_axis=0, tiled=True)  21.5 us
    pallas_call x1, Pallas kernels, _forward(): pl.pallas_call(_forward_kernel, in_specs=[pl.BlockSpec(memory_space=pltpu...  17.1 us
    unnamed x60, local copies, waits for them, and re-layouts  9.74 us
    pallas_call x1, Pallas kernels, _residual(): pl.pallas_call(_residual_kernel, in_specs=[pl.BlockSpec(memory_space=pltp...  8.59 us
    pallas_call x1, Pallas kernels, _teacher_far(): pl.pallas_call(_teacher_far_kernel, in_specs=[pl.BlockSpec(memory_space=p...  5.69 us
    pallas_call x1, Pallas kernels, _teacher_act(): pl.pallas_call(_teacher_act_kernel, grid=(steps,), in_specs=[pl.BlockSpec...  5.62 us
  transfers between devices with their start and end apart: 37, of which 20 were waited for; matrix products, arithmetic and copies ran while one was open for 4% of the time, Pallas kernels for 16%

profile of v2, /device:TPU:0, one launch (start us, length us, event | category | flops | bytes accessed | tf_op | source)
XLA Modules:
  0.0 202.4 jit_solution(18092977807436830502)
XLA Ops:
  1.4 3.0 %pack_kernels.1 = (bf16[768,128]{1,0:T(8,128)(2,1)}, bf16[2048,128]{1,0:T(8,128)(2,1)}) custom-call(s32[5]{0:T(128)} %stack.107.place, bf16[448,256]{1,0:T(8,128)(2,1)} %near_dilated.1, bf16[64,256]{1,0:T(8,128)(2,1)} %near_mix.1, bf16[1024,512]{1,0:T(8,128)(2,1)} %near_down.1, bf16[128,1024]{1,0:T(8,128)(2,1)} %near_proj.1, bf16[2048,1024]{1,0:T(8,128)(2,1)} %bitcast.84), custom_call_target="tpu_custom_call" | custom-call | flops 1000 | bytes 1000 | tf_op jit(solution)/shard_map/pack_kernels/pallas_call | solution.py:152
  4.3 3.1 %collective-permute-start = (bf16[768,128]{1,0:T(8,128)(2,1)}, bf16[768,128]{1,0:T(8,128)(2,1)S(1)}, u32[]{:S(2)}, u32[]{:S(2)}) collective-permute-start(bf16[768,128]{1,0:T(8,128)(2,1)} %get-tuple-element.45), channel_id=1, source_target_pairs={{0,1},{1,0},{2,3},{3,2},{4,5},{5,4},{6,7},{7,6},{8,9},{9,8},{10,11... | collective-permute-start | bytes 589832 | tf_op jit(solution)/shard_map/ppermute | solution.py:526
  7.4 2.6 %collective-permute-start.1 = (bf16[768,128]{1,0:T(8,128)(2,1)}, bf16[768,128]{1,0:T(8,128)(2,1)S(1)}, u32[]{:S(2)}, u32[]{:S(2)}) collective-permute-start(bf16[768,128]{1,0:T(8,128)(2,1)} %get-tuple-element.45), channel_id=1, source_target_pairs={{0,2},{1,3},{2,0},{3,1},{4,6},{5,7},{6,4},{7,5},{8,10},{9,11},{10,... | collective-permute-start | bytes 589832 | tf_op jit(solution)/shard_map/ppermute | solution.py:526
  10.0 5.6 %teacher_act.1 = (bf16[2,16,128,128]{3,2,1,0:T(8,128)(2,1)S(1)}, bf16[2,16,128,128]{3,2,1,0:T(8,128)(2,1)S(1)}) custom-call(s32[5]{0:T(128)S(1)} %copy-done.19, bf16[2048,512]{1,0:T(8,128)(2,1)S(1)} %bitcast.82, f32[1,512]{1,0:T(1,128)S(1)} %bitcast.83), custom_call_target="tpu_custom_call" | custom-call | flops 1000 | bytes 1000 | tf_op jit(solution)/shard_map/teacher_act/pallas_call | solution.py:112
  16.0 8.8 %collective-permute-done.1 = bf16[768,128]{1,0:T(8,128)(2,1)S(1)} collective-permute-done((bf16[768,128]{1,0:T(8,128)(2,1)}, bf16[768,128]{1,0:T(8,128)(2,1)S(1)}, u32[]{:S(2)}, u32[]{:S(2)}) %collective-permute-start.1) | collective-permute-done | bytes 196640 | tf_op jit(solution)/shard_map/ppermute | solution.py:526
  24.9 1.6 collective-permute-start.5
  26.5 4.4 %collective-permute-start.11 = (bf16[2048,128]{1,0:T(8,128)(2,1)S(1)}, bf16[2048,128]{1,0:T(8,128)(2,1)S(1)}, u32[]{:S(2)}, u32[]{:S(2)}) collective-permute-start(bf16[2048,128]{1,0:T(8,128)(2,1)S(1)} %copy-done.26), channel_id=1, source_target_pairs={{0,2},{1,3},{2,0},{3,1},{4,6},{5,7},{6,4},{7,5},{8,10},{9,11},{10,... | collective-permute-start | bytes 1572872 | tf_op jit(solution)/shard_map/ppermute | solution.py:526
  30.9 1.6 collective-permute-start.3
  33.3 7.6 %collective-permute-done.3 = bf16[3,384,128]{2,1,0:T(8,128)(2,1)S(1)} collective-permute-done((bf16[3,384,128]{2,1,0:T(8,128)(2,1)S(1)}, bf16[3,384,128]{2,1,0:T(8,128)(2,1)S(1)}, u32[]{:S(2)}, u32[]{:S(2)}) %collective-permute-start.3) | collective-permute-done | bytes 294944 | tf_op jit(solution)/shard_map/ppermute | solution.py:526
  41.6 11.1 %collective-permute-done.11 = bf16[2048,128]{1,0:T(8,128)(2,1)S(1)} collective-permute-done((bf16[2048,128]{1,0:T(8,128)(2,1)S(1)}, bf16[2048,128]{1,0:T(8,128)(2,1)S(1)}, u32[]{:S(2)}, u32[]{:S(2)}) %collective-permute-start.11) | collective-permute-done | bytes 524320 | tf_op jit(solution)/shard_map/ppermute | solution.py:526
  52.8 1.6 collective-permute-start.12
  54.4 5.5 %collective-permute-done.12 = bf16[1024,128]{1,0:T(8,128)(2,1)S(1)} collective-permute-done((bf16[1024,128]{1,0:T(8,128)(2,1)S(1)}, bf16[1024,128]{1,0:T(8,128)(2,1)S(1)}, u32[]{:S(2)}, u32[]{:S(2)}) %collective-permute-start.12) | collective-permute-done | bytes 262176 | tf_op jit(solution)/shard_map/ppermute | solution.py:526
  61.2 5.0 %collective-permute-done.13 = bf16[1024,128]{1,0:T(8,128)(2,1)S(1)} collective-permute-done((bf16[1024,128]{1,0:T(8,128)(2,1)S(1)}, bf16[1024,128]{1,0:T(8,128)(2,1)S(1)}, u32[]{:S(2)}, u32[]{:S(2)}) %collective-permute-start.13) | collective-permute-done | bytes 262176 | tf_op jit(solution)/shard_map/ppermute | solution.py:526
  69.0 1.5 collective-permute-start.16
  70.9 4.1 %teacher_near.1.near = f32[512,1024]{1,0:T(8,128)S(1)} custom-call(bf16[2,16,128,128]{3,2,1,0:T(8,128)(2,1)S(1)} %get-tuple-element.51.mine, bf16[2,16,128,128]{3,2,1,0:T(8,128)(2,1)S(1)} %collective-permute-done.14.theirs, bf16[2048,1024]{1,0:T(8,128)(2,1)} %bitcast.85), custom_call_target="tpu_custom_call" | custom-call | flops 1000 | bytes 1000 | tf_op jit(solution)/shard_map/teacher_near/pallas_call | solution.py:193
  76.4 17.1 %student_forward.1 = (bf16[16,128,256]{2,1,0:T(8,128)(2,1)}, bf16[16,128,256]{2,1,0:T(8,128)(2,1)}, bf16[16,128,256]{2,1,0:T(8,128)(2,1)}, f32[16,128,256]{2,1,0...) custom-call(s32[5]{0:T(128)S(1)} %copy-done.19, ...), custom_call_target="tpu_custom_call" | custom-call | flops 1000 | bytes 1000 | tf_op jit(solution)/shard_map/student_forward/pallas_call | solution.py:357
  94.8 4.4 %all-to-all-start = ((bf16[8,656,256]{2,1,0:T(8,128)(2,1)}), bf16[8,656,256]{2,1,0:T(8,128)(2,1)}, u32[]{:S(2)}, u32[]{:S(2)}) async-start(bf16[8,656,256]{2,1,0:T(8,128)(2,1)} %get-tuple-element.62), calls=%async_computation | async-start | bytes 5373952 | tf_op jit(solution)/shard_map/all_to_all | solution.py:590
  104.0 5.7 %teacher_far.1 = (f32[256,1024]{1,0:T(8,128)S(1)}, bf16[256,1024]{1,0:T(8,128)(2,1)}) custom-call(s32[5]{0:T(128)S(1)} %copy-done.19, f32[512,1024]{1,0:T(8,128)} %copy-done, bf16[2,16,128,128]{3,2,1,0:T(8,128)(2,1)} %copy-done.1, bf16[2,16,128,128]{3,2,1,0:T(8,128)(2,1)} %copy-done.2, bf16[2,1024,128]{2,1,0:T(8,128)(2,1)} %pad_maximum_fusion.2.refs_0_, ...), custom_call_target="tpu_custom_call" | custom-call | flops 1000 | bytes 1000 | tf_op jit(solution)/shard_map/teacher_far/pallas_call | solution.py:231
  110.7 21.5 %all-to-all-done.parcels = bf16[8,656,256]{2,1,0:T(8,128)(2,1)} async-done(((bf16[8,656,256]{2,1,0:T(8,128)(2,1)}), bf16[8,656,256]{2,1,0:T(8,128)(2,1)}, u32[]{:S(2)}, u32[]{:S(2)}) %all-to-all-start) | async-done | bytes 2687008 | tf_op jit(solution)/shard_map/all_to_all | solution.py:590
  135.9 1.6 error_backward.1
  137.5 8.6 %residual_backward.1 = (bf16[16,128,256]{2,1,0:T(8,128)(2,1)S(1)}, f32[16,128,256]{2,1,0:T(8,128)}) custom-call(s32[5]{0:T(128)S(1)} %copy-done.19, bf16[2,128,512]{2,1,0:T(8,128)(2,1)S(1)} %get-tuple-element.70.back_student, bf16[256,1024]{1,0:T(8,128)(2,1)S(1)} %get-tuple-element.71.error, bf16[256,512]{1,0:T(8,128)(2,1)S(1)} %copy-done.15, ...), custom_call_target="tpu_custom_call" | custom-call | flops 1000 | bytes 1000 | tf_op jit(solution)/shard_map/residual_backward/pallas_call | solution.py:506
  146.8 2.0 collective-permute-done.22
  148.8 1.8 add_convert_fusion
  153.3 4.3 %collective-permute-done.25 = bf16[128,512]{1,0:T(8,128)(2,1)S(1)} collective-permute-done((bf16[128,512]{1,0:T(8,128)(2,1)S(1)}, bf16[128,512]{1,0:T(8,128)(2,1)S(1)}, u32[]{:S(2)}, u32[]{:S(2)}) %collective-permute-start.25) | collective-permute-done | bytes 131104 | tf_op jit(solution)/shard_map/ppermute | solution.py:526
  157.6 1.5 collective-permute-start.26
  159.7 2.4 %collective-permute-done.28.refs_3_ = bf16[2,128,512]{2,1,0:T(8,128)(2,1)S(1)} collective-permute-done((bf16[2,128,512]{2,1,0:T(8,128)(2,1)S(1)}, bf16[2,128,512]{2,1,0:T(8,128)(2,1)S(1)}, u32[]{:S(2)}, u32[]{:S(2)}) %collective-permute-start.28) | collective-permute-done | bytes 262176 | tf_op jit(solution)/shard_map/ppermute | solution.py:526
  162.1 8.2 %collective-permute-done.26.refs_1_ = bf16[2,128,512]{2,1,0:T(8,128)(2,1)S(1)} collective-permute-done((bf16[2,128,512]{2,1,0:T(8,128)(2,1)S(1)}, bf16[2,128,512]{2,1,0:T(8,128)(2,1)S(1)}, u32[]{:S(2)}, u32[]{:S(2)}) %collective-permute-start.26) | collective-permute-done | bytes 262176 | tf_op jit(solution)/shard_map/ppermute | solution.py:526
  171.8 7.4 %collective-permute-done.24.rest_received = bf16[4,128,256]{2,1,0:T(8,128)(2,1)S(1)} collective-permute-done((bf16[4,128,256]{2,1,0:T(8,128)(2,1)S(1)}, bf16[4,128,256]{2,1,0:T(8,128)(2,1)S(1)}, u32[]{:S(2)}, u32[]{:S(2)}) %collective-permute-start.24) | collective-permute-done | bytes 262176 | tf_op jit(solution)/shard_map/ppermute | solution.py:526
  179.1 3.1 %down_gradient.1 = (f32[384,256]{1,0:T(8,128)S(1)}, bf16[384,256]{1,0:T(8,128)(2,1)S(1)}, bf16[384,256]{1,0:T(8,128)(2,1)S(1)}, bf16[384,256]{1,0:T(8,128)(2,1)S(1)}) custom-call(s32[5]{0:T(128)S(1)} %copy-done.19, bf16[8,656,256]{2,1,0:T(8,128)(2,1)} %all-to-all-done.parcels, f32[4,128,256]{2,1,0:T(8,128)S(1)} %get-tuple-element.88.rest_keep, ...), custom_call_target="tpu_custom_call" | custom-call | flops 1000 | bytes 1000 | tf_op jit(solution)/shard_map/down_gradient/pallas_call | solution.py:443
  183.6 3.1 %collective-permute-start.35 = (bf16[384,256]{1,0:T(8,128)(2,1)S(1)}, bf16[384,256]{1,0:T(8,128)(2,1)S(1)}, u32[]{:S(2)}, u32[]{:S(2)}) collective-permute-start(bf16[384,256]{1,0:T(8,128)(2,1)S(1)} %get-tuple-element.84), channel_id=1, source_target_pairs={{0,3},{1,2},{2,1},{3,0},{4,7},{5,6},{6,5},{7,4},{8,11},{9,10},{10,... | collective-permute-start | bytes 589832 | tf_op jit(solution)/shard_map/ppermute | solution.py:526
  189.0 2.2 %collective-permute-done.33 = bf16[384,256]{1,0:T(8,128)(2,1)S(1)} collective-permute-done((bf16[384,256]{1,0:T(8,128)(2,1)S(1)}, bf16[384,256]{1,0:T(8,128)(2,1)S(1)}, u32[]{:S(2)}, u32[]{:S(2)}) %collective-permute-start.33) | collective-permute-done | bytes 196640 | tf_op jit(solution)/shard_map/ppermute | solution.py:526
  191.2 8.3 %collective-permute-done.34 = bf16[384,256]{1,0:T(8,128)(2,1)S(1)} collective-permute-done((bf16[384,256]{1,0:T(8,128)(2,1)S(1)}, bf16[384,256]{1,0:T(8,128)(2,1)S(1)}, u32[]{:S(2)}, u32[]{:S(2)}) %collective-permute-start.34) | collective-permute-done | bytes 196640 | tf_op jit(solution)/shard_map/ppermute | solution.py:526
  (140 shorter events, 31.1 us)
Async XLA Ops:
  4.3 11.6 %collective-permute-start = (bf16[768,128]{1,0:T(8,128)(2,1)}, bf16[768,128]{1,0:T(8,128)(2,1)S(1)}, u32[]{:S(2)}, u32[]{:S(2)}) collective-permute-start(bf16[768,128]{1,0:T(8,128)(2,1)} %get-tuple-element.45), channel_id=1, source_target_pairs={{0,1},{1,0},{2,3},{3,2},{4,5},{5,4},{6,7},{7,6},{8,9},{9,8},{10,11... | collective-permute-start | bytes 589832 | tf_op jit(solution)/shard_map/ppermute | solution.py:526
  7.4 17.4 %collective-permute-start.1 = (bf16[768,128]{1,0:T(8,128)(2,1)}, bf16[768,128]{1,0:T(8,128)(2,1)S(1)}, u32[]{:S(2)}, u32[]{:S(2)}) collective-permute-start(bf16[768,128]{1,0:T(8,128)(2,1)} %get-tuple-element.45), channel_id=1, source_target_pairs={{0,2},{1,3},{2,0},{3,1},{4,6},{5,7},{6,4},{7,5},{8,10},{9,11},{10,... | collective-permute-start | bytes 589832 | tf_op jit(solution)/shard_map/ppermute | solution.py:526
  10.0 14.8 %collective-permute-start.2 = (bf16[768,128]{1,0:T(8,128)(2,1)}, bf16[768,128]{1,0:T(8,128)(2,1)S(1)}, u32[]{:S(2)}, u32[]{:S(2)}) collective-permute-start(bf16[768,128]{1,0:T(8,128)(2,1)} %get-tuple-element.45), channel_id=1, source_target_pairs={{0,3},{1,2},{2,1},{3,0},{4,7},{5,6},{6,5},{7,4},{8,11},{9,10},{10,... | collective-permute-start | bytes 589832 | tf_op jit(solution)/shard_map/ppermute | solution.py:526
  24.9 7.6 %collective-permute-start.5 = (bf16[3,384,128]{2,1,0:T(8,128)(2,1)S(1)}, bf16[3,384,128]{2,1,0:T(8,128)(2,1)S(1)}, u32[]{:S(2)}, u32[]{:S(2)}) collective-permute-start(bf16[3,384,128]{2,1,0:T(8,128)(2,1)S(1)} %get-tuple-element.100), channel_id=1, source_target_pairs={{0,16},{4,20},{8,24},{12,28},{16,0},{20,4},{24,8},{28,12},{1,17},{... | collective-permute-start | bytes 884744 | tf_op jit(solution)/shard_map/ppermute | solution.py:526
  26.5 26.2 %collective-permute-start.11 = (bf16[2048,128]{1,0:T(8,128)(2,1)S(1)}, bf16[2048,128]{1,0:T(8,128)(2,1)S(1)}, u32[]{:S(2)}, u32[]{:S(2)}) collective-permute-start(bf16[2048,128]{1,0:T(8,128)(2,1)S(1)} %copy-done.26), channel_id=1, source_target_pairs={{0,2},{1,3},{2,0},{3,1},{4,6},{5,7},{6,4},{7,5},{8,10},{9,11},{10,... | collective-permute-start | bytes 1572872 | tf_op jit(solution)/shard_map/ppermute | solution.py:526
  30.9 10.0 %collective-permute-start.3 = (bf16[3,384,128]{2,1,0:T(8,128)(2,1)S(1)}, bf16[3,384,128]{2,1,0:T(8,128)(2,1)S(1)}, u32[]{:S(2)}, u32[]{:S(2)}) collective-permute-start(bf16[3,384,128]{2,1,0:T(8,128)(2,1)S(1)} %get-tuple-element.102), channel_id=1, source_target_pairs={{0,8},{4,12},{8,0},{12,4},{16,24},{20,28},{24,16},{28,20},{1,9},{5... | collective-permute-start | bytes 884744 | tf_op jit(solution)/shard_map/ppermute | solution.py:526
  32.5 36.6 %collective-permute-start.14 = (bf16[2,16,128,128]{3,2,1,0:T(8,128)(2,1)S(1)}, bf16[2,16,128,128]{3,2,1,0:T(8,128)(2,1)S(1)}, u32[]{:S(2)}, u32[]{:S(2)}) collective-permute-start(bf16[2,16,128,128]{3,2,1,0:T(8,128)(2,1)S(1)} %get-tuple-element.52), channel_id=1, source_target_pairs={{0,1},{1,0},{2,3},{3,2},{4,5},{5,4},{6,7},{7,6},{8,9},{9,8},{10,11... | collective-permute-start | bytes 3145736 | tf_op jit(solution)/shard_map/ppermute | solution.py:526
  32.5 33.7 %collective-permute-start.6 = (bf16[2,3,384,128]{3,2,1,0:T(8,128)(2,1)S(1)}, bf16[2,3,384,128]{3,2,1,0:T(8,128)(2,1)}, u32[]{:S(2)}, u32[]{:S(2)}) collective-permute-start(bf16[2,3,384,128]{3,2,1,0:T(8,128)(2,1)S(1)} %pad_maximum_fusion.1.own_c), channel_id=1, source_target_pairs={{0,8},{4,12},{8,0},{12,4},{16,24},{20,28},{24,16},{28,20},{1,9},{5... | collective-permute-start | bytes 1769480 | tf_op jit(solution)/shard_map/ppermute | solution.py:526
  41.0 25.8 %collective-permute-start.4 = (bf16[2,3,384,128]{3,2,1,0:T(8,128)(2,1)S(1)}, bf16[2,3,384,128]{3,2,1,0:T(8,128)(2,1)}, u32[]{:S(2)}, u32[]{:S(2)}) collective-permute-start(bf16[2,3,384,128]{3,2,1,0:T(8,128)(2,1)S(1)} %pad_maximum_fusion.own_a), channel_id=1, source_target_pairs={{0,16},{4,20},{8,24},{12,28},{16,0},{20,4},{24,8},{28,12},{1,17},{... | collective-permute-start | bytes 1769480 | tf_op jit(solution)/shard_map/ppermute | solution.py:526
  52.8 7.1 %collective-permute-start.12 = (bf16[1024,128]{1,0:T(8,128)(2,1)S(1)}, bf16[1024,128]{1,0:T(8,128)(2,1)S(1)}, u32[]{:S(2)}, u32[]{:S(2)}) collective-permute-start(bf16[1024,128]{1,0:T(8,128)(2,1)S(1)} %get-tuple-element.92), channel_id=1, source_target_pairs={{0,8},{4,12},{8,0},{12,4},{16,24},{20,28},{24,16},{28,20},{1,9},{5... | collective-permute-start | bytes 786440 | tf_op jit(solution)/shard_map/ppermute | solution.py:526
  54.4 13.3 %collective-permute-start.9 = (bf16[2,3,384,128]{3,2,1,0:T(8,128)(2,1)S(1)}, bf16[2,3,384,128]{3,2,1,0:T(8,128)(2,1)S(1)}, u32[]{:S(2)}, u32[]{:S(2)}) collective-permute-start(bf16[2,3,384,128]{3,2,1,0:T(8,128)(2,1)S(1)} %pad_maximum_fusion.1.own_c), channel_id=1, source_target_pairs={{0,4},{4,0},{8,12},{12,8},{16,20},{20,16},{24,28},{28,24},{1,5},{5... | collective-permute-start | bytes 1769480 | tf_op jit(solution)/shard_map/ppermute | solution.py:526
  59.9 6.4 %collective-permute-start.13 = (bf16[1024,128]{1,0:T(8,128)(2,1)S(1)}, bf16[1024,128]{1,0:T(8,128)(2,1)S(1)}, u32[]{:S(2)}, u32[]{:S(2)}) collective-permute-start(bf16[1024,128]{1,0:T(8,128)(2,1)S(1)} %get-tuple-element.91), channel_id=1, source_target_pairs={{0,16},{4,20},{8,24},{12,28},{16,0},{20,4},{24,8},{28,12},{1,17},{... | collective-permute-start | bytes 786440 | tf_op jit(solution)/shard_map/ppermute | solution.py:526
  66.3 10.0 %collective-permute-start.7 = (bf16[2,3,384,128]{3,2,1,0:T(8,128)(2,1)S(1)}, bf16[2,3,384,128]{3,2,1,0:T(8,128)(2,1)}, u32[]{:S(2)}, u32[]{:S(2)}) collective-permute-start(bf16[2,3,384,128]{3,2,1,0:T(8,128)(2,1)S(1)} %pad_maximum_fusion.own_a), channel_id=1, source_target_pairs={{0,4},{4,0},{8,12},{12,8},{16,20},{20,16},{24,28},{28,24},{1,5},{5... | collective-permute-start | bytes 1769480 | tf_op jit(solution)/shard_map/ppermute | solution.py:526
  66.3 10.0 %collective-permute-start.10 = (bf16[2,3,384,128]{3,2,1,0:T(8,128)(2,1)}, bf16[2,3,384,128]{3,2,1,0:T(8,128)(2,1)}, u32[]{:S(2)}, u32[]{:S(2)}) collective-permute-start(bf16[2,3,384,128]{3,2,1,0:T(8,128)(2,1)} %collective-permute-done.6.own_d), channel_id=1, source_target_pairs={{0,4},{4,0},{8,12},{12,8},{16,20},{20,16},{24,28},{28,24},{1,5},{5... | collective-permute-start | bytes 1769480 | tf_op jit(solution)/shard_map/ppermute | solution.py:526
  66.8 9.5 %collective-permute-start.8 = (bf16[2,3,384,128]{3,2,1,0:T(8,128)(2,1)}, bf16[2,3,384,128]{3,2,1,0:T(8,128)(2,1)}, u32[]{:S(2)}, u32[]{:S(2)}) collective-permute-start(bf16[2,3,384,128]{3,2,1,0:T(8,128)(2,1)} %collective-permute-done.4.own_b), channel_id=1, source_target_pairs={{0,4},{4,0},{8,12},{12,8},{16,20},{20,16},{24,28},{28,24},{1,5},{5... | collective-permute-start | bytes 1769480 | tf_op jit(solution)/shard_map/ppermute | solution.py:526
  68.5 26.3 %collective-permute-start.15 = (bf16[2,1024,128]{2,1,0:T(8,128)(2,1)}, bf16[2,1024,128]{2,1,0:T(8,128)(2,1)}, u32[]{:S(2)}, u32[]{:S(2)}) collective-permute-start(bf16[2,1024,128]{2,1,0:T(8,128)(2,1)} %pad_maximum_fusion.2.refs_0_), channel_id=1, source_target_pairs={{0,16},{4,20},{8,24},{12,28},{16,0},{20,4},{24,8},{28,12},{1,17},{... | collective-permute-start | bytes 1572872 | tf_op jit(solution)/shard_map/ppermute | solution.py:526
  69.0 25.8 %collective-permute-start.16 = (bf16[2,1024,128]{2,1,0:T(8,128)(2,1)}, bf16[2,1024,128]{2,1,0:T(8,128)(2,1)}, u32[]{:S(2)}, u32[]{:S(2)}) collective-permute-start(bf16[2,1024,128]{2,1,0:T(8,128)(2,1)} %pad_maximum_fusion.3.refs_2_), channel_id=1, source_target_pairs={{0,8},{4,12},{8,0},{12,4},{16,24},{20,28},{24,16},{28,20},{1,9},{5... | collective-permute-start | bytes 1572872 | tf_op jit(solution)/shard_map/ppermute | solution.py:526
  94.8 37.4 %all-to-all-start = ((bf16[8,656,256]{2,1,0:T(8,128)(2,1)}), bf16[8,656,256]{2,1,0:T(8,128)(2,1)}, u32[]{:S(2)}, u32[]{:S(2)}) async-start(bf16[8,656,256]{2,1,0:T(8,128)(2,1)} %get-tuple-element.62), calls=%async_computation | async-start | bytes 5373952 | tf_op jit(solution)/shard_map/all_to_all | solution.py:590
  100.2 3.8 %collective-permute-start.20 = (bf16[2,1024,128]{2,1,0:T(8,128)(2,1)}, bf16[2,1024,128]{2,1,0:T(8,128)(2,1)S(1)}, u32[]{:S(2)}, u32[]{:S(2)}) collective-permute-start(bf16[2,1024,128]{2,1,0:T(8,128)(2,1)} %collective-permute-done.16.refs_3_), channel_id=1, source_target_pairs={{0,4},{4,0},{8,12},{12,8},{16,20},{20,16},{24,28},{28,24},{1,5},{5... | collective-permute-start | bytes 1572872 | tf_op jit(solution)/shard_map/ppermute | solution.py:526
  110.7 22.7 %collective-permute-start.21 = (bf16[256,1024]{1,0:T(8,128)(2,1)}, bf16[256,1024]{1,0:T(8,128)(2,1)}, u32[]{:S(2)}, u32[]{:S(2)}) collective-permute-start(bf16[256,1024]{1,0:T(8,128)(2,1)} %get-tuple-element.67), channel_id=1, source_target_pairs={{0,1},{1,0},{2,3},{3,2},{4,5},{5,4},{6,7},{7,6},{8,9},{9,8},{10,11... | collective-permute-start | bytes 1572872 | tf_op jit(solution)/shard_map/ppermute | solution.py:526
  146.2 6.0 %collective-permute-start.27 = (bf16[128,512]{1,0:T(8,128)(2,1)S(1)}, bf16[128,512]{1,0:T(8,128)(2,1)S(1)}, u32[]{:S(2)}, u32[]{:S(2)}) collective-permute-start(bf16[128,512]{1,0:T(8,128)(2,1)S(1)} %get-tuple-element.105), channel_id=1, source_target_pairs={{0,16},{4,20},{8,24},{12,28},{16,0},{20,4},{24,8},{28,12},{1,17},{... | collective-permute-start | bytes 393224 | tf_op jit(solution)/shard_map/ppermute | solution.py:526
  150.6 19.7 %collective-permute-start.23 = (bf16[2,4,128,256]{3,2,1,0:T(8,128)(2,1)S(1)}, bf16[2,4,128,256]{3,2,1,0:T(8,128)(2,1)S(1)}, u32[]{:S(2)}, u32[]{:S(2)}) collective-permute-start(bf16[2,4,128,256]{3,2,1,0:T(8,128)(2,1)S(1)} %bitcast.88), channel_id=1, source_target_pairs={{0,16},{4,20},{8,24},{12,28},{16,0},{20,4},{24,8},{28,12},{1,17},{... | collective-permute-start | bytes 1572872 | tf_op jit(solution)/shard_map/ppermute | solution.py:526
  151.2 6.4 %collective-permute-start.25 = (bf16[128,512]{1,0:T(8,128)(2,1)S(1)}, bf16[128,512]{1,0:T(8,128)(2,1)S(1)}, u32[]{:S(2)}, u32[]{:S(2)}) collective-permute-start(bf16[128,512]{1,0:T(8,128)(2,1)S(1)} %get-tuple-element.104), channel_id=1, source_target_pairs={{0,8},{4,12},{8,0},{12,4},{16,24},{20,28},{24,16},{28,20},{1,9},{5... | collective-permute-start | bytes 393224 | tf_op jit(solution)/shard_map/ppermute | solution.py:526
  152.2 9.9 %collective-permute-start.28 = (bf16[2,128,512]{2,1,0:T(8,128)(2,1)S(1)}, bf16[2,128,512]{2,1,0:T(8,128)(2,1)S(1)}, u32[]{:S(2)}, u32[]{:S(2)}) collective-permute-start(bf16[2,128,512]{2,1,0:T(8,128)(2,1)S(1)} %pad_maximum_fusion.7.refs_2_), channel_id=1, source_target_pairs={{0,8},{4,12},{8,0},{12,4},{16,24},{20,28},{24,16},{28,20},{1,9},{5... | collective-permute-start | bytes 786440 | tf_op jit(solution)/shard_map/ppermute | solution.py:526
  157.6 12.6 %collective-permute-start.26 = (bf16[2,128,512]{2,1,0:T(8,128)(2,1)S(1)}, bf16[2,128,512]{2,1,0:T(8,128)(2,1)S(1)}, u32[]{:S(2)}, u32[]{:S(2)}) collective-permute-start(bf16[2,128,512]{2,1,0:T(8,128)(2,1)S(1)} %pad_maximum_fusion.6.refs_0_), channel_id=1, source_target_pairs={{0,16},{4,20},{8,24},{12,28},{16,0},{20,4},{24,8},{28,12},{1,17},{... | collective-permute-start | bytes 786440 | tf_op jit(solution)/shard_map/ppermute | solution.py:526
  159.1 11.8 %collective-permute-start.31 = (bf16[2,128,512]{2,1,0:T(8,128)(2,1)S(1)}, bf16[2,128,512]{2,1,0:T(8,128)(2,1)S(1)}, u32[]{:S(2)}, u32[]{:S(2)}) collective-permute-start(bf16[2,128,512]{2,1,0:T(8,128)(2,1)S(1)} %pad_maximum_fusion.7.refs_2_), channel_id=1, source_target_pairs={{0,4},{4,0},{8,12},{12,8},{16,20},{20,16},{24,28},{28,24},{1,5},{5... | collective-permute-start | bytes 786440 | tf_op jit(solution)/shard_map/ppermute | solution.py:526
  159.1 11.8 %collective-permute-start.29 = (bf16[2,128,512]{2,1,0:T(8,128)(2,1)S(1)}, bf16[2,128,512]{2,1,0:T(8,128)(2,1)S(1)}, u32[]{:S(2)}, u32[]{:S(2)}) collective-permute-start(bf16[2,128,512]{2,1,0:T(8,128)(2,1)S(1)} %pad_maximum_fusion.6.refs_0_), channel_id=1, source_target_pairs={{0,4},{4,0},{8,12},{12,8},{16,20},{20,16},{24,28},{28,24},{1,5},{5... | collective-permute-start | bytes 786440 | tf_op jit(solution)/shard_map/ppermute | solution.py:526
  162.1 8.9 %collective-permute-start.32 = (bf16[2,128,512]{2,1,0:T(8,128)(2,1)S(1)}, bf16[2,128,512]{2,1,0:T(8,128)(2,1)S(1)}, u32[]{:S(2)}, u32[]{:S(2)}) collective-permute-start(bf16[2,128,512]{2,1,0:T(8,128)(2,1)S(1)} %collective-permute-done.28.refs_3_), channel_id=1, source_target_pairs={{0,4},{4,0},{8,12},{12,8},{16,20},{20,16},{24,28},{28,24},{1,5},{5... | collective-permute-start | bytes 786440 | tf_op jit(solution)/shard_map/ppermute | solution.py:526
  170.3 8.8 %collective-permute-start.24 = (bf16[4,128,256]{2,1,0:T(8,128)(2,1)S(1)}, bf16[4,128,256]{2,1,0:T(8,128)(2,1)S(1)}, u32[]{:S(2)}, u32[]{:S(2)}) collective-permute-start(bf16[4,128,256]{2,1,0:T(8,128)(2,1)S(1)} %get-tuple-element.87), channel_id=1, source_target_pairs={{0,8},{4,12},{8,0},{12,4},{16,24},{20,28},{24,16},{28,20},{1,9},{5... | collective-permute-start | bytes 786440 | tf_op jit(solution)/shard_map/ppermute | solution.py:526
  182.3 9.0 %collective-permute-start.33 = (bf16[384,256]{1,0:T(8,128)(2,1)S(1)}, bf16[384,256]{1,0:T(8,128)(2,1)S(1)}, u32[]{:S(2)}, u32[]{:S(2)}) collective-permute-start(bf16[384,256]{1,0:T(8,128)(2,1)S(1)} %get-tuple-element.82), channel_id=1, source_target_pairs={{0,1},{1,0},{2,3},{3,2},{4,5},{5,4},{6,7},{7,6},{8,9},{9,8},{10,11... | collective-permute-start | bytes 589832 | tf_op jit(solution)/shard_map/ppermute | solution.py:526
  182.3 17.2 %collective-permute-start.34 = (bf16[384,256]{1,0:T(8,128)(2,1)S(1)}, bf16[384,256]{1,0:T(8,128)(2,1)S(1)}, u32[]{:S(2)}, u32[]{:S(2)}) collective-permute-start(bf16[384,256]{1,0:T(8,128)(2,1)S(1)} %get-tuple-element.83), channel_id=1, source_target_pairs={{0,2},{1,3},{2,0},{3,1},{4,6},{5,7},{6,4},{7,5},{8,10},{9,11},{10,... | collective-permute-start | bytes 589832 | tf_op jit(solution)/shard_map/ppermute | solution.py:526
  183.6 15.9 %collective-permute-start.35 = (bf16[384,256]{1,0:T(8,128)(2,1)S(1)}, bf16[384,256]{1,0:T(8,128)(2,1)S(1)}, u32[]{:S(2)}, u32[]{:S(2)}) collective-permute-start(bf16[384,256]{1,0:T(8,128)(2,1)S(1)} %get-tuple-element.84), channel_id=1, source_target_pairs={{0,3},{1,2},{2,1},{3,0},{4,7},{5,6},{6,5},{7,4},{8,11},{9,10},{10,... | collective-permute-start | bytes 589832 | tf_op jit(solution)/shard_map/ppermute | solution.py:526
  (32 other events, 421.5 us)

commit v3 on v2

--- a/solution.py
+++ b/solution.py
@@ -20,7 +20,7 @@
 MARGIN = (KS - STRIDE) // 2
 SHARE = TILE_DEV // 8
 WINDOW_ROWS = 2 * OUTF * TILE_DEV
-WEIGHT_ROW = WINDOW_ROWS + OUTF * DL // CS * SHARE
+PARCEL_ROWS = WINDOW_ROWS + OUTF * DL // CS * SHARE
 ROWS = TILE_DEV * TILE_FRAMES
 LATENTS = TILE_DEV * OUTF
 N_FSDP = 4
@@ -125,7 +125,7 @@
     )(place, tiles.reshape(ROWS, CT), alpha.reshape(1, CT))
 
 
-def _pack_kernel(place, dilated, mix, down, proj, teacher, packed, columns, sems):
+def _pack_kernel(place, dilated, mix, down, proj, teacher, packed, early, late, sems):
     core, slab = place[0], place[3]
     copies = []
     row = 0
@@ -140,7 +140,10 @@
             ))
             row += rows
     begin = pl.multiple_of((core * SLABS + slab) * 128, 128)
-    copies.append(pltpu.make_async_copy(teacher.at[:, pl.ds(begin, 128)], columns, sems.at[len(copies)]))
+    half = KS * QUARTER // 2
+    for index, out in enumerate((early, late)):
+        source = teacher.at[index * half : (index + 1) * half, pl.ds(begin, 128)]
+        copies.append(pltpu.make_async_copy(source, out, sems.at[len(copies)]))
     for copy in copies:
         copy.start()
     for copy in copies:
@@ -152,12 +155,13 @@
     return pl.pallas_call(
         _pack_kernel,
         in_specs=[pl.BlockSpec(memory_space=pltpu.SMEM)] + [anywhere] * 5,
-        out_specs=[pl.BlockSpec(memory_space=pltpu.VMEM)] * 2,
+        out_specs=[pl.BlockSpec(memory_space=pltpu.VMEM)] * 3,
         out_shape=[
             jax.ShapeDtypeStruct((PACK_ROWS, 128), BF16),
-            jax.ShapeDtypeStruct((KS * QUARTER, 128), BF16),
+            jax.ShapeDtypeStruct((KS * QUARTER // 2, 128), BF16),
+            jax.ShapeDtypeStruct((KS * QUARTER // 2, 128), BF16),
         ],
-        scratch_shapes=[pltpu.SemaphoreType.DMA((9,))],
+        scratch_shapes=[pltpu.SemaphoreType.DMA((10,))],
         name="pack_kernels",
         cost_estimate=COST,
     )(place, *kernels)
@@ -245,7 +249,7 @@
 
 def _forward_kernel(
     place, tiles, own_a, own_b, own_c, own_d, other_a, other_b, other_c, other_d,
-    near_dilated, near_mix, near_down, near_proj, alphas, routes, weights,
+    near_dilated, near_mix, near_down, near_proj, alphas, routes,
     act_one, act_two, act_three, slope_two, slope_three, student, predicted, mix, down, proj, parcel,
     dilated, held,
 ):
@@ -334,13 +338,6 @@
                 parcel[owner, row : row + SHARE, :] = picked[
                     owner * SHARE : (owner + 1) * SHARE, block * CS : (block + 1) * CS
                 ]
-    first = weights[...].astype(BF16).astype(F32)
-    second = (weights[...] - first).astype(BF16).astype(F32)
-    third = weights[...] - first - second
-    lane = lax.broadcasted_iota(jnp.int32, (TILE_DEV, CS), 1)
-    split = jnp.where(lane == 0, first, jnp.where(lane == 1, second, jnp.where(lane == 2, third, 0.0))).astype(BF16)
-    for owner in range(8):
-        parcel[owner, WEIGHT_ROW:, :] = split[owner * SHARE : (owner + 1) * SHARE, :]
     for tap in range(KS):
         for offset in range(OUTF):
             frame = STRIDE * offset - MARGIN + tap
@@ -351,7 +348,7 @@
                 parcel[tap // 2, row : row + TILE_DEV, :] = jnp.zeros((TILE_DEV, CS), BF16)
 
 
-def _forward(place, tiles, own, other, kernels, alphas, routes, weights):
+def _forward(place, tiles, own, other, kernels, alphas, routes):
     frames = (TILE_FRAMES, TILE_DEV, CS)
     whole = pl.BlockSpec(memory_space=pltpu.VMEM)
     return pl.pallas_call(
@@ -360,7 +357,7 @@
             pl.BlockSpec(memory_space=pltpu.SMEM),
             whole,
         ]
-        + [whole] * 15,
+        + [whole] * 14,
         out_specs=[whole] * 11,
         out_shape=[
             jax.ShapeDtypeStruct(frames, BF16),
@@ -373,7 +370,7 @@
             jax.ShapeDtypeStruct((CS // 128, CS, 128), BF16),
             jax.ShapeDtypeStruct((CSO // 128, KS * CS, 128), BF16),
             jax.ShapeDtypeStruct((DL // 128, CSO, 128), BF16),
-            jax.ShapeDtypeStruct((8, WEIGHT_ROW + SHARE, CS), BF16),
+            jax.ShapeDtypeStruct((8, PARCEL_ROWS, CS), BF16),
         ],
         scratch_shapes=[
             pltpu.VMEM((CS // 128, DILATED_TAPS * CS, 128), BF16),
@@ -382,7 +379,7 @@
         name="student_forward",
         compiler_params=pltpu.CompilerParams(vmem_limit_bytes=VMEM_LIMIT),
         cost_estimate=COST,
-    )(place, tiles.reshape(ROWS, CS), *own, *other, *kernels, alphas, routes, weights)
+    )(place, tiles.reshape(ROWS, CS), *own, *other, *kernels, alphas, routes)
 
 
 def _stacked(values, columns):
@@ -391,7 +388,10 @@
     )
 
 
-def _error_kernel(target_own, target_other, predicted, weights, proj, back_student, error):
+def _error_kernel(
+    place, target_own, target_other, predicted, weights, student, proj, back_student, send, keep, error, grad_proj
+):
+    me = place[1]
     weight = weights[...] * (1.0 / LATENTS)
     for offset in range(OUTF):
         rows = slice(offset * TILE_DEV, (offset + 1) * TILE_DEV)
@@ -400,25 +400,33 @@
         error[rows, :] = (weight * (predicted[rows, :] - target)).astype(BF16)
     back = _dot_nt(error[...], _lanes(proj, slice(None))).astype(BF16)
     back_student[...] = back.reshape(OUTF, TILE_DEV, CSO)
-
-
-def _error(targets, predicted, weights, proj):
+    grad_proj[...] = _dot_tn(student[...], error[...])
+    for spot in range(CHUNKS):
+        share = grad_proj[pl.ds(pl.multiple_of((me ^ spot) * 16, 16), 16), :]
+        out = send if (spot // 4) % 2 else keep
+        out[(spot // 8 % 2) * 8 + (spot // 16) * 4 + spot % 4] = _stacked(share, 256).astype(out.dtype)
+
+
+def _error(place, targets, predicted, weights, student, proj):
+    half = (CHUNKS // 2, 64, 256)
     whole = pl.BlockSpec(memory_space=pltpu.VMEM)
     return pl.pallas_call(
         _error_kernel,
-        in_specs=[whole] * 5,
-        out_specs=[whole] * 2,
+        in_specs=[pl.BlockSpec(memory_space=pltpu.SMEM)] + [whole] * 6,
+        out_specs=[whole] * 3,
         out_shape=[
             jax.ShapeDtypeStruct((OUTF, TILE_DEV, CSO), BF16),
-            jax.ShapeDtypeStruct((LATENTS, DL), BF16),
+            jax.ShapeDtypeStruct(half, BF16),
+            jax.ShapeDtypeStruct(half, F32),
         ],
+        scratch_shapes=[pltpu.VMEM((LATENTS, DL), BF16), pltpu.VMEM((CSO, DL), F32)],
         name="error_backward",
-        compiler_params=pltpu.CompilerParams(vmem_limit_bytes=VMEM_LIMIT),
-        cost_estimate=COST,
-    )(*targets, predicted, weights, proj)
-
-
-def _down_kernel(place, parcels, rest_keep, rest_received, *refs):
+        compiler_params=pltpu.CompilerParams(vmem_limit_bytes=60 * 1024 * 1024),
+        cost_estimate=COST,
+    )(place, *targets, predicted, weights, student, proj)
+
+
+def _down_kernel(place, parcels, *refs):
     own, other, (keep, *sends), grads = refs[:4], refs[4:8], refs[8:12], refs[12]
     fsdp, chip = place[2], place[4]
     back = []
@@ -434,27 +442,59 @@
         grads[tap * CS : (tap + 1) * CS, :] = _dot_tn(jnp.concatenate(rows, axis=0), back)
     for spot, out in enumerate((keep, *sends)):
         part = grads[pl.ds(pl.multiple_of((spot ^ fsdp) * 128, 128), 128), :]
-        out[0:256, :] = _stacked(part, 256).astype(out.dtype)
-        out[256:384, :] = (rest_keep[spot] + rest_received[spot].astype(F32)).astype(out.dtype)
-
-
-def _down(place, parcels, rest, own, other):
+        out[...] = part.astype(out.dtype)
+
+
+def _down(place, parcels, own, other):
     whole = pl.BlockSpec(memory_space=pltpu.VMEM)
     return pl.pallas_call(
         _down_kernel,
-        in_specs=[pl.BlockSpec(memory_space=pltpu.SMEM)] + [whole] * 11,
+        in_specs=[pl.BlockSpec(memory_space=pltpu.SMEM)] + [whole] * 9,
         out_specs=[whole] * 4,
-        out_shape=[jax.ShapeDtypeStruct((384, 256), F32)] + [jax.ShapeDtypeStruct((384, 256), BF16)] * 3,
+        out_shape=[jax.ShapeDtypeStruct((128, CSO), F32)] + [jax.ShapeDtypeStruct((128, CSO), BF16)] * 3,
         scratch_shapes=[pltpu.VMEM((CSO, CSO), F32)],
         name="down_gradient",
         compiler_params=pltpu.CompilerParams(vmem_limit_bytes=VMEM_LIMIT),
         cost_estimate=COST,
-    )(place, parcels, *rest, *own, *other)
+    )(place, parcels, *own, *other)
+
+
+def _flat(out, values):
+    blocks = values.shape[1] // 128
+    for block in range(blocks):
+        out[pl.ds(block, values.shape[0], stride=blocks), :] = values[:, block * 128 : (block + 1) * 128]
+
+
+def _finish_kernel(down, rest_proj, rest_other, *refs):
+    downs, rests, (dilated, mix, full_down, proj) = refs[:3], refs[3:6], refs[6:]
+    total = down[...]
+    for part in downs:
+        total += part[...].astype(F32)
+    _flat(full_down, total)
+    total = jnp.concatenate([rest_proj[...], rest_other[...]], axis=0)
+    for part in rests:
+        total += part[...].astype(F32)
+    _flat(proj, jnp.concatenate([total[16 * i : 16 * (i + 1)] for i in range(4)], axis=1))
+    _flat(dilated, total[64:120])
+    _flat(mix, total[120:128])
+
+
+def _finish(down, downs, rest, rests):
+    whole = pl.BlockSpec(memory_space=pltpu.VMEM)
+    return pl.pallas_call(
+        _finish_kernel,
+        in_specs=[whole] * 9,
+        out_specs=[whole] * 4,
+        out_shape=[jax.ShapeDtypeStruct((rows, 128), F32) for rows in (112, 16, 512, 128)],
+        name="finish_gradients",
+        compiler_params=pltpu.CompilerParams(vmem_limit_bytes=VMEM_LIMIT),
+        cost_estimate=COST,
+    )(down, *rest, *downs, *rests)
 
 
 def _residual_kernel(
-    place, back_student, error, student, down, mix, act_one, act_two, slope_two, slope_three,
-    send, keep, back_three, back_residual, back_hidden, grad_dilated, grad_mix, grad_proj,
+    place, back_student, down, mix, act_one, act_two, slope_two, slope_three,
+    send, keep, back_three, back_residual, back_hidden, grad_dilated, grad_mix,
 ):
     me = place[1]
     back = back_student[...].reshape(LATENTS, CSO)
@@ -485,12 +525,10 @@
         grad_dilated[tap * CS : (tap + 1) * CS, :] = _dot_tn(
             act_one[first + shift : last + shift].reshape(rows, CS), back_hidden[first * TILE_DEV : last * TILE_DEV, :]
         )
-    grad_proj[...] = _dot_tn(student[...], error[...])
     for place_index in range(CHUNKS):
         chunk = me ^ place_index
         part = jnp.concatenate(
             [
-                _stacked(grad_proj[pl.ds(pl.multiple_of(chunk * 16, 16), 16), :], 256),
                 grad_dilated[pl.ds(pl.multiple_of(chunk * 56, 8), 56), :],
                 grad_mix[pl.ds(pl.multiple_of(chunk * 8, 8), 8), :],
             ],
@@ -500,12 +538,12 @@
         out[(place_index // 8) * 4 + place_index % 4] = part.astype(out.dtype)
 
 
-def _residual(place, back_student, error, student, down, mix, act_one, act_two, slope_two, slope_three):
+def _residual(place, back_student, down, mix, act_one, act_two, slope_two, slope_three):
     whole = pl.BlockSpec(memory_space=pltpu.VMEM)
-    half = (CHUNKS // 2, 128, 256)
+    half = (CHUNKS // 2, 64, 256)
     return pl.pallas_call(
         _residual_kernel,
-        in_specs=[pl.BlockSpec(memory_space=pltpu.SMEM)] + [whole] * 9,
+        in_specs=[pl.BlockSpec(memory_space=pltpu.SMEM)] + [whole] * 7,
         out_specs=[whole] * 2,
         out_shape=[jax.ShapeDtypeStruct(half, BF16), jax.ShapeDtypeStruct(half, F32)],
         scratch_shapes=[
@@ -514,12 +552,11 @@
             pltpu.VMEM((ROWS, CS), BF16),
             pltpu.VMEM((DILATED_TAPS * CS, CS), F32),
             pltpu.VMEM((CS, CS), F32),
-            pltpu.VMEM((CSO, DL), F32),
         ],
         name="residual_backward",
         compiler_params=pltpu.CompilerParams(vmem_limit_bytes=VMEM_LIMIT),
         cost_estimate=COST,
-    )(place, back_student, error, student, down, mix, act_one, act_two, slope_two, slope_three)
+    )(place, back_student, down, mix, act_one, act_two, slope_two, slope_three)
 
 
 def _swap(values, axis, bit):
@@ -552,81 +589,88 @@
         return jnp.stack([early, _swap(early, "dp", 2)]), jnp.stack([late, _swap(late, "dp", 4)])
 
     def plane_gather(early, late):
-        own = (early, _swap(early, "dp", 4), late, _swap(late, "dp", 2))
+        return early, _swap(early, "dp", 4), late, _swap(late, "dp", 2)
+
+    def core_gather(own):
         return own, tuple(_swap(part, "dp", 1) for part in own)
 
     kernels = (kernel_dilated, kernel_mix, kernel_down, kernel_proj)
     flat_teacher = kernel_teacher.reshape(KS * QUARTER, DL)
-    packed, columns = _pack(place, *kernels, flat_teacher)
+    packed, early, late = _pack(place, *kernels, flat_teacher)
     fetched = [_swap(packed, "fsdp", bit) for bit in range(1, N_FSDP)]
-    columns = _swap(columns, "fsdp", 2)
+    early, late = _swap(early, "fsdp", 2), _swap(late, "fsdp", 2)
+
+    routes = send_list.reshape(-1)
+    slot_weights = lax.all_to_all(
+        clip_weight.reshape(n_dp, TILE_DEV // n_dp), "dp", split_axis=0, concat_axis=0, tiled=True
+    ).reshape(-1)
+    hits = routes[:, None] == jnp.arange(TILE_DEV, dtype=jnp.int32)[None, :]
+    weights = jnp.sum(jnp.where(hits, slot_weights[:, None], 0.0), axis=0)[:, None]
 
     mine, sent = _teacher_act(place, teacher_tiles, alpha_teacher)
-    fetched, sent = lax.optimization_barrier((fetched, sent))
+    fetched, sent, weights = lax.optimization_barrier((fetched, sent, weights))
     theirs = _swap(sent, "fsdp", 1)
 
     half = PACK_ROWS // 2
     spread = plane_spread(
         jnp.stack([part[:half] for part in fetched]), jnp.stack([part[half:] for part in fetched])
     )
-    own, other = plane_gather(*spread)
-    spread = plane_spread(columns[: KS * QUARTER // 2], columns[KS * QUARTER // 2 :])
-    near = _teacher_near(mine, theirs, flat_teacher)
-    teacher_own, teacher_other = plane_gather(*spread)
-    own, other, _, near = lax.optimization_barrier((own, other, spread, near))
+    spread, early = lax.optimization_barrier((spread, early))
+    own, other = core_gather(plane_gather(*spread))
+    early, late, _ = lax.optimization_barrier((early, late, own))
+    spread = plane_spread(early, late)
+    teacher_own = plane_gather(*spread)
+    own, other, _ = lax.optimization_barrier((own, other, spread))
 
     alphas = jnp.stack([alpha_one, alpha_two, alpha_three])
-    routes = send_list.reshape(-1)
     (
         act_one, act_two, act_three, slope_two, slope_three, student, predicted, mix, down, proj, parcel,
-    ) = _forward(place, student_tiles, own, other, kernels, alphas, routes[:, None], clip_weight[:, None])
-    near, predicted = lax.optimization_barrier((near, predicted))
+    ) = _forward(place, student_tiles, own, other, kernels, alphas, routes[:, None])
+    theirs, teacher_own, predicted = lax.optimization_barrier((theirs, teacher_own, predicted))
+    teacher_own, teacher_other = core_gather(teacher_own)
+    near = _teacher_near(mine, theirs, flat_teacher)
     target, partial = _teacher_far(place, near, mine, theirs, teacher_own, teacher_other)
     targets = (target, _swap(partial, "fsdp", 1))
 
-    latent_rows = parcel[:, WINDOW_ROWS:WEIGHT_ROW].reshape(8, OUTF * DL // CS, SHARE, CS)
+    latent_rows = parcel[:, WINDOW_ROWS:].reshape(8, OUTF * DL // CS, SHARE, CS)
     if halving:
-        parcel, _ = lax.optimization_barrier((parcel, teacher_own))
         parcels = lax.all_to_all(parcel, "dp", split_axis=0, concat_axis=0, tiled=True)
-        latent = parcels[:, WINDOW_ROWS:WEIGHT_ROW].reshape(8, OUTF * DL // CS, SHARE, CS).transpose(0, 2, 1, 3)
-        slot_weights = jnp.sum(parcels[:, WEIGHT_ROW:, :3].astype(F32), axis=2).reshape(-1)
+        latent = parcels[:, WINDOW_ROWS:].reshape(8, OUTF * DL // CS, SHARE, CS).transpose(0, 2, 1, 3)
     else:
         latent = latent_rows.transpose(0, 2, 1, 3).reshape(TILE_DEV, OUTF * DL)
         latent = lax.all_to_all(latent, "dp", split_axis=0, concat_axis=0, tiled=True)
-        slot_weights = lax.all_to_all(
-            clip_weight.reshape(n_dp, TILE_DEV // n_dp), "dp", split_axis=0, concat_axis=0, tiled=True
-        ).reshape(-1)
     latent = latent.reshape(TILE_DEV, OUTF, DL)
-    hits = routes[:, None] == jnp.arange(TILE_DEV, dtype=jnp.int32)[None, :]
-    weights = jnp.sum(jnp.where(hits, slot_weights[:, None], 0.0), axis=0)[:, None]
-
-    back_student, error = _error(targets, predicted, weights, proj)
-    send, keep = _residual(place, back_student, error, student, down, mix, act_one, act_two, slope_two, slope_three)
+    back_student, send_a, keep_a = _error(place, targets, predicted, weights, student, proj)
+    send_b, keep_b = _residual(place, back_student, down, mix, act_one, act_two, slope_two, slope_three)
 
     if halving:
-        keep = keep.reshape(2, 2, N_FSDP, 128, 256)
-        received = _swap(send, "dp", 1).reshape(keep.shape)
-        for bit in (4, 2):
-            keep, out = keep[0] + received[0].astype(F32), (keep[1] + received[1].astype(F32)).astype(BF16)
-            received = _swap(out, "dp", bit)
-        part, *sends = _down(
-            place, parcels, (keep, received), *plane_gather(*plane_spread(back_student[0], back_student[1]))
-        )
-        for bit, out in zip(range(1, N_FSDP), sends):
-            part = part + _swap(out, "fsdp", bit).astype(F32)
-        grad_down = jnp.concatenate([part[:128], part[128:256]], axis=1).reshape(-1)
-        grad_proj = jnp.concatenate([part[256 + 16 * i : 272 + 16 * i] for i in range(4)], axis=1).reshape(-1)
-        grad_dilated, grad_mix = part[320:376].reshape(-1), part[376:].reshape(-1)
+        def reduce_plane(send, keep, order):
+            keep = keep.reshape(2, 2, N_FSDP, 64, 256)
+            received = _swap(send, "dp", 1).reshape(keep.shape)
+            for bit in (2, 4) if order == "xy" else (4, 2):
+                keep, out = keep[0] + received[0].astype(F32), (keep[1] + received[1].astype(F32)).astype(BF16)
+                received = _swap(out, "dp", bit)
+            return keep + received.astype(F32)
+
+        back_student, parcels = lax.optimization_barrier((back_student, parcels))
+        keep_d, *sends = _down(place, parcels, *core_gather(plane_gather(*plane_spread(back_student[0], back_student[1]))))
+        downs = [_swap(out, "fsdp", bit) for bit, out in zip(range(1, N_FSDP), sends)]
+        rest_a, rest_b = reduce_plane(send_a, keep_a, "xy"), reduce_plane(send_b, keep_b, "yx")
+        rest = jnp.concatenate([rest_a, rest_b], axis=1)
+        rests = [_swap(rest[bit].astype(BF16), "fsdp", bit) for bit in range(1, N_FSDP)]
+        grads = _finish(keep_d, downs, (rest_a[0], rest_b[0]), rests)
+        grad_dilated, grad_mix, grad_down, grad_proj = [grad.reshape(-1) for grad in grads]
     else:
         def joined(send, keep):
-            rows = keep.shape[1]
+            rows = keep.shape[-2]
             both = jnp.stack([keep.reshape(4, 4, rows, 256), send.astype(F32).reshape(4, 4, rows, 256)], axis=1)
             return both.reshape(CHUNKS, rows, 256)
 
         def scattered(values):
             return lax.psum_scatter(values.reshape(-1), ("dp", "fsdp"), scatter_dimension=0, tiled=True)
 
-        part = joined(send, keep)
+        turned = [jnp.swapaxes(half.reshape(2, 2, N_FSDP, 64, 256), 0, 1) for half in (send_a, keep_a)]
+        part = jnp.concatenate([joined(*turned), joined(send_b, keep_b)], axis=1)
         windows = parcel[:, :WINDOW_ROWS].reshape(KS, OUTF, TILE_DEV, CS)
         grad_down = scattered(jnp.einsum("kotc,otd->kcd", windows, back_student, preferred_element_type=F32))
         grad_proj = scattered(jnp.concatenate([part[:, 16 * i : 16 * (i + 1)] for i in range(4)], axis=2))

time: 203 us -> 192 us (0.946)
  waiting for transfers between devices: 99.4 us -> 62.5 us
  starting transfers between devices: 34.8 us -> 48.8 us
  local copies, waits for them, and re-layouts: 13.3 us -> 20.4 us
  other arithmetic: 4.91 us -> 7.45 us
    all_to_all x1, waiting for transfers between devices: 21.5 us -> 0.01 us  [on_device(): lax.all_to_all(parcel, 'dp', split_axis=0, concat_axis=0, tiled=True)]
    ppermute x36 -> x43, waiting for transfers between devices: 77.9 us -> 62.5 us  [_swap(): lax.ppermute(values, axis, [(i, i ^ bit) for i in range(lax.axis_size(axi...]
    ppermute x36 -> x43, starting transfers between devices: 30.3 us -> 41 us  [_swap(): lax.ppermute(values, axis, [(i, i ^ bit) for i in range(lax.axis_size(axi...]
    unnamed x60 -> x68, local copies, waits for them, and re-layouts: 9.74 us -> 16.3 us
    pallas_call x1 -> x2, Pallas kernels: 1.59 us -> 5.73 us  [the longest x1 4.1 us: _error(): pl.pallas_call(_error_kernel, in_specs=[pl.BlockSpec(memory_space=pltpu.S...]
    all_to_all x0 -> x1, starting transfers between devices: none -> 3.94 us  [on_device(): lax.all_to_all(clip_weight.reshape(n_dp, TILE_DEV // n_dp), 'dp', split_a...]
    pallas_call x1, Pallas kernels: 8.59 us -> 6.42 us  [_residual(): pl.pallas_call(_residual_kernel, in_specs=[pl.BlockSpec(memory_space=pltp...]
  transfers between devices with their start and end apart: 37 -> 45, of which waited for: 20 -> 18; matrix products, arithmetic and copies ran while one was open for 4% -> 5% of each run, Pallas kernels for 16% -> 24%
where the time goes in v3:
time: 192 us; the launch traced here: 191 us
  waiting for transfers between devices  62.5 us (33%)
  Pallas kernels  50.8 us (26%)
  starting transfers between devices  48.8 us (25%)
  local copies, waits for them, and re-layouts  20.4 us (11%)
  other arithmetic  7.45 us (4%)
    ppermute x43, waiting for transfers between devices, _swap(): lax.ppermute(values, axis, [(i, i ^ bit) for i in range(lax.axis_size(axi...  62.5 us
    ppermute x43, starting transfers between devices, _swap(): lax.ppermute(values, axis, [(i, i ^ bit) for i in range(lax.axis_size(axi...  41 us
    pallas_call x1, Pallas kernels, _forward(): pl.pallas_call(_forward_kernel, in_specs=[pl.BlockSpec(memory_space=pltpu...  16.7 us
    unnamed x68, local copies, waits for them, and re-layouts  16.3 us
    pallas_call x1, Pallas kernels, _residual(): pl.pallas_call(_residual_kernel, in_specs=[pl.BlockSpec(memory_space=pltp...  6.42 us
    pallas_call x1, Pallas kernels, _teacher_act(): pl.pallas_call(_teacher_act_kernel, grid=(steps,), in_specs=[pl.BlockSpec...  6.36 us
    pallas_call x1, Pallas kernels, _teacher_far(): pl.pallas_call(_teacher_far_kernel, in_specs=[pl.BlockSpec(memory_space=p...  6.04 us
    pallas_call x1, Pallas kernels, _error(): pl.pallas_call(_error_kernel, in_specs=[pl.BlockSpec(memory_space=pltpu.S...  4.1 us
  transfers between devices with their start and end apart: 45, of which 18 were waited for; matrix products, arithmetic and copies ran while one was open for 5% of the time, Pallas kernels for 24%

profile of v3, /device:TPU:0, one launch (start us, length us, event | category | flops | bytes accessed | tf_op | source)
XLA Modules:
  0.0 191.0 jit_solution(4477492042427363465)
XLA Ops:
  1.4 3.0 %pack_kernels.1 = (bf16[768,128]{1,0:T(8,128)(2,1)}, bf16[1024,128]{1,0:T(8,128)(2,1)}, bf16[1024,128]{1,0:T(8,128)(2,1)}) custom-call(s32[5]{0:T(128)} %stack.107.place, bf16[448,256]{1,0:T(8,128)(2,1)} %near_dilated.1, bf16[64,256]{1,0:T(8,128)(2,1)} %near_mix.1, bf16[1024,512]{1,0:T(8,128)(2,1)} %near_down.1, bf16[128,1024]{1,0:T(8,128)(2,1)} %near_proj.1, ...), custom_call_target="tpu_custom_call" | custom-call | flops 1000 | bytes 1000 | tf_op jit(solution)/shard_map/pack_kernels/pallas_call | solution.py:155
  4.3 3.1 %collective-permute-start = (bf16[768,128]{1,0:T(8,128)(2,1)}, bf16[768,128]{1,0:T(8,128)(2,1)S(1)}, u32[]{:S(2)}, u32[]{:S(2)}) collective-permute-start(bf16[768,128]{1,0:T(8,128)(2,1)} %get-tuple-element.61), channel_id=1, source_target_pairs={{0,1},{1,0},{2,3},{3,2},{4,5},{5,4},{6,7},{7,6},{8,9},{9,8},{10,11... | collective-permute-start | bytes 589832 | tf_op jit(solution)/shard_map/ppermute | solution.py:563
  7.4 2.6 %collective-permute-start.1 = (bf16[768,128]{1,0:T(8,128)(2,1)}, bf16[768,128]{1,0:T(8,128)(2,1)S(1)}, u32[]{:S(2)}, u32[]{:S(2)}) collective-permute-start(bf16[768,128]{1,0:T(8,128)(2,1)} %get-tuple-element.61), channel_id=1, source_target_pairs={{0,2},{1,3},{2,0},{3,1},{4,6},{5,7},{6,4},{7,5},{8,10},{9,11},{10,... | collective-permute-start | bytes 589832 | tf_op jit(solution)/shard_map/ppermute | solution.py:563
  10.7 3.9 %all-to-all-start = ((f32[8,1,16]{2,1,0:T(1,128)}), f32[8,1,16]{2,1,0:T(1,128)S(1)}, u32[]{:S(2)}, u32[]{:S(2)}) async-start(f32[8,1,16]{2,1,0:T(1,128)} %bitcast.10), calls=%async_computation | async-start | bytes 8192 | tf_op jit(solution)/shard_map/all_to_all | solution.py:604
  14.7 6.4 %teacher_act.1 = (bf16[2,16,128,128]{3,2,1,0:T(8,128)(2,1)S(1)}, bf16[2,16,128,128]{3,2,1,0:T(8,128)(2,1)}) custom-call(s32[5]{0:T(128)S(1)} %copy-done.20, bf16[2048,512]{1,0:T(8,128)(2,1)S(1)} %bitcast.109, f32[1,512]{1,0:T(1,128)S(1)} %bitcast.110), custom_call_target="tpu_custom_call" | custom-call | flops 1000 | bytes 1000 | tf_op jit(solution)/shard_map/teacher_act/pallas_call | solution.py:112
  24.9 1.6 collective-permute-start.4
  26.6 1.6 collective-permute-start.3
  28.1 4.4 %collective-permute-start.5 = (bf16[1024,128]{1,0:T(8,128)(2,1)S(1)}, bf16[1024,128]{1,0:T(8,128)(2,1)S(1)}, u32[]{:S(2)}, u32[]{:S(2)}) collective-permute-start(bf16[1024,128]{1,0:T(8,128)(2,1)S(1)} %copy-done.33), channel_id=1, source_target_pairs={{0,2},{1,3},{2,0},{3,1},{4,6},{5,7},{6,4},{7,5},{8,10},{9,11},{10,... | collective-permute-start | bytes 786440 | tf_op jit(solution)/shard_map/ppermute | solution.py:563
  34.6 8.1 %collective-permute-done.5 = bf16[1024,128]{1,0:T(8,128)(2,1)S(1)} collective-permute-done((bf16[1024,128]{1,0:T(8,128)(2,1)S(1)}, bf16[1024,128]{1,0:T(8,128)(2,1)S(1)}, u32[]{:S(2)}, u32[]{:S(2)}) %collective-permute-start.5) | collective-permute-done | bytes 262176 | tf_op jit(solution)/shard_map/ppermute | solution.py:563
  44.3 12.2 %collective-permute-done.12 = bf16[1024,128]{1,0:T(8,128)(2,1)S(1)} collective-permute-done((bf16[1024,128]{1,0:T(8,128)(2,1)S(1)}, bf16[1024,128]{1,0:T(8,128)(2,1)S(1)}, u32[]{:S(2)}, u32[]{:S(2)}) %collective-permute-start.12) | collective-permute-done | bytes 262176 | tf_op jit(solution)/shard_map/ppermute | solution.py:563
  57.1 1.5 collective-permute-start.14
  59.7 5.1 %collective-permute-done.14 = bf16[1024,128]{1,0:T(8,128)(2,1)S(1)} collective-permute-done((bf16[1024,128]{1,0:T(8,128)(2,1)S(1)}, bf16[1024,128]{1,0:T(8,128)(2,1)S(1)}, u32[]{:S(2)}, u32[]{:S(2)}) %collective-permute-start.14) | collective-permute-done | bytes 262176 | tf_op jit(solution)/shard_map/ppermute | solution.py:563
  73.4 16.7 %student_forward.1 = (bf16[16,128,256]{2,1,0:T(8,128)(2,1)}, bf16[16,128,256]{2,1,0:T(8,128)(2,1)}, bf16[16,128,256]{2,1,0:T(8,128)(2,1)}, f32[16,128,256]{2,1,0...) custom-call(s32[5]{0:T(128)S(1)} %copy-done.20, ...), custom_call_target="tpu_custom_call" | custom-call | flops 1000 | bytes 1000 | tf_op jit(solution)/shard_map/student_forward/pallas_call | solution.py:354
  92.8 3.8 %all-to-all-start.1 = ((bf16[8,640,256]{2,1,0:T(8,128)(2,1)}), bf16[8,640,256]{2,1,0:T(8,128)(2,1)S(1)}, u32[]{:S(2)}, u32[]{:S(2)}) async-start(bf16[8,640,256]{2,1,0:T(8,128)(2,1)} %get-tuple-element.81), calls=%async_computation.1 | async-start | bytes 5242880 | tf_op jit(solution)/shard_map/all_to_all | solution.py:637
  99.1 4.0 %teacher_near.1.near = f32[512,1024]{1,0:T(8,128)S(1)} custom-call(bf16[2,16,128,128]{3,2,1,0:T(8,128)(2,1)S(1)} %copy-done.2, bf16[2,16,128,128]{3,2,1,0:T(8,128)(2,1)S(1)} %copy-done.4, bf16[2048,1024]{1,0:T(8,128)(2,1)} %bitcast.112), custom_call_target="tpu_custom_call" | custom-call | flops 1000 | bytes 1000 | tf_op jit(solution)/shard_map/teacher_near/pallas_call | solution.py:197
  104.5 6.0 %teacher_far.1 = (f32[256,1024]{1,0:T(8,128)S(1)}, bf16[256,1024]{1,0:T(8,128)(2,1)}) custom-call(s32[5]{0:T(128)S(1)} %copy-done.20, f32[512,1024]{1,0:T(8,128)} %copy-done, bf16[2,16,128,128]{3,2,1,0:T(8,128)(2,1)} %copy-done.1, bf16[2,16,128,128]{3,2,1,0:T(8,128)(2,1)} %copy-done.3, bf16[2,1024,128]{2,1,0:T(8,128)(2,1)} %pad_maximum_fusion.2.refs_0_, ...), custom_call_target="tpu_custom_call" | custom-call | flops 1000 | bytes 1000 | tf_op jit(solution)/shard_map/teacher_far/pallas_call | solution.py:235
  111.5 1.7 collective-permute-start.22
  113.9 11.9 %collective-permute-done.22.target_other = bf16[256,1024]{1,0:T(8,128)(2,1)} collective-permute-done((bf16[256,1024]{1,0:T(8,128)(2,1)}, bf16[256,1024]{1,0:T(8,128)(2,1)}, u32[]{:S(2)}, u32[]{:S(2)}) %collective-permute-start.22) | collective-permute-done | bytes 524320 | tf_op jit(solution)/shard_map/ppermute | solution.py:563
  125.9 4.1 %error_backward.1 = (bf16[2,128,512]{2,1,0:T(8,128)(2,1)}, bf16[16,64,256]{2,1,0:T(8,128)(2,1)}, f32[16,64,256]{2,1,0:T(8,128)}) custom-call(s32[5]{0:T(128)} %stack.107.place, f32[256,1024]{1,0:T(8,128)} %copy-done.10, bf16[256,1024]{1,0:T(8,128)(2,1)} %collective-permute-done.22.target_other, f32[256,1024]{1,0:T(8,128)} %get-tuple-element.92.predicted, ...), custom_call_target="tpu_custom_call" | custom-call | flops 1000 | bytes 1000 | tf_op jit(solution)/shard_map/error_backward/pallas_call | solution.py:413
  130.0 1.6 copy-done.6
  135.0 6.4 %residual_backward.1 = (bf16[16,64,256]{2,1,0:T(8,128)(2,1)S(1)}, f32[16,64,256]{2,1,0:T(8,128)S(1)}) custom-call(s32[5]{0:T(128)S(1)} %copy-done.21, bf16[2,128,512]{2,1,0:T(8,128)(2,1)S(1)} %copy-done.8, bf16[4,4096,128]{2,1,0:T(8,128)(2,1)} %get-tuple-element.102.down, bf16[2,256,128]{2,1,0:T(8,128)(2,1)S(1)} %get-tuple-element.103.mix, ...), custom_call_target="tpu_custom_call" | custom-call | flops 1000 | bytes 1000 | tf_op jit(solution)/shard_map/residual_backward/pallas_call | solution.py:544
  143.5 1.7 collective-permute-start.35
  147.8 4.2 %collective-permute-done.35 = bf16[2,4,64,256]{3,2,1,0:T(8,128)(2,1)S(1)} collective-permute-done((bf16[2,4,64,256]{3,2,1,0:T(8,128)(2,1)S(1)}, bf16[2,4,64,256]{3,2,1,0:T(8,128)(2,1)S(1)}, u32[]{:S(2)}, u32[]{:S(2)}) %collective-permute-start.35) | collective-permute-done | bytes 262176 | tf_op jit(solution)/shard_map/ppermute | solution.py:563
  152.7 1.7 collective-permute-start.36
  154.4 1.6 collective-permute-start.25
  157.9 2.3 %collective-permute-done.25 = bf16[128,512]{1,0:T(8,128)(2,1)S(1)} collective-permute-done((bf16[128,512]{1,0:T(8,128)(2,1)S(1)}, bf16[128,512]{1,0:T(8,128)(2,1)S(1)}, u32[]{:S(2)}, u32[]{:S(2)}) %collective-permute-start.25) | collective-permute-done | bytes 131104 | tf_op jit(solution)/shard_map/ppermute | solution.py:563
  168.8 1.7 collective-permute-start.40
  170.9 2.5 %collective-permute-start.42 = (bf16[128,256]{1,0:T(8,128)(2,1)}, bf16[128,256]{1,0:T(8,128)(2,1)}, u32[]{:S(2)}, u32[]{:S(2)}) collective-permute-start(bf16[128,256]{1,0:T(8,128)(2,1)} %get-tuple-element.121), channel_id=1, source_target_pairs={{0,3},{1,2},{2,1},{3,0},{4,7},{5,6},{6,5},{7,4},{8,11},{9,10},{10,... | collective-permute-start | bytes 196616 | tf_op jit(solution)/shard_map/ppermute | solution.py:563
  173.3 2.6 %down_gradient.1 = (f32[128,512]{1,0:T(8,128)S(1)}, bf16[128,512]{1,0:T(8,128)(2,1)}, bf16[128,512]{1,0:T(8,128)(2,1)}, bf16[128,512]{1,0:T(8,128)(2,1)}) custom-call(s32[5]{0:T(128)S(1)} %copy-done.21, bf16[8,640,256]{2,1,0:T(8,128)(2,1)S(1)} %all-to-all-done.1.parcels, bf16[2,128,512]{2,1,0:T(8,128)(2,1)S(1)} %pad_maximum_fusion.6.refs_0_, ...), custom_call_target="tpu_custom_call" | custom-call | flops 1000 | bytes 1000 | tf_op jit(solution)/shard_map/down_gradient/pallas_call | solution.py:450
  177.9 2.5 %collective-permute-start.39 = (bf16[128,512]{1,0:T(8,128)(2,1)}, bf16[128,512]{1,0:T(8,128)(2,1)S(1)}, u32[]{:S(2)}, u32[]{:S(2)}) collective-permute-start(bf16[128,512]{1,0:T(8,128)(2,1)} %get-tuple-element.112), channel_id=1, source_target_pairs={{0,3},{1,2},{2,1},{3,0},{4,7},{5,6},{6,5},{7,4},{8,11},{9,10},{10,... | collective-permute-start | bytes 393224 | tf_op jit(solution)/shard_map/ppermute | solution.py:563
  182.7 6.7 %collective-permute-done.38.refs_1_ = bf16[128,512]{1,0:T(8,128)(2,1)S(1)} collective-permute-done((bf16[128,512]{1,0:T(8,128)(2,1)}, bf16[128,512]{1,0:T(8,128)(2,1)S(1)}, u32[]{:S(2)}, u32[]{:S(2)}) %collective-permute-start.38) | collective-permute-done | bytes 131104 | tf_op jit(solution)/shard_map/ppermute | solution.py:563
  189.4 1.6 finish_gradients.1
  (167 shorter events, 51.5 us)
Async XLA Ops:
  4.3 19.0 %collective-permute-start = (bf16[768,128]{1,0:T(8,128)(2,1)}, bf16[768,128]{1,0:T(8,128)(2,1)S(1)}, u32[]{:S(2)}, u32[]{:S(2)}) collective-permute-start(bf16[768,128]{1,0:T(8,128)(2,1)} %get-tuple-element.61), channel_id=1, source_target_pairs={{0,1},{1,0},{2,3},{3,2},{4,5},{5,4},{6,7},{7,6},{8,9},{9,8},{10,11... | collective-permute-start | bytes 589832 | tf_op jit(solution)/shard_map/ppermute | solution.py:563
  7.4 17.4 %collective-permute-start.1 = (bf16[768,128]{1,0:T(8,128)(2,1)}, bf16[768,128]{1,0:T(8,128)(2,1)S(1)}, u32[]{:S(2)}, u32[]{:S(2)}) collective-permute-start(bf16[768,128]{1,0:T(8,128)(2,1)} %get-tuple-element.61), channel_id=1, source_target_pairs={{0,2},{1,3},{2,0},{3,1},{4,6},{5,7},{6,4},{7,5},{8,10},{9,11},{10,... | collective-permute-start | bytes 589832 | tf_op jit(solution)/shard_map/ppermute | solution.py:563
  10.0 14.8 %collective-permute-start.2 = (bf16[768,128]{1,0:T(8,128)(2,1)}, bf16[768,128]{1,0:T(8,128)(2,1)S(1)}, u32[]{:S(2)}, u32[]{:S(2)}) collective-permute-start(bf16[768,128]{1,0:T(8,128)(2,1)} %get-tuple-element.61), channel_id=1, source_target_pairs={{0,3},{1,2},{2,1},{3,0},{4,7},{5,6},{6,5},{7,4},{8,11},{9,10},{10,... | collective-permute-start | bytes 589832 | tf_op jit(solution)/shard_map/ppermute | solution.py:563
  10.7 11.3 %all-to-all-start = ((f32[8,1,16]{2,1,0:T(1,128)}), f32[8,1,16]{2,1,0:T(1,128)S(1)}, u32[]{:S(2)}, u32[]{:S(2)}) async-start(f32[8,1,16]{2,1,0:T(1,128)} %bitcast.10), calls=%async_computation | async-start | bytes 8192 | tf_op jit(solution)/shard_map/all_to_all | solution.py:604
  24.9 8.1 %collective-permute-start.4 = (bf16[3,384,128]{2,1,0:T(8,128)(2,1)S(1)}, bf16[3,384,128]{2,1,0:T(8,128)(2,1)S(1)}, u32[]{:S(2)}, u32[]{:S(2)}) collective-permute-start(bf16[3,384,128]{2,1,0:T(8,128)(2,1)S(1)} %get-tuple-element.125), channel_id=1, source_target_pairs={{0,16},{4,20},{8,24},{12,28},{16,0},{20,4},{24,8},{28,12},{1,17},{... | collective-permute-start | bytes 884744 | tf_op jit(solution)/shard_map/ppermute | solution.py:563
  26.6 8.0 %collective-permute-start.3 = (bf16[3,384,128]{2,1,0:T(8,128)(2,1)S(1)}, bf16[3,384,128]{2,1,0:T(8,128)(2,1)S(1)}, u32[]{:S(2)}, u32[]{:S(2)}) collective-permute-start(bf16[3,384,128]{2,1,0:T(8,128)(2,1)S(1)} %get-tuple-element.127), channel_id=1, source_target_pairs={{0,8},{4,12},{8,0},{12,4},{16,24},{20,28},{24,16},{28,20},{1,9},{5... | collective-permute-start | bytes 884744 | tf_op jit(solution)/shard_map/ppermute | solution.py:563
  28.1 14.6 %collective-permute-start.5 = (bf16[1024,128]{1,0:T(8,128)(2,1)S(1)}, bf16[1024,128]{1,0:T(8,128)(2,1)S(1)}, u32[]{:S(2)}, u32[]{:S(2)}) collective-permute-start(bf16[1024,128]{1,0:T(8,128)(2,1)S(1)} %copy-done.33), channel_id=1, source_target_pairs={{0,2},{1,3},{2,0},{3,1},{4,6},{5,7},{6,4},{7,5},{8,10},{9,11},{10,... | collective-permute-start | bytes 786440 | tf_op jit(solution)/shard_map/ppermute | solution.py:563
  42.7 14.2 %collective-permute-start.6 = (bf16[2,3,384,128]{3,2,1,0:T(8,128)(2,1)S(1)}, bf16[2,3,384,128]{3,2,1,0:T(8,128)(2,1)}, u32[]{:S(2)}, u32[]{:S(2)}) collective-permute-start(bf16[2,3,384,128]{3,2,1,0:T(8,128)(2,1)S(1)} %pad_maximum_fusion.own_a), channel_id=1, source_target_pairs={{0,16},{4,20},{8,24},{12,28},{16,0},{20,4},{24,8},{28,12},{1,17},{... | collective-permute-start | bytes 1769480 | tf_op jit(solution)/shard_map/ppermute | solution.py:563
  43.2 13.9 %collective-permute-start.7 = (bf16[2,3,384,128]{3,2,1,0:T(8,128)(2,1)S(1)}, bf16[2,3,384,128]{3,2,1,0:T(8,128)(2,1)}, u32[]{:S(2)}, u32[]{:S(2)}) collective-permute-start(bf16[2,3,384,128]{3,2,1,0:T(8,128)(2,1)S(1)} %pad_maximum_fusion.1.own_c), channel_id=1, source_target_pairs={{0,8},{4,12},{8,0},{12,4},{16,24},{20,28},{24,16},{28,20},{1,9},{5... | collective-permute-start | bytes 1769480 | tf_op jit(solution)/shard_map/ppermute | solution.py:563
  43.8 12.7 %collective-permute-start.12 = (bf16[1024,128]{1,0:T(8,128)(2,1)S(1)}, bf16[1024,128]{1,0:T(8,128)(2,1)S(1)}, u32[]{:S(2)}, u32[]{:S(2)}) collective-permute-start(bf16[1024,128]{1,0:T(8,128)(2,1)S(1)} %copy-done.32), channel_id=1, source_target_pairs={{0,2},{1,3},{2,0},{3,1},{4,6},{5,7},{6,4},{7,5},{8,10},{9,11},{10,... | collective-permute-start | bytes 786440 | tf_op jit(solution)/shard_map/ppermute | solution.py:563
  43.8 23.3 %collective-permute-start.10 = (bf16[2,3,384,128]{3,2,1,0:T(8,128)(2,1)S(1)}, bf16[2,3,384,128]{3,2,1,0:T(8,128)(2,1)S(1)}, u32[]{:S(2)}, u32[]{:S(2)}) collective-permute-start(bf16[2,3,384,128]{3,2,1,0:T(8,128)(2,1)S(1)} %pad_maximum_fusion.1.own_c), channel_id=1, source_target_pairs={{0,4},{4,0},{8,12},{12,8},{16,20},{20,16},{24,28},{28,24},{1,5},{5... | collective-permute-start | bytes 1769480 | tf_op jit(solution)/shard_map/ppermute | solution.py:563
  43.8 25.5 %collective-permute-start.8 = (bf16[2,3,384,128]{3,2,1,0:T(8,128)(2,1)S(1)}, bf16[2,3,384,128]{3,2,1,0:T(8,128)(2,1)S(1)}, u32[]{:S(2)}, u32[]{:S(2)}) collective-permute-start(bf16[2,3,384,128]{3,2,1,0:T(8,128)(2,1)S(1)} %pad_maximum_fusion.own_a), channel_id=1, source_target_pairs={{0,4},{4,0},{8,12},{12,8},{16,20},{20,16},{24,28},{28,24},{1,5},{5... | collective-permute-start | bytes 1769480 | tf_op jit(solution)/shard_map/ppermute | solution.py:563
  56.4 34.3 %collective-permute-start.15 = (bf16[2,16,128,128]{3,2,1,0:T(8,128)(2,1)}, bf16[2,16,128,128]{3,2,1,0:T(8,128)(2,1)S(1)}, u32[]{:S(2)}, u32[]{:S(2)}) collective-permute-start(bf16[2,16,128,128]{3,2,1,0:T(8,128)(2,1)} %get-tuple-element.83), channel_id=1, source_target_pairs={{0,1},{1,0},{2,3},{3,2},{4,5},{5,4},{6,7},{7,6},{8,9},{9,8},{10,11... | collective-permute-start | bytes 3145736 | tf_op jit(solution)/shard_map/ppermute | solution.py:563
  57.1 7.6 %collective-permute-start.14 = (bf16[1024,128]{1,0:T(8,128)(2,1)S(1)}, bf16[1024,128]{1,0:T(8,128)(2,1)S(1)}, u32[]{:S(2)}, u32[]{:S(2)}) collective-permute-start(bf16[1024,128]{1,0:T(8,128)(2,1)S(1)} %collective-permute-done.12), channel_id=1, source_target_pairs={{0,16},{4,20},{8,24},{12,28},{16,0},{20,4},{24,8},{28,12},{1,17},{... | collective-permute-start | bytes 786440 | tf_op jit(solution)/shard_map/ppermute | solution.py:563
  58.6 7.5 %collective-permute-start.13 = (bf16[1024,128]{1,0:T(8,128)(2,1)S(1)}, bf16[1024,128]{1,0:T(8,128)(2,1)S(1)}, u32[]{:S(2)}, u32[]{:S(2)}) collective-permute-start(bf16[1024,128]{1,0:T(8,128)(2,1)S(1)} %collective-permute-done.5), channel_id=1, source_target_pairs={{0,8},{4,12},{8,0},{12,4},{16,24},{20,28},{24,16},{28,20},{1,9},{5... | collective-permute-start | bytes 786440 | tf_op jit(solution)/shard_map/ppermute | solution.py:563
  67.9 23.9 %collective-permute-start.17 = (bf16[2,1024,128]{2,1,0:T(8,128)(2,1)S(1)}, bf16[2,1024,128]{2,1,0:T(8,128)(2,1)}, u32[]{:S(2)}, u32[]{:S(2)}) collective-permute-start(bf16[2,1024,128]{2,1,0:T(8,128)(2,1)S(1)} %pad_maximum_fusion.3.refs_2_), channel_id=1, source_target_pairs={{0,8},{4,12},{8,0},{12,4},{16,24},{20,28},{24,16},{28,20},{1,9},{5... | collective-permute-start | bytes 1572872 | tf_op jit(solution)/shard_map/ppermute | solution.py:563
  70.1 21.7 %collective-permute-start.16 = (bf16[2,1024,128]{2,1,0:T(8,128)(2,1)}, bf16[2,1024,128]{2,1,0:T(8,128)(2,1)}, u32[]{:S(2)}, u32[]{:S(2)}) collective-permute-start(bf16[2,1024,128]{2,1,0:T(8,128)(2,1)} %pad_maximum_fusion.2.refs_0_), channel_id=1, source_target_pairs={{0,16},{4,20},{8,24},{12,28},{16,0},{20,4},{24,8},{28,12},{1,17},{... | collective-permute-start | bytes 1572872 | tf_op jit(solution)/shard_map/ppermute | solution.py:563
  91.8 12.6 %collective-permute-start.18 = (bf16[2,1024,128]{2,1,0:T(8,128)(2,1)}, bf16[2,1024,128]{2,1,0:T(8,128)(2,1)}, u32[]{:S(2)}, u32[]{:S(2)}) collective-permute-start(bf16[2,1024,128]{2,1,0:T(8,128)(2,1)} %pad_maximum_fusion.2.refs_0_), channel_id=1, source_target_pairs={{0,4},{4,0},{8,12},{12,8},{16,20},{20,16},{24,28},{28,24},{1,5},{5... | collective-permute-start | bytes 1572872 | tf_op jit(solution)/shard_map/ppermute | solution.py:563
  91.8 12.6 %collective-permute-start.19 = (bf16[2,1024,128]{2,1,0:T(8,128)(2,1)}, bf16[2,1024,128]{2,1,0:T(8,128)(2,1)}, u32[]{:S(2)}, u32[]{:S(2)}) collective-permute-start(bf16[2,1024,128]{2,1,0:T(8,128)(2,1)} %collective-permute-done.16.refs_1_), channel_id=1, source_target_pairs={{0,4},{4,0},{8,12},{12,8},{16,20},{20,16},{24,28},{28,24},{1,5},{5... | collective-permute-start | bytes 1572872 | tf_op jit(solution)/shard_map/ppermute | solution.py:563
  92.3 12.1 %collective-permute-start.20 = (bf16[2,1024,128]{2,1,0:T(8,128)(2,1)S(1)}, bf16[2,1024,128]{2,1,0:T(8,128)(2,1)}, u32[]{:S(2)}, u32[]{:S(2)}) collective-permute-start(bf16[2,1024,128]{2,1,0:T(8,128)(2,1)S(1)} %pad_maximum_fusion.3.refs_2_), channel_id=1, source_target_pairs={{0,4},{4,0},{8,12},{12,8},{16,20},{20,16},{24,28},{28,24},{1,5},{5... | collective-permute-start | bytes 1572872 | tf_op jit(solution)/shard_map/ppermute | solution.py:563
  92.4 12.1 %collective-permute-start.21 = (bf16[2,1024,128]{2,1,0:T(8,128)(2,1)}, bf16[2,1024,128]{2,1,0:T(8,128)(2,1)}, u32[]{:S(2)}, u32[]{:S(2)}) collective-permute-start(bf16[2,1024,128]{2,1,0:T(8,128)(2,1)} %collective-permute-done.17.refs_3_), channel_id=1, source_target_pairs={{0,4},{4,0},{8,12},{12,8},{16,20},{20,16},{24,28},{28,24},{1,5},{5... | collective-permute-start | bytes 1572872 | tf_op jit(solution)/shard_map/ppermute | solution.py:563
  92.8 61.5 %all-to-all-start.1 = ((bf16[8,640,256]{2,1,0:T(8,128)(2,1)}), bf16[8,640,256]{2,1,0:T(8,128)(2,1)S(1)}, u32[]{:S(2)}, u32[]{:S(2)}) async-start(bf16[8,640,256]{2,1,0:T(8,128)(2,1)} %get-tuple-element.81), calls=%async_computation.1 | async-start | bytes 5242880 | tf_op jit(solution)/shard_map/all_to_all | solution.py:637
  111.5 14.4 %collective-permute-start.22 = (bf16[256,1024]{1,0:T(8,128)(2,1)}, bf16[256,1024]{1,0:T(8,128)(2,1)}, u32[]{:S(2)}, u32[]{:S(2)}) collective-permute-start(bf16[256,1024]{1,0:T(8,128)(2,1)} %get-tuple-element.91), channel_id=1, source_target_pairs={{0,1},{1,0},{2,3},{3,2},{4,5},{5,4},{6,7},{7,6},{8,9},{9,8},{10,11... | collective-permute-start | bytes 1572872 | tf_op jit(solution)/shard_map/ppermute | solution.py:563
  143.5 8.4 %collective-permute-start.35 = (bf16[2,4,64,256]{3,2,1,0:T(8,128)(2,1)S(1)}, bf16[2,4,64,256]{3,2,1,0:T(8,128)(2,1)S(1)}, u32[]{:S(2)}, u32[]{:S(2)}) collective-permute-start(bf16[2,4,64,256]{3,2,1,0:T(8,128)(2,1)S(1)} %bitcast.117), channel_id=1, source_target_pairs={{0,16},{4,20},{8,24},{12,28},{16,0},{20,4},{24,8},{28,12},{1,17},{... | collective-permute-start | bytes 786440 | tf_op jit(solution)/shard_map/ppermute | solution.py:563
  146.3 10.2 %collective-permute-start.32 = (bf16[2,4,64,256]{3,2,1,0:T(8,128)(2,1)}, bf16[2,4,64,256]{3,2,1,0:T(8,128)(2,1)}, u32[]{:S(2)}, u32[]{:S(2)}) collective-permute-start(bf16[2,4,64,256]{3,2,1,0:T(8,128)(2,1)} %bitcast.37), channel_id=1, source_target_pairs={{0,8},{4,12},{8,0},{12,4},{16,24},{20,28},{24,16},{28,20},{1,9},{5... | collective-permute-start | bytes 786440 | tf_op jit(solution)/shard_map/ppermute | solution.py:563
  152.7 10.0 %collective-permute-start.36 = (bf16[4,64,256]{2,1,0:T(8,128)(2,1)}, bf16[4,64,256]{2,1,0:T(8,128)(2,1)}, u32[]{:S(2)}, u32[]{:S(2)}) collective-permute-start(bf16[4,64,256]{2,1,0:T(8,128)(2,1)} %fusion.11), channel_id=1, source_target_pairs={{0,8},{4,12},{8,0},{12,4},{16,24},{20,28},{24,16},{28,20},{1,9},{5... | collective-permute-start | bytes 393224 | tf_op jit(solution)/shard_map/ppermute | solution.py:563
  168.8 9.0 %collective-permute-start.40 = (bf16[128,256]{1,0:T(8,128)(2,1)S(1)}, bf16[128,256]{1,0:T(8,128)(2,1)S(1)}, u32[]{:S(2)}, u32[]{:S(2)}) collective-permute-start(bf16[128,256]{1,0:T(8,128)(2,1)S(1)} %get-tuple-element.123), channel_id=1, source_target_pairs={{0,1},{1,0},{2,3},{3,2},{4,5},{5,4},{6,7},{7,6},{8,9},{9,8},{10,11... | collective-permute-start | bytes 196616 | tf_op jit(solution)/shard_map/ppermute | solution.py:563
  170.5 11.0 %collective-permute-start.41 = (bf16[128,256]{1,0:T(8,128)(2,1)}, bf16[128,256]{1,0:T(8,128)(2,1)S(1)}, u32[]{:S(2)}, u32[]{:S(2)}) collective-permute-start(bf16[128,256]{1,0:T(8,128)(2,1)} %get-tuple-element.122), channel_id=1, source_target_pairs={{0,2},{1,3},{2,0},{3,1},{4,6},{5,7},{6,4},{7,5},{8,10},{9,11},{10,... | collective-permute-start | bytes 196616 | tf_op jit(solution)/shard_map/ppermute | solution.py:563
  170.9 10.7 %collective-permute-start.42 = (bf16[128,256]{1,0:T(8,128)(2,1)}, bf16[128,256]{1,0:T(8,128)(2,1)}, u32[]{:S(2)}, u32[]{:S(2)}) collective-permute-start(bf16[128,256]{1,0:T(8,128)(2,1)} %get-tuple-element.121), channel_id=1, source_target_pairs={{0,3},{1,2},{2,1},{3,0},{4,7},{5,6},{6,5},{7,4},{8,11},{9,10},{10,... | collective-permute-start | bytes 196616 | tf_op jit(solution)/shard_map/ppermute | solution.py:563
  175.9 6.8 %collective-permute-start.37 = (bf16[128,512]{1,0:T(8,128)(2,1)}, bf16[128,512]{1,0:T(8,128)(2,1)S(1)}, u32[]{:S(2)}, u32[]{:S(2)}) collective-permute-start(bf16[128,512]{1,0:T(8,128)(2,1)} %get-tuple-element.110), channel_id=1, source_target_pairs={{0,1},{1,0},{2,3},{3,2},{4,5},{5,4},{6,7},{7,6},{8,9},{9,8},{10,11... | collective-permute-start | bytes 393224 | tf_op jit(solution)/shard_map/ppermute | solution.py:563
  176.7 12.7 %collective-permute-start.38 = (bf16[128,512]{1,0:T(8,128)(2,1)}, bf16[128,512]{1,0:T(8,128)(2,1)S(1)}, u32[]{:S(2)}, u32[]{:S(2)}) collective-permute-start(bf16[128,512]{1,0:T(8,128)(2,1)} %get-tuple-element.111), channel_id=1, source_target_pairs={{0,2},{1,3},{2,0},{3,1},{4,6},{5,7},{6,4},{7,5},{8,10},{9,11},{10,... | collective-permute-start | bytes 393224 | tf_op jit(solution)/shard_map/ppermute | solution.py:563
  177.9 11.5 %collective-permute-start.39 = (bf16[128,512]{1,0:T(8,128)(2,1)}, bf16[128,512]{1,0:T(8,128)(2,1)S(1)}, u32[]{:S(2)}, u32[]{:S(2)}) collective-permute-start(bf16[128,512]{1,0:T(8,128)(2,1)} %get-tuple-element.112), channel_id=1, source_target_pairs={{0,3},{1,2},{2,1},{3,0},{4,7},{5,6},{6,5},{7,4},{8,11},{9,10},{10,... | collective-permute-start | bytes 393224 | tf_op jit(solution)/shard_map/ppermute | solution.py:563
  (47 other events, 501.4 us)

commit v4 on v3

--- a/solution.py
+++ b/solution.py
@@ -30,6 +30,7 @@
 F32 = jnp.float32
 BF16 = jnp.bfloat16
 VMEM_LIMIT = 48 * 1024 * 1024
+WHOLE_VMEM = 60 * 1024 * 1024
 COST = pl.CostEstimate(flops=1000, bytes_accessed=1000, transcendentals=0)
 
 PACK = {
@@ -198,7 +199,7 @@
         _teacher_near_kernel,
         out_shape=jax.ShapeDtypeStruct((2 * LATENTS, DL), F32),
         name="teacher_near",
-        compiler_params=pltpu.CompilerParams(vmem_limit_bytes=VMEM_LIMIT),
+        compiler_params=pltpu.CompilerParams(vmem_limit_bytes=WHOLE_VMEM),
         cost_estimate=COST,
     )(mine, theirs, kernel)
 
@@ -238,7 +239,7 @@
         out_specs=[whole] * 2,
         out_shape=[jax.ShapeDtypeStruct((LATENTS, DL), F32), jax.ShapeDtypeStruct((LATENTS, DL), BF16)],
         name="teacher_far",
-        compiler_params=pltpu.CompilerParams(vmem_limit_bytes=VMEM_LIMIT),
+        compiler_params=pltpu.CompilerParams(vmem_limit_bytes=WHOLE_VMEM),
         cost_estimate=COST,
     )(place, near, mine, theirs, *own, *other)
 
@@ -377,7 +378,7 @@
             pltpu.VMEM(frames, BF16),
         ],
         name="student_forward",
-        compiler_params=pltpu.CompilerParams(vmem_limit_bytes=VMEM_LIMIT),
+        compiler_params=pltpu.CompilerParams(vmem_limit_bytes=WHOLE_VMEM),
         cost_estimate=COST,
     )(place, tiles.reshape(ROWS, CS), *own, *other, *kernels, alphas, routes)
 
@@ -421,7 +422,7 @@
         ],
         scratch_shapes=[pltpu.VMEM((LATENTS, DL), BF16), pltpu.VMEM((CSO, DL), F32)],
         name="error_backward",
-        compiler_params=pltpu.CompilerParams(vmem_limit_bytes=60 * 1024 * 1024),
+        compiler_params=pltpu.CompilerParams(vmem_limit_bytes=WHOLE_VMEM),
         cost_estimate=COST,
     )(place, *targets, predicted, weights, student, proj)
 
@@ -554,7 +555,7 @@
             pltpu.VMEM((CS, CS), F32),
         ],
         name="residual_backward",
-        compiler_params=pltpu.CompilerParams(vmem_limit_bytes=VMEM_LIMIT),
+        compiler_params=pltpu.CompilerParams(vmem_limit_bytes=WHOLE_VMEM),
         cost_estimate=COST,
     )(place, back_student, down, mix, act_one, act_two, slope_two, slope_three)
 

time: 192 us -> 187 us (0.974)
  local copies, waits for them, and re-layouts: 20.4 us -> 8.25 us
  Pallas kernels: 50.8 us -> 56 us
  other arithmetic: 7.45 us -> 10 us
    unnamed x68 -> x50, local copies, waits for them, and re-layouts: 16.3 us -> 3.61 us
    pallas_call x1, Pallas kernels: 6.42 us -> 8.68 us  [_residual(): pl.pallas_call(_residual_kernel, in_specs=[pl.BlockSpec(memory_space=pltp...]
    pallas_call x1, Pallas kernels: 3.97 us -> 6.01 us  [_teacher_near(): pl.pallas_call(_teacher_near_kernel, out_shape=jax.ShapeDtypeStruct((2 *...]
  transfers between devices with their start and end apart: 45 -> 45, of which waited for: 18 -> 18; matrix products, arithmetic and copies ran while one was open for 5% -> 7% of each run, Pallas kernels for 24% -> 28%
where the time goes in v4:
time: 187 us; the launch traced here: 186 us
  waiting for transfers between devices  61.3 us (33%)
  Pallas kernels  56 us (30%)
  starting transfers between devices  49.9 us (27%)
  other arithmetic  10 us (5%)
  local copies, waits for them, and re-layouts  8.25 us (4%)
    ppermute x43, waiting for transfers between devices, _swap(): lax.ppermute(values, axis, [(i, i ^ bit) for i in range(lax.axis_size(axi...  61.3 us
    ppermute x43, starting transfers between devices, _swap(): lax.ppermute(values, axis, [(i, i ^ bit) for i in range(lax.axis_size(axi...  42.1 us
    pallas_call x1, Pallas kernels, _forward(): pl.pallas_call(_forward_kernel, in_specs=[pl.BlockSpec(memory_space=pltpu...  17.9 us
    pallas_call x1, Pallas kernels, _residual(): pl.pallas_call(_residual_kernel, in_specs=[pl.BlockSpec(memory_space=pltp...  8.68 us
    pallas_call x1, Pallas kernels, _teacher_far(): pl.pallas_call(_teacher_far_kernel, in_specs=[pl.BlockSpec(memory_space=p...  6.52 us
    pallas_call x1, Pallas kernels, _teacher_near(): pl.pallas_call(_teacher_near_kernel, out_shape=jax.ShapeDtypeStruct((2 *...  6.01 us
    pallas_call x1, Pallas kernels, _teacher_act(): pl.pallas_call(_teacher_act_kernel, grid=(steps,), in_specs=[pl.BlockSpec...  5.62 us
    pallas_call x1, Pallas kernels, _error(): pl.pallas_call(_error_kernel, in_specs=[pl.BlockSpec(memory_space=pltpu.S...  4.14 us
  transfers between devices with their start and end apart: 45, of which 18 were waited for; matrix products, arithmetic and copies ran while one was open for 7% of the time, Pallas kernels for 28%

profile of v4, /device:TPU:0, one launch (start us, length us, event | category | flops | bytes accessed | tf_op | source)
XLA Modules:
  0.0 186.5 jit_solution(3874222160419741701)
XLA Ops:
  1.3 3.0 %pack_kernels.1 = (bf16[768,128]{1,0:T(8,128)(2,1)}, bf16[1024,128]{1,0:T(8,128)(2,1)}, bf16[1024,128]{1,0:T(8,128)(2,1)}) custom-call(s32[5]{0:T(128)} %stack.107.place, bf16[448,256]{1,0:T(8,128)(2,1)} %near_dilated.1, bf16[64,256]{1,0:T(8,128)(2,1)} %near_mix.1, bf16[1024,512]{1,0:T(8,128)(2,1)} %near_down.1, bf16[128,1024]{1,0:T(8,128)(2,1)} %near_proj.1, ...), custom_call_target="tpu_custom_call" | custom-call | flops 1000 | bytes 1000 | tf_op jit(solution)/shard_map/pack_kernels/pallas_call | solution.py:156
  4.3 3.1 %collective-permute-start = (bf16[768,128]{1,0:T(8,128)(2,1)}, bf16[768,128]{1,0:T(8,128)(2,1)S(1)}, u32[]{:S(2)}, u32[]{:S(2)}) collective-permute-start(bf16[768,128]{1,0:T(8,128)(2,1)} %get-tuple-element.61), channel_id=1, source_target_pairs={{0,1},{1,0},{2,3},{3,2},{4,5},{5,4},{6,7},{7,6},{8,9},{9,8},{10,11... | collective-permute-start | bytes 589832 | tf_op jit(solution)/shard_map/ppermute | solution.py:564
  7.4 2.6 %collective-permute-start.1 = (bf16[768,128]{1,0:T(8,128)(2,1)}, bf16[768,128]{1,0:T(8,128)(2,1)S(1)}, u32[]{:S(2)}, u32[]{:S(2)}) collective-permute-start(bf16[768,128]{1,0:T(8,128)(2,1)} %get-tuple-element.61), channel_id=1, source_target_pairs={{0,2},{1,3},{2,0},{3,1},{4,6},{5,7},{6,4},{7,5},{8,10},{9,11},{10,... | collective-permute-start | bytes 589832 | tf_op jit(solution)/shard_map/ppermute | solution.py:564
  10.6 3.9 %all-to-all-start = ((f32[8,1,16]{2,1,0:T(1,128)}), f32[8,1,16]{2,1,0:T(1,128)S(1)}, u32[]{:S(2)}, u32[]{:S(2)}) async-start(f32[8,1,16]{2,1,0:T(1,128)} %bitcast.10), calls=%async_computation | async-start | bytes 8192 | tf_op jit(solution)/shard_map/all_to_all | solution.py:605
  14.6 5.6 %teacher_act.1 = (bf16[2,16,128,128]{3,2,1,0:T(8,128)(2,1)S(1)}, bf16[2,16,128,128]{3,2,1,0:T(8,128)(2,1)S(1)}) custom-call(s32[5]{0:T(128)S(1)} %copy-done.2, bf16[2048,512]{1,0:T(8,128)(2,1)S(1)} %bitcast.109, f32[1,512]{1,0:T(1,128)S(1)} %bitcast.110), custom_call_target="tpu_custom_call" | custom-call | flops 1000 | bytes 1000 | tf_op jit(solution)/shard_map/teacher_act/pallas_call | solution.py:113
  24.8 1.6 collective-permute-start.4
  26.5 1.6 collective-permute-start.3
  28.0 4.4 %collective-permute-start.5 = (bf16[1024,128]{1,0:T(8,128)(2,1)}, bf16[1024,128]{1,0:T(8,128)(2,1)S(1)}, u32[]{:S(2)}, u32[]{:S(2)}) collective-permute-start(bf16[1024,128]{1,0:T(8,128)(2,1)} %get-tuple-element.66), channel_id=1, source_target_pairs={{0,2},{1,3},{2,0},{3,1},{4,6},{5,7},{6,4},{7,5},{8,10},{9,11},{10,... | collective-permute-start | bytes 786440 | tf_op jit(solution)/shard_map/ppermute | solution.py:564
  34.8 8.0 %collective-permute-done.5 = bf16[1024,128]{1,0:T(8,128)(2,1)S(1)} collective-permute-done((bf16[1024,128]{1,0:T(8,128)(2,1)}, bf16[1024,128]{1,0:T(8,128)(2,1)S(1)}, u32[]{:S(2)}, u32[]{:S(2)}) %collective-permute-start.5) | collective-permute-done | bytes 262176 | tf_op jit(solution)/shard_map/ppermute | solution.py:564
  44.4 12.5 %collective-permute-done.12 = bf16[1024,128]{1,0:T(8,128)(2,1)S(1)} collective-permute-done((bf16[1024,128]{1,0:T(8,128)(2,1)S(1)}, bf16[1024,128]{1,0:T(8,128)(2,1)S(1)}, u32[]{:S(2)}, u32[]{:S(2)}) %collective-permute-start.12) | collective-permute-done | bytes 262176 | tf_op jit(solution)/shard_map/ppermute | solution.py:564
  60.0 5.0 %collective-permute-done.14 = bf16[1024,128]{1,0:T(8,128)(2,1)S(1)} collective-permute-done((bf16[1024,128]{1,0:T(8,128)(2,1)S(1)}, bf16[1024,128]{1,0:T(8,128)(2,1)S(1)}, u32[]{:S(2)}, u32[]{:S(2)}) %collective-permute-start.14) | collective-permute-done | bytes 262176 | tf_op jit(solution)/shard_map/ppermute | solution.py:564
  68.4 1.7 collective-permute-start.16
  71.5 17.9 %student_forward.1 = (bf16[16,128,256]{2,1,0:T(8,128)(2,1)}, bf16[16,128,256]{2,1,0:T(8,128)(2,1)}, bf16[16,128,256]{2,1,0:T(8,128)(2,1)}, f32[16,128,256]{2,1,0...) custom-call(s32[5]{0:T(128)} %stack.107.place, ...), custom_call_target="tpu_custom_call" | custom-call | flops 1000 | bytes 1000 | tf_op jit(solution)/shard_map/student_forward/pallas_call | solution.py:355
  90.5 3.8 %all-to-all-start.1 = ((bf16[8,640,256]{2,1,0:T(8,128)(2,1)}), bf16[8,640,256]{2,1,0:T(8,128)(2,1)S(1)}, u32[]{:S(2)}, u32[]{:S(2)}) async-start(bf16[8,640,256]{2,1,0:T(8,128)(2,1)} %get-tuple-element.81), calls=%async_computation.1 | async-start | bytes 5242880 | tf_op jit(solution)/shard_map/all_to_all | solution.py:638
  94.3 6.0 %teacher_near.1.near = f32[512,1024]{1,0:T(8,128)} custom-call(bf16[2,16,128,128]{3,2,1,0:T(8,128)(2,1)} %copy-done, bf16[2,16,128,128]{3,2,1,0:T(8,128)(2,1)} %copy-done.7, bf16[2048,1024]{1,0:T(8,128)(2,1)} %bitcast.112), custom_call_target="tpu_custom_call" | custom-call | flops 1000 | bytes 1000 | tf_op jit(solution)/shard_map/teacher_near/pallas_call | solution.py:198
  101.1 6.5 %teacher_far.1 = (f32[256,1024]{1,0:T(8,128)}, bf16[256,1024]{1,0:T(8,128)(2,1)}) custom-call(s32[5]{0:T(128)} %stack.107.place, f32[512,1024]{1,0:T(8,128)} %teacher_near.1.near, bf16[2,16,128,128]{3,2,1,0:T(8,128)(2,1)} %copy-done, bf16[2,16,128,128]{3,2,1,0:T(8,128)(2,1)} %copy-done.7, bf16[2,1024,128]{2,1,0:T(8,128)(2,1)} %pad_maximum_fusion.2.refs_0_, ...), custom_call_target="tpu_custom_call" | custom-call | flops 1000 | bytes 1000 | tf_op jit(solution)/shard_map/teacher_far/pallas_call | solution.py:236
  107.6 1.7 collective-permute-start.22
  110.0 11.9 %collective-permute-done.22.target_other = bf16[256,1024]{1,0:T(8,128)(2,1)S(1)} collective-permute-done((bf16[256,1024]{1,0:T(8,128)(2,1)}, bf16[256,1024]{1,0:T(8,128)(2,1)S(1)}, u32[]{:S(2)}, u32[]{:S(2)}) %collective-permute-start.22) | collective-permute-done | bytes 524320 | tf_op jit(solution)/shard_map/ppermute | solution.py:564
  122.7 4.1 %error_backward.1 = (bf16[2,128,512]{2,1,0:T(8,128)(2,1)}, bf16[16,64,256]{2,1,0:T(8,128)(2,1)}, f32[16,64,256]{2,1,0:T(8,128)}) custom-call(s32[5]{0:T(128)} %stack.107.place, f32[256,1024]{1,0:T(8,128)} %get-tuple-element.90.target_own, bf16[256,1024]{1,0:T(8,128)(2,1)} %copy-done.16, f32[256,1024]{1,0:T(8,128)} %get-tuple-element.92.predicted, ...), custom_call_target="tpu_custom_call" | custom-call | flops 1000 | bytes 1000 | tf_op jit(solution)/shard_map/error_backward/pallas_call | solution.py:414
  126.8 8.7 %residual_backward.1 = (bf16[16,64,256]{2,1,0:T(8,128)(2,1)}, f32[16,64,256]{2,1,0:T(8,128)}) custom-call(s32[5]{0:T(128)} %stack.107.place, bf16[2,128,512]{2,1,0:T(8,128)(2,1)} %get-tuple-element.98.back_student, bf16[4,4096,128]{2,1,0:T(8,128)(2,1)} %get-tuple-element.102.down, bf16[2,256,128]{2,1,0:T(8,128)(2,1)} %get-tuple-element.103.mix, ...), custom_call_target="tpu_custom_call" | custom-call | flops 1000 | bytes 1000 | tf_op jit(solution)/shard_map/residual_backward/pallas_call | solution.py:545
  136.0 1.6 collective-permute-done.34
  139.0 1.8 collective-permute-start.35
  143.2 4.2 %collective-permute-done.35 = bf16[2,4,64,256]{3,2,1,0:T(8,128)(2,1)S(1)} collective-permute-done((bf16[2,4,64,256]{3,2,1,0:T(8,128)(2,1)S(1)}, bf16[2,4,64,256]{3,2,1,0:T(8,128)(2,1)S(1)}, u32[]{:S(2)}, u32[]{:S(2)}) %collective-permute-start.35) | collective-permute-done | bytes 262176 | tf_op jit(solution)/shard_map/ppermute | solution.py:564
  148.2 1.7 collective-permute-start.36
  149.9 1.5 collective-permute-start.25
  153.4 2.2 %collective-permute-done.25 = bf16[128,512]{1,0:T(8,128)(2,1)S(1)} collective-permute-done((bf16[128,512]{1,0:T(8,128)(2,1)S(1)}, bf16[128,512]{1,0:T(8,128)(2,1)S(1)}, u32[]{:S(2)}, u32[]{:S(2)}) %collective-permute-start.25) | collective-permute-done | bytes 131104 | tf_op jit(solution)/shard_map/ppermute | solution.py:564
  164.3 1.7 collective-permute-start.40
  166.6 2.2 %collective-permute-start.42 = (bf16[128,256]{1,0:T(8,128)(2,1)}, bf16[128,256]{1,0:T(8,128)(2,1)}, u32[]{:S(2)}, u32[]{:S(2)}) collective-permute-start(bf16[128,256]{1,0:T(8,128)(2,1)} %get-tuple-element.121), channel_id=1, source_target_pairs={{0,3},{1,2},{2,1},{3,0},{4,7},{5,6},{6,5},{7,4},{8,11},{9,10},{10,... | collective-permute-start | bytes 196616 | tf_op jit(solution)/shard_map/ppermute | solution.py:564
  168.8 2.6 %down_gradient.1 = (f32[128,512]{1,0:T(8,128)S(1)}, bf16[128,512]{1,0:T(8,128)(2,1)}, bf16[128,512]{1,0:T(8,128)(2,1)}, bf16[128,512]{1,0:T(8,128)(2,1)}) custom-call(s32[5]{0:T(128)S(1)} %copy-done.3, bf16[8,640,256]{2,1,0:T(8,128)(2,1)S(1)} %all-to-all-done.1.parcels, bf16[2,128,512]{2,1,0:T(8,128)(2,1)S(1)} %pad_maximum_fusion.6.refs_0_, ...), custom_call_target="tpu_custom_call" | custom-call | flops 1000 | bytes 1000 | tf_op jit(solution)/shard_map/down_gradient/pallas_call | solution.py:451
  173.5 2.2 %collective-permute-start.39 = (bf16[128,512]{1,0:T(8,128)(2,1)}, bf16[128,512]{1,0:T(8,128)(2,1)S(1)}, u32[]{:S(2)}, u32[]{:S(2)}) collective-permute-start(bf16[128,512]{1,0:T(8,128)(2,1)} %get-tuple-element.112), channel_id=1, source_target_pairs={{0,3},{1,2},{2,1},{3,0},{4,7},{5,6},{6,5},{7,4},{8,11},{9,10},{10,... | collective-permute-start | bytes 393224 | tf_op jit(solution)/shard_map/ppermute | solution.py:564
  178.4 6.4 %collective-permute-done.38.refs_1_ = bf16[128,512]{1,0:T(8,128)(2,1)S(1)} collective-permute-done((bf16[128,512]{1,0:T(8,128)(2,1)}, bf16[128,512]{1,0:T(8,128)(2,1)S(1)}, u32[]{:S(2)}, u32[]{:S(2)}) %collective-permute-start.38) | collective-permute-done | bytes 131104 | tf_op jit(solution)/shard_map/ppermute | solution.py:564
  184.8 1.6 finish_gradients.1
  (149 shorter events, 42.2 us)
Async XLA Ops:
  4.3 19.3 %collective-permute-start = (bf16[768,128]{1,0:T(8,128)(2,1)}, bf16[768,128]{1,0:T(8,128)(2,1)S(1)}, u32[]{:S(2)}, u32[]{:S(2)}) collective-permute-start(bf16[768,128]{1,0:T(8,128)(2,1)} %get-tuple-element.61), channel_id=1, source_target_pairs={{0,1},{1,0},{2,3},{3,2},{4,5},{5,4},{6,7},{7,6},{8,9},{9,8},{10,11... | collective-permute-start | bytes 589832 | tf_op jit(solution)/shard_map/ppermute | solution.py:564
  7.4 17.4 %collective-permute-start.1 = (bf16[768,128]{1,0:T(8,128)(2,1)}, bf16[768,128]{1,0:T(8,128)(2,1)S(1)}, u32[]{:S(2)}, u32[]{:S(2)}) collective-permute-start(bf16[768,128]{1,0:T(8,128)(2,1)} %get-tuple-element.61), channel_id=1, source_target_pairs={{0,2},{1,3},{2,0},{3,1},{4,6},{5,7},{6,4},{7,5},{8,10},{9,11},{10,... | collective-permute-start | bytes 589832 | tf_op jit(solution)/shard_map/ppermute | solution.py:564
  9.9 14.8 %collective-permute-start.2 = (bf16[768,128]{1,0:T(8,128)(2,1)}, bf16[768,128]{1,0:T(8,128)(2,1)S(1)}, u32[]{:S(2)}, u32[]{:S(2)}) collective-permute-start(bf16[768,128]{1,0:T(8,128)(2,1)} %get-tuple-element.61), channel_id=1, source_target_pairs={{0,3},{1,2},{2,1},{3,0},{4,7},{5,6},{6,5},{7,4},{8,11},{9,10},{10,... | collective-permute-start | bytes 589832 | tf_op jit(solution)/shard_map/ppermute | solution.py:564
  10.6 11.6 %all-to-all-start = ((f32[8,1,16]{2,1,0:T(1,128)}), f32[8,1,16]{2,1,0:T(1,128)S(1)}, u32[]{:S(2)}, u32[]{:S(2)}) async-start(f32[8,1,16]{2,1,0:T(1,128)} %bitcast.10), calls=%async_computation | async-start | bytes 8192 | tf_op jit(solution)/shard_map/all_to_all | solution.py:605
  24.8 8.4 %collective-permute-start.4 = (bf16[3,384,128]{2,1,0:T(8,128)(2,1)S(1)}, bf16[3,384,128]{2,1,0:T(8,128)(2,1)S(1)}, u32[]{:S(2)}, u32[]{:S(2)}) collective-permute-start(bf16[3,384,128]{2,1,0:T(8,128)(2,1)S(1)} %get-tuple-element.125), channel_id=1, source_target_pairs={{0,16},{4,20},{8,24},{12,28},{16,0},{20,4},{24,8},{28,12},{1,17},{... | collective-permute-start | bytes 884744 | tf_op jit(solution)/shard_map/ppermute | solution.py:564
  26.5 8.2 %collective-permute-start.3 = (bf16[3,384,128]{2,1,0:T(8,128)(2,1)S(1)}, bf16[3,384,128]{2,1,0:T(8,128)(2,1)S(1)}, u32[]{:S(2)}, u32[]{:S(2)}) collective-permute-start(bf16[3,384,128]{2,1,0:T(8,128)(2,1)S(1)} %get-tuple-element.127), channel_id=1, source_target_pairs={{0,8},{4,12},{8,0},{12,4},{16,24},{20,28},{24,16},{28,20},{1,9},{5... | collective-permute-start | bytes 884744 | tf_op jit(solution)/shard_map/ppermute | solution.py:564
  28.0 14.8 %collective-permute-start.5 = (bf16[1024,128]{1,0:T(8,128)(2,1)}, bf16[1024,128]{1,0:T(8,128)(2,1)S(1)}, u32[]{:S(2)}, u32[]{:S(2)}) collective-permute-start(bf16[1024,128]{1,0:T(8,128)(2,1)} %get-tuple-element.66), channel_id=1, source_target_pairs={{0,2},{1,3},{2,0},{3,1},{4,6},{5,7},{6,4},{7,5},{8,10},{9,11},{10,... | collective-permute-start | bytes 786440 | tf_op jit(solution)/shard_map/ppermute | solution.py:564
  42.8 14.2 %collective-permute-start.6 = (bf16[2,3,384,128]{3,2,1,0:T(8,128)(2,1)S(1)}, bf16[2,3,384,128]{3,2,1,0:T(8,128)(2,1)}, u32[]{:S(2)}, u32[]{:S(2)}) collective-permute-start(bf16[2,3,384,128]{3,2,1,0:T(8,128)(2,1)S(1)} %pad_maximum_fusion.own_a), channel_id=1, source_target_pairs={{0,16},{4,20},{8,24},{12,28},{16,0},{20,4},{24,8},{28,12},{1,17},{... | collective-permute-start | bytes 1769480 | tf_op jit(solution)/shard_map/ppermute | solution.py:564
  43.3 13.9 %collective-permute-start.7 = (bf16[2,3,384,128]{3,2,1,0:T(8,128)(2,1)S(1)}, bf16[2,3,384,128]{3,2,1,0:T(8,128)(2,1)}, u32[]{:S(2)}, u32[]{:S(2)}) collective-permute-start(bf16[2,3,384,128]{3,2,1,0:T(8,128)(2,1)S(1)} %pad_maximum_fusion.1.own_c), channel_id=1, source_target_pairs={{0,8},{4,12},{8,0},{12,4},{16,24},{20,28},{24,16},{28,20},{1,9},{5... | collective-permute-start | bytes 1769480 | tf_op jit(solution)/shard_map/ppermute | solution.py:564
  43.9 13.0 %collective-permute-start.12 = (bf16[1024,128]{1,0:T(8,128)(2,1)S(1)}, bf16[1024,128]{1,0:T(8,128)(2,1)S(1)}, u32[]{:S(2)}, u32[]{:S(2)}) collective-permute-start(bf16[1024,128]{1,0:T(8,128)(2,1)S(1)} %copy-done.24), channel_id=1, source_target_pairs={{0,2},{1,3},{2,0},{3,1},{4,6},{5,7},{6,4},{7,5},{8,10},{9,11},{10,... | collective-permute-start | bytes 786440 | tf_op jit(solution)/shard_map/ppermute | solution.py:564
  43.9 23.3 %collective-permute-start.10 = (bf16[2,3,384,128]{3,2,1,0:T(8,128)(2,1)S(1)}, bf16[2,3,384,128]{3,2,1,0:T(8,128)(2,1)S(1)}, u32[]{:S(2)}, u32[]{:S(2)}) collective-permute-start(bf16[2,3,384,128]{3,2,1,0:T(8,128)(2,1)S(1)} %pad_maximum_fusion.1.own_c), channel_id=1, source_target_pairs={{0,4},{4,0},{8,12},{12,8},{16,20},{20,16},{24,28},{28,24},{1,5},{5... | collective-permute-start | bytes 1769480 | tf_op jit(solution)/shard_map/ppermute | solution.py:564
  43.9 24.5 %collective-permute-start.8 = (bf16[2,3,384,128]{3,2,1,0:T(8,128)(2,1)S(1)}, bf16[2,3,384,128]{3,2,1,0:T(8,128)(2,1)S(1)}, u32[]{:S(2)}, u32[]{:S(2)}) collective-permute-start(bf16[2,3,384,128]{3,2,1,0:T(8,128)(2,1)S(1)} %pad_maximum_fusion.own_a), channel_id=1, source_target_pairs={{0,4},{4,0},{8,12},{12,8},{16,20},{20,16},{24,28},{28,24},{1,5},{5... | collective-permute-start | bytes 1769480 | tf_op jit(solution)/shard_map/ppermute | solution.py:564
  56.9 32.4 %collective-permute-start.15 = (bf16[2,16,128,128]{3,2,1,0:T(8,128)(2,1)S(1)}, bf16[2,16,128,128]{3,2,1,0:T(8,128)(2,1)S(1)}, u32[]{:S(2)}, u32[]{:S(2)}) collective-permute-start(bf16[2,16,128,128]{3,2,1,0:T(8,128)(2,1)S(1)} %copy-done.6), channel_id=1, source_target_pairs={{0,1},{1,0},{2,3},{3,2},{4,5},{5,4},{6,7},{7,6},{8,9},{9,8},{10,11... | collective-permute-start | bytes 3145736 | tf_op jit(solution)/shard_map/ppermute | solution.py:564
  57.2 7.8 %collective-permute-start.14 = (bf16[1024,128]{1,0:T(8,128)(2,1)S(1)}, bf16[1024,128]{1,0:T(8,128)(2,1)S(1)}, u32[]{:S(2)}, u32[]{:S(2)}) collective-permute-start(bf16[1024,128]{1,0:T(8,128)(2,1)S(1)} %collective-permute-done.12), channel_id=1, source_target_pairs={{0,16},{4,20},{8,24},{12,28},{16,0},{20,4},{24,8},{28,12},{1,17},{... | collective-permute-start | bytes 786440 | tf_op jit(solution)/shard_map/ppermute | solution.py:564
  58.8 7.2 %collective-permute-start.13 = (bf16[1024,128]{1,0:T(8,128)(2,1)S(1)}, bf16[1024,128]{1,0:T(8,128)(2,1)S(1)}, u32[]{:S(2)}, u32[]{:S(2)}) collective-permute-start(bf16[1024,128]{1,0:T(8,128)(2,1)S(1)} %collective-permute-done.5), channel_id=1, source_target_pairs={{0,8},{4,12},{8,0},{12,4},{16,24},{20,28},{24,16},{28,20},{1,9},{5... | collective-permute-start | bytes 786440 | tf_op jit(solution)/shard_map/ppermute | solution.py:564
  67.2 22.1 %collective-permute-start.17 = (bf16[2,1024,128]{2,1,0:T(8,128)(2,1)}, bf16[2,1024,128]{2,1,0:T(8,128)(2,1)}, u32[]{:S(2)}, u32[]{:S(2)}) collective-permute-start(bf16[2,1024,128]{2,1,0:T(8,128)(2,1)} %pad_maximum_fusion.3.refs_2_), channel_id=1, source_target_pairs={{0,8},{4,12},{8,0},{12,4},{16,24},{20,28},{24,16},{28,20},{1,9},{5... | collective-permute-start | bytes 1572872 | tf_op jit(solution)/shard_map/ppermute | solution.py:564
  68.4 21.0 %collective-permute-start.16 = (bf16[2,1024,128]{2,1,0:T(8,128)(2,1)}, bf16[2,1024,128]{2,1,0:T(8,128)(2,1)}, u32[]{:S(2)}, u32[]{:S(2)}) collective-permute-start(bf16[2,1024,128]{2,1,0:T(8,128)(2,1)} %pad_maximum_fusion.2.refs_0_), channel_id=1, source_target_pairs={{0,16},{4,20},{8,24},{12,28},{16,0},{20,4},{24,8},{28,12},{1,17},{... | collective-permute-start | bytes 1572872 | tf_op jit(solution)/shard_map/ppermute | solution.py:564
  89.4 10.9 %collective-permute-start.18 = (bf16[2,1024,128]{2,1,0:T(8,128)(2,1)}, bf16[2,1024,128]{2,1,0:T(8,128)(2,1)S(1)}, u32[]{:S(2)}, u32[]{:S(2)}) collective-permute-start(bf16[2,1024,128]{2,1,0:T(8,128)(2,1)} %pad_maximum_fusion.2.refs_0_), channel_id=1, source_target_pairs={{0,4},{4,0},{8,12},{12,8},{16,20},{20,16},{24,28},{28,24},{1,5},{5... | collective-permute-start | bytes 1572872 | tf_op jit(solution)/shard_map/ppermute | solution.py:564
  89.4 10.8 %collective-permute-start.19 = (bf16[2,1024,128]{2,1,0:T(8,128)(2,1)}, bf16[2,1024,128]{2,1,0:T(8,128)(2,1)}, u32[]{:S(2)}, u32[]{:S(2)}) collective-permute-start(bf16[2,1024,128]{2,1,0:T(8,128)(2,1)} %collective-permute-done.16.refs_1_), channel_id=1, source_target_pairs={{0,4},{4,0},{8,12},{12,8},{16,20},{20,16},{24,28},{28,24},{1,5},{5... | collective-permute-start | bytes 1572872 | tf_op jit(solution)/shard_map/ppermute | solution.py:564
  89.9 10.4 %collective-permute-start.20 = (bf16[2,1024,128]{2,1,0:T(8,128)(2,1)}, bf16[2,1024,128]{2,1,0:T(8,128)(2,1)}, u32[]{:S(2)}, u32[]{:S(2)}) collective-permute-start(bf16[2,1024,128]{2,1,0:T(8,128)(2,1)} %pad_maximum_fusion.3.refs_2_), channel_id=1, source_target_pairs={{0,4},{4,0},{8,12},{12,8},{16,20},{20,16},{24,28},{28,24},{1,5},{5... | collective-permute-start | bytes 1572872 | tf_op jit(solution)/shard_map/ppermute | solution.py:564
  90.0 10.3 %collective-permute-start.21 = (bf16[2,1024,128]{2,1,0:T(8,128)(2,1)}, bf16[2,1024,128]{2,1,0:T(8,128)(2,1)}, u32[]{:S(2)}, u32[]{:S(2)}) collective-permute-start(bf16[2,1024,128]{2,1,0:T(8,128)(2,1)} %collective-permute-done.17.refs_3_), channel_id=1, source_target_pairs={{0,4},{4,0},{8,12},{12,8},{16,20},{20,16},{24,28},{28,24},{1,5},{5... | collective-permute-start | bytes 1572872 | tf_op jit(solution)/shard_map/ppermute | solution.py:564
  90.5 59.4 %all-to-all-start.1 = ((bf16[8,640,256]{2,1,0:T(8,128)(2,1)}), bf16[8,640,256]{2,1,0:T(8,128)(2,1)S(1)}, u32[]{:S(2)}, u32[]{:S(2)}) async-start(bf16[8,640,256]{2,1,0:T(8,128)(2,1)} %get-tuple-element.81), calls=%async_computation.1 | async-start | bytes 5242880 | tf_op jit(solution)/shard_map/all_to_all | solution.py:638
  107.6 14.3 %collective-permute-start.22 = (bf16[256,1024]{1,0:T(8,128)(2,1)}, bf16[256,1024]{1,0:T(8,128)(2,1)S(1)}, u32[]{:S(2)}, u32[]{:S(2)}) collective-permute-start(bf16[256,1024]{1,0:T(8,128)(2,1)} %get-tuple-element.91), channel_id=1, source_target_pairs={{0,1},{1,0},{2,3},{3,2},{4,5},{5,4},{6,7},{7,6},{8,9},{9,8},{10,11... | collective-permute-start | bytes 1572872 | tf_op jit(solution)/shard_map/ppermute | solution.py:564
  139.0 8.4 %collective-permute-start.35 = (bf16[2,4,64,256]{3,2,1,0:T(8,128)(2,1)S(1)}, bf16[2,4,64,256]{3,2,1,0:T(8,128)(2,1)S(1)}, u32[]{:S(2)}, u32[]{:S(2)}) collective-permute-start(bf16[2,4,64,256]{3,2,1,0:T(8,128)(2,1)S(1)} %bitcast.117), channel_id=1, source_target_pairs={{0,16},{4,20},{8,24},{12,28},{16,0},{20,4},{24,8},{28,12},{1,17},{... | collective-permute-start | bytes 786440 | tf_op jit(solution)/shard_map/ppermute | solution.py:564
  141.8 10.2 %collective-permute-start.32 = (bf16[2,4,64,256]{3,2,1,0:T(8,128)(2,1)}, bf16[2,4,64,256]{3,2,1,0:T(8,128)(2,1)}, u32[]{:S(2)}, u32[]{:S(2)}) collective-permute-start(bf16[2,4,64,256]{3,2,1,0:T(8,128)(2,1)} %bitcast.37), channel_id=1, source_target_pairs={{0,8},{4,12},{8,0},{12,4},{16,24},{20,28},{24,16},{28,20},{1,9},{5... | collective-permute-start | bytes 786440 | tf_op jit(solution)/shard_map/ppermute | solution.py:564
  148.2 10.0 %collective-permute-start.36 = (bf16[4,64,256]{2,1,0:T(8,128)(2,1)}, bf16[4,64,256]{2,1,0:T(8,128)(2,1)S(1)}, u32[]{:S(2)}, u32[]{:S(2)}) collective-permute-start(bf16[4,64,256]{2,1,0:T(8,128)(2,1)} %fusion.11), channel_id=1, source_target_pairs={{0,8},{4,12},{8,0},{12,4},{16,24},{20,28},{24,16},{28,20},{1,9},{5... | collective-permute-start | bytes 393224 | tf_op jit(solution)/shard_map/ppermute | solution.py:564
  164.3 9.2 %collective-permute-start.40 = (bf16[128,256]{1,0:T(8,128)(2,1)S(1)}, bf16[128,256]{1,0:T(8,128)(2,1)S(1)}, u32[]{:S(2)}, u32[]{:S(2)}) collective-permute-start(bf16[128,256]{1,0:T(8,128)(2,1)S(1)} %get-tuple-element.123), channel_id=1, source_target_pairs={{0,1},{1,0},{2,3},{3,2},{4,5},{5,4},{6,7},{7,6},{8,9},{9,8},{10,11... | collective-permute-start | bytes 196616 | tf_op jit(solution)/shard_map/ppermute | solution.py:564
  166.0 11.0 %collective-permute-start.41 = (bf16[128,256]{1,0:T(8,128)(2,1)}, bf16[128,256]{1,0:T(8,128)(2,1)S(1)}, u32[]{:S(2)}, u32[]{:S(2)}) collective-permute-start(bf16[128,256]{1,0:T(8,128)(2,1)} %get-tuple-element.122), channel_id=1, source_target_pairs={{0,2},{1,3},{2,0},{3,1},{4,6},{5,7},{6,4},{7,5},{8,10},{9,11},{10,... | collective-permute-start | bytes 196616 | tf_op jit(solution)/shard_map/ppermute | solution.py:564
  166.6 10.5 %collective-permute-start.42 = (bf16[128,256]{1,0:T(8,128)(2,1)}, bf16[128,256]{1,0:T(8,128)(2,1)}, u32[]{:S(2)}, u32[]{:S(2)}) collective-permute-start(bf16[128,256]{1,0:T(8,128)(2,1)} %get-tuple-element.121), channel_id=1, source_target_pairs={{0,3},{1,2},{2,1},{3,0},{4,7},{5,6},{6,5},{7,4},{8,11},{9,10},{10,... | collective-permute-start | bytes 196616 | tf_op jit(solution)/shard_map/ppermute | solution.py:564
  171.4 7.0 %collective-permute-start.37 = (bf16[128,512]{1,0:T(8,128)(2,1)}, bf16[128,512]{1,0:T(8,128)(2,1)S(1)}, u32[]{:S(2)}, u32[]{:S(2)}) collective-permute-start(bf16[128,512]{1,0:T(8,128)(2,1)} %get-tuple-element.110), channel_id=1, source_target_pairs={{0,1},{1,0},{2,3},{3,2},{4,5},{5,4},{6,7},{7,6},{8,9},{9,8},{10,11... | collective-permute-start | bytes 393224 | tf_op jit(solution)/shard_map/ppermute | solution.py:564
  172.2 12.7 %collective-permute-start.38 = (bf16[128,512]{1,0:T(8,128)(2,1)}, bf16[128,512]{1,0:T(8,128)(2,1)S(1)}, u32[]{:S(2)}, u32[]{:S(2)}) collective-permute-start(bf16[128,512]{1,0:T(8,128)(2,1)} %get-tuple-element.111), channel_id=1, source_target_pairs={{0,2},{1,3},{2,0},{3,1},{4,6},{5,7},{6,4},{7,5},{8,10},{9,11},{10,... | collective-permute-start | bytes 393224 | tf_op jit(solution)/shard_map/ppermute | solution.py:564
  173.5 11.3 %collective-permute-start.39 = (bf16[128,512]{1,0:T(8,128)(2,1)}, bf16[128,512]{1,0:T(8,128)(2,1)S(1)}, u32[]{:S(2)}, u32[]{:S(2)}) collective-permute-start(bf16[128,512]{1,0:T(8,128)(2,1)} %get-tuple-element.112), channel_id=1, source_target_pairs={{0,3},{1,2},{2,1},{3,0},{4,7},{5,6},{6,5},{7,4},{8,11},{9,10},{10,... | collective-permute-start | bytes 393224 | tf_op jit(solution)/shard_map/ppermute | solution.py:564
  (38 other events, 469.2 us)
